TPU v7x, 32 devices: a whole 2x2x4 slice. The times are simulated.
32 devices in a mesh: rays: 8 (over z, y), rep: 4 (over x, core).
Axes of the slice: x: 2, y: 2, z: 4, core: 2. Of those that a mesh axis runs over, the one named last changes fastest.
Arguments:
- sample_means: float32 [2, 3, 2048, 128], P(None, None, ('rays', 'rep')), may hold values from -1.5 to 1.5
- sample_vars: float32 [2, 3, 2048, 128], P(None, None, ('rays', 'rep')), may hold values from 0.0001 to 0.01
- sample_spacing: float32 [2, 2048, 128], P(None, ('rays', 'rep')), may hold values from 0.01 to 0.1
- view_dirs: float32 [3, 2048], P(None, ('rays', 'rep')), may hold values from -2.5 to 2.5
- target_rgb: float32 [3, 2048], P(None, ('rays', 'rep')), may hold values from 0 to 1
- sample_counts: int32 [2, 2048], P(None, ('rays', 'rep')), may hold values from 10 to 128, as said below
- ray_mask: int32 [2048], P(('rays', 'rep')), may hold values from 0 to 1
- w_in: float32 [96, 256], replicated, may hold values from -0.625 to 0.625
- w_mid: float32 [2, 256, 256], replicated, may hold values from -0.375 to 0.375
- w_head: float32 [283, 128], replicated, may hold values from -0.375 to 0.375
- w_rgb: float32 [128, 3], replicated, may hold values from -0.5 to 0.5
- vectors: float32 [1156], replicated, may hold values from -0.6 to 0.6
- first_in: float32 [96, 256], replicated, may hold values from -9.1552734e-05 to 9.1552734e-05
- first_mid: float32 [2, 256, 256], replicated, may hold values from -9.1552734e-05 to 9.1552734e-05
- first_head: float32 [283, 128], replicated, may hold values from -9.1552734e-05 to 9.1552734e-05
- first_rgb: float32 [128, 3], replicated, may hold values from -9.1552734e-05 to 9.1552734e-05
- first_vec: float32 [1156], replicated, may hold values from -9.1552734e-05 to 9.1552734e-05
- second_in: float32 [96, 256], replicated, may hold values from 4.394531e-12 to 1.7578125e-11
- second_mid: float32 [2, 256, 256], replicated, may hold values from 4.394531e-12 to 1.7578125e-11
- second_head: float32 [283, 128], replicated, may hold values from 4.394531e-12 to 1.7578125e-11
- second_rgb: float32 [128, 3], replicated, may hold values from 4.394531e-12 to 1.7578125e-11
- second_vec: float32 [1156], replicated, may hold values from 4.394531e-12 to 1.7578125e-11
Outputs:
- loss_sum: float32 [], replicated
- ray_count: float32 [], replicated
- new_first_in: float32 [96, 256], replicated
- new_second_in: float32 [96, 256], replicated
- new_w_in: float32 [96, 256], replicated
- new_first_mid: float32 [2, 256, 256], replicated
- new_second_mid: float32 [2, 256, 256], replicated
- new_w_mid: float32 [2, 256, 256], replicated
- new_first_head: float32 [283, 128], replicated
- new_second_head: float32 [283, 128], replicated
- new_w_head: float32 [283, 128], replicated
- new_first_rgb: float32 [128, 3], replicated
- new_second_rgb: float32 [128, 3], replicated
- new_w_rgb: float32 [128, 3], replicated
- new_first_vec: float32 [1156], replicated
- new_second_vec: float32 [1156], replicated
- new_vectors: float32 [1156], replicated
Inputs may be any that keep to these rules, and one draw needn't show every extreme that they name: `sample_counts`: in each pass a ray's valid samples are its first slots. Over the rays of one device a pass has at most 6144 valid samples, and some device of each group along rays has exactly 6144. Over the devices of one group along rays (one index of rep) the valid samples of a pass total exactly 20480.
All inputs are finite; a program needn't handle non-finite values.
Results may differ from a plain program's by a relative error of at most 0.0003.
The roundings to bfloat16 on the way count: a program that leaves them out, or rounds other values in their place, can miss the bound.
Values sent between devices are 32-bit elements; how exact they have to be, the bound alone decides.
No kernel may reach another device: no remote copies, remote signals or barrier semaphores. Data moves between devices by JAX's collectives and lax.ppermute only.
A program may use at most 64 MiB of HBM per device.

v0:
```python
import jax
import jax.numpy as jnp
from jax import lax
from jax.sharding import PartitionSpec as P

L_POS = 16
L_DIR = 4
STEP = 7


LEARN_RATE = 0.05
BETA_ONE = 0.9
BETA_TWO = 0.999
EPSILON = 1e-08
DECAY = 0.01
COARSE_SHARE = 0.1


def entering(part, axis, combine, identity):
    place = lax.axis_index(axis)
    gathered = lax.all_gather(part, axis)
    state = jnp.zeros_like(part) + jnp.asarray(identity, part.dtype)

    def one(lap, state):
        return combine(state, lax.dynamic_index_in_dim(gathered, lap, 0, False))

    return lax.fori_loop(0, place, one, state)


def encode_position(means, variances):
    powers = 2.0 ** jnp.arange(L_POS).astype(jnp.float32)
    scaled = (powers[:, None, None] * means[None]).reshape(3 * L_POS, -1)
    damping = jnp.exp(-0.5 * (powers * powers)[:, None, None] * variances[None]).reshape(
        3 * L_POS, -1
    )
    return jnp.concatenate([jnp.sin(scaled) * damping, jnp.cos(scaled) * damping], axis=0)


def view_code(directions):
    powers = 2.0 ** jnp.arange(L_DIR).astype(jnp.float32)
    scaled = (powers[:, None, None] * directions[None]).reshape(3 * L_DIR, -1)
    return jnp.concatenate([directions, jnp.sin(scaled), jnp.cos(scaled)], axis=0)


def unpack_vector(vectors, hidden, features, layers):
    biases = vectors[: (layers + 1) * hidden].reshape(layers + 1, hidden)
    offset = (layers + 1) * hidden
    density_w = vectors[offset : offset + hidden]
    feature_b = vectors[offset + hidden : offset + hidden + features]
    color_b = vectors[offset + hidden + features : offset + hidden + features + 3]
    density_b = vectors[offset + hidden + features + 3]
    return (biases, density_w, feature_b, color_b, density_b)


def contract_rows(left, right):
    return lax.dot_general(
        left, right, (((0,), (0,)), ((), ())), preferred_element_type=jnp.float32
    )


def contract_cols(left, right):
    return lax.dot_general(
        left, right, (((1,), (1,)), ((), ())), preferred_element_type=jnp.float32
    )


def smooth_grad(values):
    sigmoid_of = jax.nn.sigmoid(values)
    return sigmoid_of * (1.0 + values * (1.0 - sigmoid_of))


def compact_rays(values, counts, offsets, length, slots):
    rows = values.shape[0]
    buffer = jnp.zeros((rows, length + slots), jnp.float32)

    def place(ray_index, current):
        piece = lax.dynamic_slice_in_dim(values, ray_index * slots, slots, 1)
        return lax.dynamic_update_slice_in_dim(current, piece, offsets[ray_index], 1)

    buffer = lax.fori_loop(0, counts.shape[0], place, buffer)
    total = offsets[-1] + counts[-1]
    keep = jnp.arange(length, dtype=jnp.int32) < total
    return jnp.where(keep[None, :], buffer[:, :length], 0.0)


def expand_rays(stream, offsets, rays_here, slots):
    rows = stream.shape[0]
    padded = jnp.concatenate([stream, jnp.zeros((rows, slots), jnp.float32)], axis=1)

    def take(ray_index, current):
        piece = lax.dynamic_slice_in_dim(padded, offsets[ray_index], slots, 1)
        return lax.dynamic_update_slice_in_dim(current, piece, ray_index * slots, 1)

    return lax.fori_loop(0, rays_here, take, jnp.zeros((rows, rays_here * slots), jnp.float32))


def deal_stream(stream, rotation, ways, depth):
    rows = stream.shape[0]
    laid = jnp.zeros((rows, depth * ways), jnp.float32)
    laid = lax.dynamic_update_slice_in_dim(laid, stream, rotation, 1)
    return laid.reshape(rows, depth, ways)


def undeal_stream(arrived, rotation, length):
    rows = arrived.shape[0]
    return lax.dynamic_slice_in_dim(arrived.reshape(rows, -1), rotation, length, 1)


def collect_sources(arrived, bases, share):
    rows, depth, ways = arrived.shape
    buffer = jnp.zeros((rows, share + depth), jnp.float32)

    def add_source(source, current):
        piece = lax.dynamic_index_in_dim(arrived, source, 2, keepdims=False)
        present = lax.dynamic_slice_in_dim(current, bases[source], depth, 1)
        return lax.dynamic_update_slice_in_dim(current, present + piece, bases[source], 1)

    buffer = lax.fori_loop(0, ways, add_source, buffer)
    return buffer[:, :share]


def spread_sources(produced, bases, depth, ways):
    rows = produced.shape[0]
    padded = jnp.concatenate([produced, jnp.zeros((rows, depth), jnp.float32)], axis=1)

    def put_source(source, current):
        piece = lax.dynamic_slice_in_dim(padded, bases[source], depth, 1)
        return lax.dynamic_update_slice_in_dim(current, piece[:, :, None], source, 2)

    return lax.fori_loop(0, ways, put_source, jnp.zeros((rows, depth, ways), jnp.float32))


def field_forward(packed, lowered, vectors):
    in_low, mid_low, head_low, rgb_low = lowered
    hidden = in_low.shape[1]
    biases, density_w, feature_b, color_b, density_b = unpack_vector(
        vectors, hidden, head_low.shape[1], mid_low.shape[0]
    )
    encoded = encode_position(packed[0:3], packed[3:6]).astype(jnp.bfloat16)
    before = contract_rows(in_low, encoded) + biases[0][:, None]
    sums_list = [before]
    actives = [jax.nn.silu(before).astype(jnp.bfloat16)]
    for layer_index in range(mid_low.shape[0]):
        before = contract_rows(mid_low[layer_index], actives[-1]) + biases[layer_index + 1][:, None]
        sums_list.append(before)
        actives.append(jax.nn.silu(before).astype(jnp.bfloat16))
    top_act = actives[-1]
    density_pre = (
        jnp.dot(density_w.astype(jnp.bfloat16), top_act, preferred_element_type=jnp.float32)
        + density_b
    )
    viewed = view_code(packed[6:9]).astype(jnp.bfloat16)
    feature_pre = (
        contract_rows(head_low[:hidden], top_act)
        + contract_rows(head_low[hidden:], viewed)
        + feature_b[:, None]
    )
    feature_act = jax.nn.silu(feature_pre).astype(jnp.bfloat16)
    color_pre = contract_rows(rgb_low, feature_act) + color_b[:, None]
    density = jax.nn.softplus(density_pre - 1.0)
    colors = 1.002 * jax.nn.sigmoid(color_pre) - 0.001
    outputs = jnp.concatenate([density[None], colors], axis=0)
    return (
        outputs,
        (encoded, sums_list, actives, viewed, density_pre, feature_pre, feature_act, color_pre),
    )


def field_backward(packed, cotangent, lowered, vectors):
    in_low, mid_low, head_low, rgb_low = lowered
    hidden = in_low.shape[1]
    layers = mid_low.shape[0]
    density_w = unpack_vector(vectors, hidden, head_low.shape[1], layers)[1]
    saved = field_forward(packed, lowered, vectors)[1]
    encoded, sums_list, actives, viewed, density_pre, feature_pre, feature_act, color_pre = saved
    top_act = actives[-1]
    color_sig = jax.nn.sigmoid(color_pre)
    color_grad = (cotangent[1:] * 1.002 * color_sig * (1.0 - color_sig)).astype(jnp.bfloat16)
    grad_rgb = contract_cols(feature_act, color_grad)
    grad_color_b = jnp.sum(color_grad.astype(jnp.float32), axis=1)
    act_grad = jnp.dot(rgb_low, color_grad, preferred_element_type=jnp.float32)
    feature_grad = (act_grad * smooth_grad(feature_pre)).astype(jnp.bfloat16)
    grad_head = jnp.concatenate(
        [contract_cols(top_act, feature_grad), contract_cols(viewed, feature_grad)], axis=0
    )
    grad_feature_b = jnp.sum(feature_grad.astype(jnp.float32), axis=1)
    density_grad = (cotangent[0] * jax.nn.sigmoid(density_pre - 1.0)).astype(jnp.bfloat16)
    grad_density_w = jnp.dot(top_act, density_grad, preferred_element_type=jnp.float32)
    grad_density_b = jnp.sum(density_grad.astype(jnp.float32))
    upward = jnp.dot(head_low[:hidden], feature_grad, preferred_element_type=jnp.float32)
    upward = (
        upward
        + density_w.astype(jnp.bfloat16).astype(jnp.float32)[:, None]
        * density_grad.astype(jnp.float32)[None]
    )
    grad_mid = [None] * layers
    grad_bias = [None] * (layers + 1)
    for layer_index in reversed(range(layers)):
        pre_grad = (upward * smooth_grad(sums_list[layer_index + 1])).astype(jnp.bfloat16)
        grad_mid[layer_index] = contract_cols(actives[layer_index], pre_grad)
        grad_bias[layer_index + 1] = jnp.sum(pre_grad.astype(jnp.float32), axis=1)
        upward = jnp.dot(mid_low[layer_index], pre_grad, preferred_element_type=jnp.float32)
    pre_grad = (upward * smooth_grad(sums_list[0])).astype(jnp.bfloat16)
    grad_in = contract_cols(encoded, pre_grad)
    grad_bias[0] = jnp.sum(pre_grad.astype(jnp.float32), axis=1)
    grad_vec = jnp.concatenate(
        grad_bias + [grad_density_w, grad_feature_b, grad_color_b, grad_density_b[None]], axis=0
    )
    return (grad_in, jnp.stack(grad_mid, axis=0), grad_head, grad_rgb, grad_vec)


def render_both(density, colors, spacing, valid, target, raymask, share):
    tau = density * spacing * valid
    inclusive = jnp.cumsum(tau, axis=1)
    exclusive = inclusive - tau
    beyond = jnp.exp(-inclusive)
    weights = jnp.exp(-exclusive) - beyond
    color = jnp.sum(weights[None] * colors, axis=2)
    error = color - target
    loss_part = share * jnp.sum(jnp.mean(error * error, axis=0) * raymask)
    color_grad = share * (2.0 / 3.0) * error * raymask[None]
    colors_grad = weights[None] * color_grad[:, :, None]
    weighted = jnp.sum(color_grad[:, :, None] * colors, axis=0)
    product = weighted * weights
    after = jnp.sum(product, axis=1, keepdims=True) - jnp.cumsum(product, axis=1)
    density_grad = (beyond * weighted - after) * spacing * valid
    return (loss_part, density_grad, colors_grad)


def adamw(weight, grad, first, second):
    first = BETA_ONE * first + (1.0 - BETA_ONE) * grad
    second = BETA_TWO * second + (1.0 - BETA_TWO) * grad * grad
    first_hat = first / (1.0 - BETA_ONE**STEP)
    second_hat = second / (1.0 - BETA_TWO**STEP)
    fresh = weight - LEARN_RATE * (first_hat / (jnp.sqrt(second_hat) + EPSILON) + DECAY * weight)
    return (first, second, fresh)


def on_device(
    sample_means,
    sample_vars,
    sample_spacing,
    view_dirs,
    target_rgb,
    sample_counts,
    ray_mask,
    w_in,
    w_mid,
    w_head,
    w_rgb,
    vectors,
    first_in,
    first_mid,
    first_head,
    first_rgb,
    first_vec,
    second_in,
    second_mid,
    second_head,
    second_rgb,
    second_vec,
):
    rays_here = view_dirs.shape[1]
    slots_per = sample_spacing.shape[2]
    ways = lax.axis_size("rays")
    most = 3 * rays_here * slots_per // 4
    depth = most // ways + 1
    even_share = 5 * rays_here * slots_per // 16
    lowered = (
        w_in.astype(jnp.bfloat16),
        w_mid.astype(jnp.bfloat16),
        w_head.astype(jnp.bfloat16),
        w_rgb.astype(jnp.bfloat16),
    )
    params = (w_in, w_mid, w_head, w_rgb, vectors)
    grads = tuple((jnp.zeros_like(weight) for weight in params))
    raymask = ray_mask.astype(jnp.float32)
    loss_sum = jnp.zeros((), jnp.float32)
    spread_dirs = jnp.broadcast_to(view_dirs[:, :, None], (3, rays_here, slots_per)).reshape(3, -1)
    positions = jnp.arange(slots_per, dtype=jnp.int32)
    totals = jnp.sum(sample_counts, axis=1)
    starts = entering(
        totals, "rays", lambda earlier, later: earlier + later, jnp.zeros((2,), jnp.int32)
    )
    for pass_index in range(2):
        counts = sample_counts[pass_index]
        valid = positions[None, :] < counts[:, None]
        offsets = jnp.cumsum(counts) - counts
        packed = jnp.concatenate(
            [
                sample_means[pass_index].reshape(3, -1),
                sample_vars[pass_index].reshape(3, -1),
                spread_dirs,
            ],
            axis=0,
        )
        stream = compact_rays(packed, counts, offsets, most, slots_per)
        rotation = starts[pass_index] % ways
        first_slot = starts[pass_index] // ways
        dealt = deal_stream(stream, rotation, ways, depth)
        slot_row = (first_slot + jnp.arange(depth, dtype=jnp.int32)).astype(jnp.float32)
        slot_row = jnp.broadcast_to(slot_row[None, :, None], (1, depth, ways))
        outgoing = jnp.concatenate([dealt, slot_row], axis=0)
        arrived = lax.all_to_all(outgoing, "rays", split_axis=2, concat_axis=2, tiled=True)
        bases = arrived[9, 0, :].astype(jnp.int32)
        incoming = collect_sources(arrived[:9], bases, even_share)
        pieces = 5
        block = even_share // pieces

        def forward_block(block_index, buffer):
            piece = lax.dynamic_slice_in_dim(incoming, block_index * block, block, 1)
            made = field_forward(piece, lowered, vectors)[0]
            return lax.dynamic_update_slice_in_dim(buffer, made, block_index * block, 1)

        produced = lax.fori_loop(0, pieces, forward_block, jnp.zeros((4, even_share), jnp.float32))
        laid_out = spread_sources(produced, bases, depth, ways)
        returned = lax.all_to_all(laid_out, "rays", split_axis=2, concat_axis=2, tiled=True)
        returned = undeal_stream(returned, rotation, most)
        picked = expand_rays(returned, offsets, rays_here, slots_per).reshape(
            4, rays_here, slots_per
        )
        share = COARSE_SHARE if pass_index == 0 else 1.0
        loss_part, density_grad, colors_grad = render_both(
            picked[0],
            picked[1:],
            sample_spacing[pass_index],
            valid.astype(jnp.float32),
            target_rgb,
            raymask,
            share,
        )
        loss_sum = loss_sum + loss_part
        sent_grads = jnp.concatenate([density_grad[None], colors_grad], axis=0).reshape(4, -1)
        backward_out = compact_rays(sent_grads, counts, offsets, most, slots_per)
        backward_raw = lax.all_to_all(
            deal_stream(backward_out, rotation, ways, depth),
            "rays",
            split_axis=2,
            concat_axis=2,
            tiled=True,
        )
        backward_in = collect_sources(backward_raw, bases, even_share)

        def backward_block(block_index, running):
            piece = lax.dynamic_slice_in_dim(incoming, block_index * block, block, 1)
            cotangent = lax.dynamic_slice_in_dim(backward_in, block_index * block, block, 1)
            extra = field_backward(piece, cotangent, lowered, vectors)
            return tuple((total + more for total, more in zip(running, extra)))

        grads = lax.fori_loop(0, pieces, backward_block, grads)
    count_here = jnp.sum(raymask)
    reduced = lax.psum(
        (grads[0], grads[1], grads[2], grads[3], grads[4], loss_sum, count_here), ("rays", "rep")
    )
    count = reduced[6]
    firsts = (first_in, first_mid, first_head, first_rgb, first_vec)
    seconds = (second_in, second_mid, second_head, second_rgb, second_vec)
    results = [
        adamw(params[group], reduced[group] / count, firsts[group], seconds[group])
        for group in range(5)
    ]
    return (
        reduced[5],
        count,
        results[0][0],
        results[0][1],
        results[0][2],
        results[1][0],
        results[1][1],
        results[1][2],
        results[2][0],
        results[2][1],
        results[2][2],
        results[3][0],
        results[3][1],
        results[3][2],
        results[4][0],
        results[4][1],
        results[4][2],
    )


def solution(mesh):
    in_specs = (
        P(None, None, ("rays", "rep"), None),
        P(None, None, ("rays", "rep"), None),
        P(None, ("rays", "rep"), None),
        P(None, ("rays", "rep")),
        P(None, ("rays", "rep")),
        P(None, ("rays", "rep")),
        P(("rays", "rep")),
        P(),
        P(),
        P(),
        P(),
        P(),
        P(),
        P(),
        P(),
        P(),
        P(),
        P(),
        P(),
        P(),
        P(),
        P(),
    )
    out_specs = (
        P(),
        P(),
        P(),
        P(),
        P(),
        P(),
        P(),
        P(),
        P(),
        P(),
        P(),
        P(),
        P(),
        P(),
        P(),
        P(),
        P(),
    )
    return jax.shard_map(
        on_device, mesh=mesh, in_specs=in_specs, out_specs=out_specs, check_vma=False
    )
```

profile of v0, /device:TPU:0, one launch (start us, length us, event | category | flops | bytes accessed | tf_op | source)
XLA Modules:
  0.0 1693.2 jit_solution(15398108455378865031)
XLA Ops:
  10.2 13.1 all-reduce.4
  26.6 1.3 fusion.206
  33.2 185.8 %while.243 = (s32[]{:T(128)}, f32[9,6272]{1,0:T(8,128)S(1)}, f32[9,8192]{1,0:T(8,128)S(1)}, s32[64]{0:T(128)S(1)}, s32[]{:T(128)}, /*index=5*/s32[]{:T(128)}, s32[]{:T(128)}, s32[]{:T(128)}, s32[]{:T(128)}) while((s32[]{:T(128)}, f32[9,6272]{1,0:T(8,128)S(1)}, f32[9,8192]{1,0:T(8,128)S(1)}, s32[64]{0:T(128)S(1)}, s32[]{:T(128)}, ...), condition=%wide.region_2.3_spmd, body=%wide.region_1.2_spmd.sunk | while | flops 9 | bytes 18625 | solution.py:80
  221.3 2.8 reshape.700
  224.3 4.2 pad_maximum_fusion.12
  228.5 4.7 copy.62
  233.2 3.5 all-to-all-start
  240.8 185.8 %while.249 = (s32[]{:T(128)}, f32[9,6272]{1,0:T(8,128)S(1)}, f32[9,8192]{1,0:T(8,128)S(1)}, s32[64]{0:T(128)S(1)}, s32[]{:T(128)}, /*index=5*/s32[]{:T(128)}, s32[]{:T(128)}, s32[]{:T(128)}, s32[]{:T(128)}) while((s32[]{:T(128)}, f32[9,6272]{1,0:T(8,128)S(1)}, f32[9,8192]{1,0:T(8,128)S(1)}, s32[64]{0:T(128)S(1)}, s32[]{:T(128)}, ...), condition=%wide.region_20.21_spmd, body=%wide.region_19.20_spmd.sunk | while | flops 9 | bytes 18625 | solution.py:80
  428.9 2.8 reshape.704
  431.9 4.2 pad_maximum_fusion.13
  436.1 4.7 copy.65
  440.8 5.9 all-to-all-start.2
  447.0 27.1 %while.245 = (s32[]{:T(128)}, f32[9,3329]{1,0:T(8,128)S(1)}, s32[8]{0:T(128)S(1)}, f32[9,769,8]{1,0,2:T(8,128)S(1)}, s32[]{:T(128)}, /*index=5*/s32[]{:T(128)}, s32[]{:T(128)}) while((s32[]{:T(128)}, f32[9,3329]{1,0:T(8,128)S(1)}, s32[8]{0:T(128)S(1)}, f32[9,769,8]{1,0,2:T(8,128)S(1)}, s32[]{:T(128)}, /*index=5*/s32[]{:T(128)}, ...), condition=%wide.region_7.8_spmd, body=%wide.region_6.7_spmd.sunk | while | flops 6926 | bytes 138555 | solution.py:118
  474.8 26.4 %while.246 = (s32[]{:T(128)}, f32[4,2560]{1,0:T(4,128)S(1)}, f32[9,2560]{1,0:T(8,128)}, bf16[96,256]{1,0:T(8,128)(2,1)S(1)}, f32[1156]{0:T(1024)S(1)}, /*index=5...) while((s32[]{:T(128)}, f32[4,2560]{1,0:T(4,128)S(1)}, ...), condition=%wide.region_9.10_spmd, body=%wide.region_8.9_spmd.sunk | while | flops 200412752 | bytes 3468007 | solution.py:315
  501.4 27.3 %while.250 = (s32[]{:T(128)}, f32[9,3329]{1,0:T(8,128)S(1)}, s32[8]{0:T(128)S(1)}, f32[9,769,8]{1,0,2:T(8,128)S(1)}, s32[]{:T(128)}, /*index=5*/s32[]{:T(128)}, s32[]{:T(128)}) while((s32[]{:T(128)}, f32[9,3329]{1,0:T(8,128)S(1)}, s32[8]{0:T(128)S(1)}, f32[9,769,8]{1,0,2:T(8,128)S(1)}, s32[]{:T(128)}, /*index=5*/s32[]{:T(128)}, ...), condition=%wide.region_22.23_spmd, body=%wide.region_21.22_spmd.sunk | while | flops 6926 | bytes 138555 | solution.py:118
  528.8 22.0 %while.251 = (s32[]{:T(128)}, f32[4,2560]{1,0:T(4,128)S(1)}, f32[9,2560]{1,0:T(8,128)S(1)}, bf16[96,256]{1,0:T(8,128)(2,1)S(1)}, f32[1156]{0:T(1024)S(1)}, /*ind...) while((s32[]{:T(128)}, f32[4,2560]{1,0:T(4,128)S(1)}, ...), condition=%wide.region_24.25_spmd, body=%wide.region_23.24_spmd.sunk | while | flops 200412752 | bytes 3468007 | solution.py:315
  551.5 25.7 %while.252 = (s32[]{:T(128)}, f32[4,769,8]{1,0,2:T(4,128)}, s32[8]{0:T(128)S(1)}, f32[4,3329]{1,0:T(4,128)S(1)}, s32[]{:T(128)}, /*index=5*/s32[]{:T(128)}, s32[]{:T(128)}) while((s32[]{:T(128)}, f32[4,769,8]{1,0,2:T(4,128)}, s32[8]{0:T(128)S(1)}, f32[4,3329]{1,0:T(4,128)S(1)}, s32[]{:T(128)}, /*index=5*/s32[]{:T(128)}, s32[]{:T(128)}) %tuple.648), condition=%wide.region_26.27_spmd, body=%wide.region_25.26_spmd.sunk | while | flops 5 | bytes 27279 | solution.py:130
  577.2 6.0 all-to-all-start.3
  583.9 25.7 %while.247 = (s32[]{:T(128)}, f32[4,769,8]{1,0,2:T(4,128)}, s32[8]{0:T(128)S(1)}, f32[4,3329]{1,0:T(4,128)S(1)}, s32[]{:T(128)}, /*index=5*/s32[]{:T(128)}, s32[]{:T(128)}) while((s32[]{:T(128)}, f32[4,769,8]{1,0,2:T(4,128)}, s32[8]{0:T(128)S(1)}, f32[4,3329]{1,0:T(4,128)S(1)}, s32[]{:T(128)}, /*index=5*/s32[]{:T(128)}, s32[]{:T(128)}) %tuple.646), condition=%wide.region_11.12_spmd, body=%wide.region_10.11_spmd.sunk | while | flops 5 | bytes 27279 | solution.py:130
  609.6 6.0 all-to-all-start.1
  616.8 167.7 %while.253 = (s32[]{:T(128)}, f32[4,8192]{1,0:T(4,128)S(1)}, s32[64]{0:T(128)S(1)}, f32[4,6272]{1,0:T(4,128)S(1)}, s32[]{:T(128)}, /*index=5*/s32[]{:T(128)}, s32[]{:T(128)}, s32[]{:T(128)}, s32[]{:T(128)}) while((s32[]{:T(128)}, f32[4,8192]{1,0:T(4,128)S(1)}, s32[64]{0:T(128)S(1)}, f32[4,6272]{1,0:T(4,128)S(1)}, s32[]{:T(128)}, ...), condition=%wide.region_28.29_spmd, body=%wide.region_27.28_spmd.sunk | while | flops 9 | bytes 4289 | solution.py:94
  785.7 167.6 %while.248 = (s32[]{:T(128)}, f32[4,8192]{1,0:T(4,128)S(1)}, s32[64]{0:T(128)S(1)}, f32[4,6272]{1,0:T(4,128)S(1)}, s32[]{:T(128)}, /*index=5*/s32[]{:T(128)}, s32[]{:T(128)}, s32[]{:T(128)}, s32[]{:T(128)}) while((s32[]{:T(128)}, f32[4,8192]{1,0:T(4,128)S(1)}, s32[64]{0:T(128)S(1)}, f32[4,6272]{1,0:T(4,128)S(1)}, s32[]{:T(128)}, ...), condition=%wide.region_13.14_spmd, body=%wide.region_12.13_spmd.sunk | while | flops 9 | bytes 4289 | solution.py:94
  955.7 180.7 %while.256 = (s32[]{:T(128)}, f32[4,6272]{1,0:T(4,128)S(1)}, f32[4,8192]{1,0:T(4,128)S(1)}, s32[64]{0:T(128)S(1)}, s32[]{:T(128)}, /*index=5*/s32[]{:T(128)}, s32[]{:T(128)}, s32[]{:T(128)}, s32[]{:T(128)}) while((s32[]{:T(128)}, f32[4,6272]{1,0:T(4,128)S(1)}, f32[4,8192]{1,0:T(4,128)S(1)}, s32[64]{0:T(128)S(1)}, s32[]{:T(128)}, ...), condition=%wide.region_55.56_spmd, body=%wide.region_54.55_spmd.sunk | while | flops 9 | bytes 8385 | solution.py:80
  1138.9 5.9 all-to-all-start.5
  1145.3 180.7 %while.254 = (s32[]{:T(128)}, f32[4,6272]{1,0:T(4,128)S(1)}, f32[4,8192]{1,0:T(4,128)S(1)}, s32[64]{0:T(128)S(1)}, s32[]{:T(128)}, /*index=5*/s32[]{:T(128)}, s32[]{:T(128)}, s32[]{:T(128)}, s32[]{:T(128)}) while((s32[]{:T(128)}, f32[4,6272]{1,0:T(4,128)S(1)}, f32[4,8192]{1,0:T(4,128)S(1)}, s32[64]{0:T(128)S(1)}, s32[]{:T(128)}, ...), condition=%wide.region_40.41_spmd, body=%wide.region_39.40_spmd.sunk | while | flops 9 | bytes 8385 | solution.py:80
  1330.4 5.9 all-to-all-start.4
  1336.4 24.3 %while.257 = (s32[]{:T(128)}, f32[4,3329]{1,0:T(4,128)S(1)}, s32[8]{0:T(128)S(1)}, f32[4,769,8]{1,0,2:T(4,128)S(1)}, s32[]{:T(128)}, /*index=5*/s32[]{:T(128)}, s32[]{:T(128)}) while((s32[]{:T(128)}, f32[4,3329]{1,0:T(4,128)S(1)}, s32[8]{0:T(128)S(1)}, f32[4,769,8]{1,0,2:T(4,128)S(1)}, s32[]{:T(128)}, /*index=5*/s32[]{:T(128)}, ...), condition=%wide.region_57.58_spmd, body=%wide.region_56.57_spmd.sunk | while | flops 3081 | bytes 61655 | solution.py:118
  1360.8 24.3 %while.255 = (s32[]{:T(128)}, f32[4,3329]{1,0:T(4,128)S(1)}, s32[8]{0:T(128)S(1)}, f32[4,769,8]{1,0,2:T(4,128)S(1)}, s32[]{:T(128)}, /*index=5*/s32[]{:T(128)}, s32[]{:T(128)}) while((s32[]{:T(128)}, f32[4,3329]{1,0:T(4,128)S(1)}, s32[8]{0:T(128)S(1)}, f32[4,769,8]{1,0,2:T(4,128)S(1)}, s32[]{:T(128)}, /*index=5*/s32[]{:T(128)}, ...), condition=%wide.region_42.43_spmd, body=%wide.region_41.42_spmd.sunk | while | flops 3081 | bytes 61655 | solution.py:118
  1385.1 82.8 %while.259 = (s32[]{:T(128)}, f32[96,256]{1,0:T(8,128)S(1)}, f32[2,256,256]{2,1,0:T(8,128)S(1)}, f32[283,128]{1,0:T(8,128)S(1)}, f32[128,3]{0,1:T(4,128)S(1)}, /...) while((s32[]{:T(128)}, f32[96,256]{1,0:T(8,128)S(1)}, ...), condition=%wide.region_50.51_spmd.clone, body=%wide.region_43.50_spmd.clone.sunk | while | flops 573169216 | bytes 20379208 | solution.py:350
  1391.0 1.3 convert_reduce_fusion.31
  1395.4 1.4 convert_reduce_fusion.34
  1399.6 1.3 convolution_bitcast_fusion.19
  1407.5 1.3 convert_reduce_fusion.31
  1412.0 1.4 convert_reduce_fusion.34
  1416.2 1.3 convolution_bitcast_fusion.19
  1424.1 1.3 convert_reduce_fusion.31
  1428.6 1.4 convert_reduce_fusion.34
  1432.7 1.3 convolution_bitcast_fusion.19
  1440.7 1.3 convert_reduce_fusion.31
  1445.1 1.4 convert_reduce_fusion.34
  1449.3 1.3 convolution_bitcast_fusion.19
  1457.2 1.3 convert_reduce_fusion.31
  1461.7 1.4 convert_reduce_fusion.34
  1465.8 1.3 convolution_bitcast_fusion.19
  1467.9 78.4 %while.258 = (s32[]{:T(128)}, f32[96,256]{1,0:T(8,128)S(1)}, f32[2,256,256]{2,1,0:T(8,128)S(1)}, f32[283,128]{1,0:T(8,128)S(1)}, f32[128,3]{0,1:T(4,128)S(1)}, /...) while((s32[]{:T(128)}, f32[96,256]{1,0:T(8,128)S(1)}, ...), condition=%wide.region_65.66_spmd, body=%wide.region_58.65_spmd.sunk | while | flops 572975808 | bytes 26670740 | solution.py:350
  1473.0 1.3 convert_reduce_fusion.25
  1477.5 1.4 convert_reduce_fusion.28
  1481.6 1.3 convolution_bitcast_fusion.17
  1488.7 1.3 convert_reduce_fusion.25
  1493.1 1.4 convert_reduce_fusion.28
  1497.3 1.3 convolution_bitcast_fusion.17
  1504.3 1.3 convert_reduce_fusion.25
  1508.8 1.4 convert_reduce_fusion.28
  1513.0 1.3 convolution_bitcast_fusion.17
  1524.5 1.4 convert_reduce_fusion.28
  1528.7 1.3 convolution_bitcast_fusion.17
  1540.2 1.4 convert_reduce_fusion.28
  1544.3 1.3 convolution_bitcast_fusion.17
  1547.2 41.2 %all-reduce.5 = (f32[]{:T(128)}, f32[]{:T(128)}, f32[128,3]{0,1:T(4,128)S(1)}, f32[1156]{0:T(1024)S(1)}) all-reduce(f32[]{:T(128)S(6)} %add.1908, f32[]{:T(128)} %get-tuple-element.2122, f32[128,3]{0,1:T(4,128)S(1)} %get-tuple-element.2057, f32[1156]{0:T(1024)S(1)} %get-tuple-element.2058), channel_id=1, replica_groups=mesh['rays'=8,'rep'=4] {'rays','rep'}, use_global_device_ids=true, to_apply=%region_33.34 | all-reduce | flops 1542 | bytes 12336 | tf_op jit(solution)/shard_map/psum | solution.py:352
  1589.7 1.3 multiply_subtract_fusion.3
  1591.0 88.0 %all-reduce.9.cloned.1.call-done = (f32[96,256]{1,0:T(8,128)}, f32[2,256,256]{2,1,0:T(8,128)}, f32[283,128]{1,0:T(8,128)}) async-done(((f32[96,256]{1,0:T(8,128)}, f32[2,256,256]{2,1,0:T(8,128)}, f32[283,128]{1,0:T(8,128)}), (f32[96,256]{1,0:T(8,128)}, f32[2,256,256]{2,1,0:T(8,128)}, f32[283,128]{1,0:T(8,128)})) %all-reduce.9.cloned.1.call-update) | async-done | bytes 767504 | tf_op jit(solution)/shard_map/psum | solution.py:352
  1679.0 2.6 multiply_subtract_fusion.1
  1681.5 3.4 multiply_subtract_fusion
  1685.0 1.4 multiply_subtract_fusion.2
  (2246 shorter events, 569.9 us)
Async XLA Ops:
  7.2 23.3 %copy-start = (f32[3,64]{1,0:T(4,128)S(1)}, f32[3,64]{1,0:T(4,128)}, u32[]{:S(2)}) copy-start(f32[3,64]{1,0:T(4,128)} %param.59) | copy-start | bytes 2308
  228.5 10.9 copy-start.4
  228.5 11.6 copy-start.11
  228.5 11.6 copy-start.14
  228.5 11.7 copy-start.26
  228.5 11.7 copy-start.10
  233.2 207.6 %all-to-all-start = ((f32[10,769,8]{1,0,2:T(8,128)}), f32[10,769,8]{1,0,2:T(8,128)S(1)}, u32[]{:S(2)}, u32[]{:S(2)}) async-start(f32[10,769,8]{1,0,2:T(8,128)} %copy.62), calls=%async_computation | async-start | bytes 917504 | tf_op jit(solution)/shard_map/all_to_all | solution.py:304
  436.1 4.7 copy-start.29
  436.1 38.7 %copy-start.16 = (bf16[2,256,256]{2,1,0:T(8,128)(2,1)S(1)}, bf16[2,256,256]{2,1,0:T(8,128)(2,1)}, u32[]{:S(2)}) copy-start(bf16[2,256,256]{2,1,0:T(8,128)(2,1)} %convert_element_type.715) | copy-start | bytes 786436
  440.8 60.3 %all-to-all-start.2 = ((f32[10,769,8]{1,0,2:T(8,128)}), f32[10,769,8]{1,0,2:T(8,128)S(1)}, u32[]{:S(2)}, u32[]{:S(2)}) async-start(f32[10,769,8]{1,0,2:T(8,128)} %copy.65), calls=%async_computation.2 | async-start | bytes 917504 | tf_op jit(solution)/shard_map/all_to_all | solution.py:304
  550.8 58.8 %copy-start.17 = (bf16[2,256,256]{2,1,0:T(8,128)(2,1)}, bf16[2,256,256]{2,1,0:T(8,128)(2,1)S(1)}, u32[]{:S(2)}) copy-start(bf16[2,256,256]{2,1,0:T(8,128)(2,1)S(1)} %get-tuple-element.3771) | copy-start | bytes 786436
  577.2 32.4 %all-to-all-start.3 = ((f32[4,769,8]{1,0,2:T(4,128)}), f32[4,769,8]{1,0,2:T(4,128)S(1)}, u32[]{:S(2)}, u32[]{:S(2)}) async-start(f32[4,769,8]{1,0,2:T(4,128)} %get-tuple-element.2043), calls=%async_computation.3 | async-start | bytes 229376 | tf_op jit(solution)/shard_map/all_to_all | solution.py:317
  609.6 174.9 %all-to-all-start.1 = ((f32[4,769,8]{1,0,2:T(4,128)}), f32[4,769,8]{1,0,2:T(4,128)S(1)}, u32[]{:S(2)}, u32[]{:S(2)}) async-start(f32[4,769,8]{1,0,2:T(4,128)} %get-tuple-element.2038), calls=%async_computation.1 | async-start | bytes 229376 | tf_op jit(solution)/shard_map/all_to_all | solution.py:317
  616.1 337.3 %copy-start.13 = (f32[2,64,128]{2,1,0:T(8,128)S(1)}, f32[2,64,128]{2,1,0:T(8,128)}, u32[]{:S(2)}) copy-start(f32[2,64,128]{2,1,0:T(8,128)} %param.58) | copy-start | bytes 196612
  616.1 337.8 %copy-start.25 = (f32[3,64]{1,0:T(4,128)S(1)}, f32[3,64]{1,0:T(4,128)}, u32[]{:S(2)}) copy-start(f32[3,64]{1,0:T(4,128)} %param.60) | copy-start | bytes 2308
  1138.9 191.5 %all-to-all-start.5 = ((f32[4,769,8]{1,0,2:T(4,128)}), f32[4,769,8]{1,0,2:T(4,128)S(1)}, u32[]{:S(2)}, u32[]{:S(2)}) async-start(f32[4,769,8]{1,0,2:T(4,128)} %copy.68), calls=%async_computation.5 | async-start | bytes 229376 | tf_op jit(solution)/shard_map/all_to_all | solution.py:335
  1330.4 30.4 %all-to-all-start.4 = ((f32[4,769,8]{1,0,2:T(4,128)}), f32[4,769,8]{1,0,2:T(4,128)S(1)}, u32[]{:S(2)}, u32[]{:S(2)}) async-start(f32[4,769,8]{1,0,2:T(4,128)} %copy.67), calls=%async_computation.4 | async-start | bytes 229376 | tf_op jit(solution)/shard_map/all_to_all | solution.py:335
  1336.3 342.6 %all-reduce.9.cloned.1.call-start = ((), (), s32[]{:S(2)}) async-start(), calls=%async_computation.6 | async-start | bytes 1540096 | tf_op jit(solution)/shard_map/psum | solution.py:352
  1385.1 4.0 copy-start.18
  1397.9 3.0 copy-start.34
  1399.6 2.1 copy-start.7
  1401.7 4.0 copy-start.18
  1414.5 3.0 copy-start.34
  1416.1 2.1 copy-start.7
  1418.2 4.0 copy-start.18
  1431.0 3.0 copy-start.34
  1432.7 2.1 copy-start.7
  1434.8 4.0 copy-start.18
  1447.6 3.0 copy-start.34
  1449.2 2.1 copy-start.7
  1451.3 4.0 copy-start.18
  1464.1 3.0 copy-start.34
  1465.8 2.1 copy-start.7
  1467.9 120.6 %copy-start.27 = (f32[128,3]{0,1:T(4,128)S(1)}, f32[128,3]{0,1:T(4,128)}, u32[]{:S(2)}) copy-start(f32[128,3]{0,1:T(4,128)} %param.76) | copy-start | bytes 4612
  1467.9 120.5 %copy-start.28 = (f32[128,3]{0,1:T(4,128)S(1)}, f32[128,3]{0,1:T(4,128)}, u32[]{:S(2)}) copy-start(f32[128,3]{0,1:T(4,128)} %param.71) | copy-start | bytes 4612
  1467.9 121.8 %copy-start.23 = (f32[1156]{0:T(1024)S(1)}, f32[1156]{0:T(1024)}, u32[]{:S(2)}) copy-start(f32[1156]{0:T(1024)} %param.77) | copy-start | bytes 13876
  1467.9 121.8 %copy-start.24 = (f32[1156]{0:T(1024)S(1)}, f32[1156]{0:T(1024)}, u32[]{:S(2)}) copy-start(f32[1156]{0:T(1024)} %param.72) | copy-start | bytes 13876
  1467.9 211.0 %copy-start.12 = (f32[283,128]{1,0:T(8,128)S(1)}, f32[283,128]{1,0:T(8,128)}, u32[]{:S(2)}) copy-start(f32[283,128]{1,0:T(8,128)} %param.65) | copy-start | bytes 434692
  1467.9 213.6 %copy-start.5 = (f32[2,256,256]{2,1,0:T(8,128)S(1)}, f32[2,256,256]{2,1,0:T(8,128)}, u32[]{:S(2)}) copy-start(f32[2,256,256]{2,1,0:T(8,128)} %param.64) | copy-start | bytes 1572868
  1468.0 3.1 copy-start.19
  1471.1 3.3 copy-start.30
  1476.9 2.1 copy-start.31
  1479.9 3.0 copy-start.36
  1481.6 2.0 copy-start.9
  1483.7 3.1 copy-start.19
  1486.8 3.3 copy-start.30
  1492.5 2.1 copy-start.31
  1495.6 3.0 copy-start.36
  1499.3 3.1 copy-start.19
  1502.5 3.3 copy-start.30
  1508.2 2.1 copy-start.31
  1511.3 3.0 copy-start.36
  1515.0 3.1 copy-start.19
  1518.1 3.3 copy-start.30
  1523.9 2.1 copy-start.31
  1527.0 3.0 copy-start.36
  1530.7 3.1 copy-start.19
  1533.8 3.3 copy-start.30
  1539.6 2.1 copy-start.31
  1542.7 3.0 copy-start.36
  1546.4 138.5 %copy-start.15 = (f32[96,256]{1,0:T(8,128)S(1)}, f32[96,256]{1,0:T(8,128)}, u32[]{:S(2)}) copy-start(f32[96,256]{1,0:T(8,128)} %param.63) | copy-start | bytes 294916
  1546.4 138.5 %copy-start.20 = (f32[96,256]{1,0:T(8,128)S(1)}, f32[96,256]{1,0:T(8,128)}, u32[]{:S(2)}) copy-start(f32[96,256]{1,0:T(8,128)} %param.73) | copy-start | bytes 294916
  1546.4 138.5 %copy-start.21 = (f32[96,256]{1,0:T(8,128)S(1)}, f32[96,256]{1,0:T(8,128)}, u32[]{:S(2)}) copy-start(f32[96,256]{1,0:T(8,128)} %param.68) | copy-start | bytes 294916
  1678.9 6.0 copy-start.22
  (42 other events, 40.6 us)
Sparse Core Ops, SparseCore 0:
  1547.4 131.5 all-reduce.8
where the time goes:
time: 1710 us; the launch traced here: 1690 us
  loops' own time  853 us (50%)
  local copies, waits for them, and re-layouts  454 us (27%)
  matrix products  114 us (7%)
  waiting for transfers between devices  88 us (5%)
  other arithmetic  72.3 us (4%)
  blocking collectives  54.2 us (3%)
  starting transfers between devices  33.3 us (2%)
  between operations  24.8 us (1%)
    another operation x4, loops' own time, compact_rays(): buffer = lax.fori_loop(0, counts.shape[0], place, buffer)  504 us
    another operation x2, loops' own time, expand_rays(): lax.fori_loop(0, rays_here, take, jnp.zeros((rows, rays_here * slots), jn...  250 us
    dynamic_slice x256, local copies, waits for them, and re-layouts, place(): offsets[ray_index]  151 us
    psum x1, waiting for transfers between devices, on_device(): lax.psum((grads[0], grads[1], grads[2], grads[3], grads[4], loss_sum, cou...  88 us
    dynamic_update_slice x256, local copies, waits for them, and re-layouts, place(): lax.dynamic_update_slice_in_dim(current, piece, offsets[ray_index], 1)  76 us
    dynamic_slice x128, local copies, waits for them, and re-layouts, take(): piece = lax.dynamic_slice_in_dim(padded, offsets[ray_index], slots, 1)  74.6 us
    another operation x4, loops' own time, collect_sources(): buffer = lax.fori_loop(0, ways, add_source, buffer)  63 us
    dot_general x100, matrix products, contract_rows(): lax.dot_general(left, right, (((0,), (0,)), ((), ())), preferred_element_...  62 us
  transfers between devices with their start and end apart: 7, of which 1 were waited for; matrix products, arithmetic and copies ran while one was open for 14% of the time, Pallas kernels for 0%

commit v1 on v0

v1 whole, which is shorter than its diff:
```python
import math

import jax
import jax.numpy as jnp
from jax import lax
from jax.experimental import pallas as pl
from jax.experimental.pallas import tpu as pltpu
from jax.sharding import PartitionSpec as P

L_POS = 16
L_DIR = 4
STEP = 7
LEARN_RATE = 0.05
BETA_ONE = 0.9
BETA_TWO = 0.999
EPSILON = 1e-08
DECAY = 0.01
COARSE_SHARE = 0.1

BLOCK = 1024
LANES = 128
PART = 96

TURN_HEAD = 0.1591796875
TURN_REST = 1.0 / (2.0 * math.pi) - TURN_HEAD
SIN_POLY = (3.1415926343, -5.1677091056, 2.5500551036, -0.5981303017, 0.0773037189)
COS_POLY = (0.9999999314, -4.9347894708, 4.0583337486, -1.3313191807, 0.2184639082)

F32 = jnp.float32
BF16 = jnp.bfloat16


def split_three(values):
    head = values.astype(BF16)
    rest = values - head.astype(F32)
    middle = rest.astype(BF16)
    tail = (rest - middle.astype(F32)).astype(BF16)
    return head, middle, tail


def dot_nt(left, right):
    return lax.dot_general(left, right, (((1,), (1,)), ((), ())), preferred_element_type=F32)


def dot_nn(left, right):
    return jnp.dot(left, right, preferred_element_type=F32)


def poly(coefficients, square):
    total = jnp.full_like(square, coefficients[-1])
    for c in coefficients[-2::-1]:
        total = total * square + c
    return total


def sin_cos_turns(r):
    square = r * r
    s = r * poly(SIN_POLY, square)
    c = poly(COS_POLY, square)
    return (s + s) * c, 1.0 - (s + s) * s


def lane_scan(values, lane):
    for step in (1, 2, 4, 8, 16, 32, 64):
        values = values + jnp.where(lane >= step, pltpu.roll(values, step, 1), 0.0)
    return values


def field_kernel(
    counts,
    place,
    means,
    variances,
    spacing,
    dirs,
    target,
    mask,
    counts_vec,
    w_in,
    w_mid,
    w_head,
    w_rgb,
    vec,
    keep,
    send,
    pk,
    xs,
    zs,
    gs,
    enc,
    hidden,
    slope,
    feat,
    feat_slope,
    one_hot,
    exp_buf,
    grad_buf,
    cols,
    wide,
    tall,
    w0t,
    wmt,
    wm,
    wht,
    whd,
    wrt,
    wr,
    bias_b,
    view_t,
    venc,
    g_in,
    g_mid,
    g_head,
    g_rgb,
    s_ray,
    g_sum,
    packed,
    sem,
):
    rays = dirs.shape[1]
    copies = []
    for p in range(2):
        for k, source in enumerate((means, variances)):
            copies.append(
                pltpu.make_async_copy(
                    source.at[p], pk.at[pl.ds((p * 8 + 3 * k) * rays, 3 * rays)], sem.at[2 * p + k]
                )
            )
    for copy in copies:
        copy.start()

    half = 0.5
    vec_t = vec[...].T
    for h in range(2):
        tall[96 * h : 96 * h + 96, :] = w_in[:, 128 * h : 128 * h + 128].astype(BF16).astype(F32) * half
        for c in range(3):
            for k in range(2):
                wide[48 * k + 16 * c : 48 * k + 16 * c + 16, 128 * h : 128 * h + 128] = tall[
                    pl.ds(96 * h + 48 * k + c, 16, stride=3), :
                ]
    b0 = jnp.concatenate([vec[0:1, :], vec[1:2, :]], axis=1) * half
    head, middle, tail = split_three(b0)
    row = lax.broadcasted_iota(jnp.int32, (32, 256), 0)
    wide[96:128, :] = jnp.where(
        row == 0,
        head.astype(F32),
        jnp.where(row == 1, middle.astype(F32), jnp.where(row == 2, tail.astype(F32), 0.0)),
    )
    w0t[...] = wide[0:128, :].T.astype(BF16)
    for k in range(2):
        rounded = w_mid[k].astype(BF16).astype(F32) * half
        wm[k] = rounded.astype(BF16)
        wmt[k] = rounded.T.astype(BF16)
        bias_b[k, 0:128, :] = jnp.broadcast_to(vec_t[:, 2 + 2 * k : 3 + 2 * k], (128, 128)) * half
        bias_b[k, 128:256, :] = jnp.broadcast_to(vec_t[:, 3 + 2 * k : 4 + 2 * k], (128, 128)) * half
    top = (w_head[0:256, :].astype(BF16).astype(F32) * half).T
    u_row = jnp.concatenate([vec[6:7, :], vec[7:8, :]], axis=1).astype(BF16).astype(F32)
    row16 = lax.broadcasted_iota(jnp.int32, (16, 256), 0)
    last = jnp.where(row16 == 3, u_row, 0.0)
    wht[0:128, :] = top.astype(BF16)
    wht[128:144, :] = last.astype(BF16)
    whd[...] = jnp.concatenate([top, last * half], axis=0).T.astype(BF16)
    wide[0:128, 0:128] = jnp.zeros((128, 128), F32)
    wide[0:128, 0:3] = w_rgb[...].astype(BF16).astype(F32)
    wr[...] = (wide[0:128, 0:16] * half).astype(BF16)
    wrt[...] = wide[0:128, 0:128].T[0:16, :].astype(BF16)

    cols[...] = jnp.zeros_like(cols)
    cols[0:3, 0:rays] = target[...]
    cols[3:4, 0:rays] = mask[...].astype(F32)
    cols[4:6, 0:rays] = counts_vec[...].astype(F32)
    col = cols[...].T[0:rays, :]
    lane8 = lax.broadcasted_iota(jnp.int32, (8, LANES), 1)
    wide[0:32, 0:128] = jnp.zeros((32, 128), F32)
    d = dirs[...]
    wide[0:3, 0:rays] = d
    for l in range(L_DIR):
        wide[3 + 3 * l : 6 + 3 * l, 0:rays] = jnp.sin(d * (2.0**l))
        wide[15 + 3 * l : 18 + 3 * l, 0:rays] = jnp.cos(d * (2.0**l))
    venc[...] = wide[0:32, 0:rays].astype(BF16)
    wide[0:32, 128:256] = jnp.zeros((32, 128), F32)
    wide[0:27, 128:256] = w_head[256:283, :].astype(BF16).astype(F32)
    view = lax.dot_general(
        wide[0:32, 128:256].astype(BF16), venc[...], (((0,), (0,)), ((), ())), preferred_element_type=F32
    )
    view = (view + vec_t[:, 8:9]) * half
    row16r = lax.broadcasted_iota(jnp.int32, (16, rays), 0)
    low_rows = jnp.where(row16r < 4, jnp.broadcast_to(vec_t[0:16, 9:10], (16, rays)), 0.0)
    view_t[...] = jnp.concatenate(split_three(jnp.concatenate([view, low_rows], axis=0)), axis=1)

    nblk = xs.shape[1]
    ones_row = (lax.broadcasted_iota(jnp.int32, (32, LANES), 0) < 3).astype(BF16)
    one_row = (lax.broadcasted_iota(jnp.int32, (16, LANES), 0) == 0).astype(BF16)

    def fill(t, carry):
        s = pl.multiple_of(t * LANES, LANES)
        enc[96:128, pl.ds(s, LANES)] = ones_row
        for k in range(2):
            hidden[k, 256:272, pl.ds(s, LANES)] = one_row
        return carry

    lax.fori_loop(0, nblk // LANES, fill, 0)
    grad_buf[...] = jnp.zeros_like(grad_buf)
    for ref in (g_in, g_mid, g_head, g_rgb, s_ray, g_sum):
        ref[...] = jnp.zeros_like(ref)

    lane1 = lax.broadcasted_iota(jnp.int32, (rays, LANES), 1)
    sub8 = lax.broadcasted_iota(jnp.int32, (8, LANES), 0)
    level = lax.broadcasted_iota(jnp.int32, (16, LANES), 0)
    power = (jnp.int32(1) << level).astype(F32)
    decay_rate = power * power * (-0.5)
    per = BLOCK // LANES

    def wide_of(tile):
        return jnp.concatenate([tile] * per, axis=1)

    for copy in copies:
        copy.wait()

    def one_pass(p, loss):
        xs[...] = jnp.zeros_like(xs)
        gs[...] = jnp.zeros_like(gs)

        def pack(r, offset):
            here = pk[pl.ds(p * 8 * rays + r, 8, stride=rays), :]
            here = jnp.where(sub8 < 6, here, r.astype(F32))
            o = offset % LANES
            t = offset - o
            turned = pltpu.roll(here, o, 1)
            low = pl.multiple_of(t, LANES)
            xs[:, pl.ds(low, LANES)] = jnp.where(lane8 >= o, turned, xs[:, pl.ds(low, LANES)])
            xs[:, pl.ds(low + LANES, LANES)] = jnp.where(lane8 < o, turned, 0.0)
            return offset + counts[p, r]

        total = lax.fori_loop(0, rays, pack, jnp.int32(0))
        blocks = (total + BLOCK - 1) // BLOCK

        def activate(y, h_ref, slope_ref):
            a = 1.0 + jnp.tanh(y)
            h = y * a
            slope_ref[...] = a + h * (2.0 - a)
            low = h.astype(BF16)
            h_ref[...] = low
            return low

        def forward(i, carry):
            at = pl.ds(pl.multiple_of(i * BLOCK, BLOCK), BLOCK)
            x = xs[:, at]
            m1 = jnp.round(x * 2.0**11) * 2.0**-11
            p1 = m1 * TURN_HEAD
            p2 = m1 * TURN_REST + (x - m1) * (TURN_HEAD + TURN_REST)
            hi = jnp.round((p1 + p2) * 2.0**20) * 2.0**-20
            lo = (p1 - hi) + p2
            pw = wide_of(power)
            dr = wide_of(decay_rate)
            for c in range(3):
                a = jnp.broadcast_to(hi[c : c + 1, :], (16, BLOCK)) * pw
                a = a - jnp.round(a)
                a = a + jnp.broadcast_to(lo[c : c + 1, :], (16, BLOCK)) * pw
                s, co = sin_cos_turns(a)
                damp = jnp.exp(jnp.broadcast_to(x[3 + c : 4 + c, :], (16, BLOCK)) * dr)
                enc[16 * c : 16 * c + 16, at] = (s * damp).astype(BF16)
                enc[48 + 16 * c : 64 + 16 * c, at] = (co * damp).astype(BF16)
            hit = (
                jnp.broadcast_to(x[6:7, :], (rays, BLOCK))
                == lax.broadcasted_iota(jnp.int32, (rays, BLOCK), 0).astype(F32)
            )
            hot = jnp.where(hit, 1.0, 0.0).astype(BF16)
            one_hot[:, at] = hot
            h = activate(dot_nn(w0t[...], enc[:, at]), hidden.at[0, 0:256, at], slope.at[0, :, at])
            for k in range(2):
                y = dot_nn(wmt[k], h) + wide_of(bias_b[k])
                h = activate(y, hidden.at[k + 1, 0:256, at], slope.at[k + 1, :, at])
            y = dot_nn(wht[...], h) + dot_nn(view_t[...], jnp.concatenate([hot, hot, hot], axis=0))
            f = activate(y[0:128, :], feat.at[:, at], feat_slope.at[:, at])
            zs[:, at] = dot_nn(wrt[...], f)[0:8, :] + y[128:136, :]
            return carry

        lax.fori_loop(0, blocks, forward, 0)
        zs[:, pl.ds(pl.multiple_of(blocks * BLOCK, BLOCK), LANES)] = jnp.zeros((8, LANES), F32)

        def expand(r, offset):
            o = offset % LANES
            t = pl.multiple_of(offset - o, LANES)
            both = jnp.where(lane8 >= o, zs[:, pl.ds(t, LANES)], zs[:, pl.ds(t + LANES, LANES)])
            exp_buf[pl.ds(r, 8, stride=rays), :] = pltpu.roll(both, (LANES - o) % LANES, 1)
            return offset + counts[p, r]

        lax.fori_loop(0, rays, expand, jnp.int32(0))

        share = jnp.where(p == 0, COARSE_SHARE, 1.0).astype(F32)
        have = jnp.where(p == 0, col[:, 4:5], col[:, 5:6])
        valid = jnp.where(lane1.astype(F32) < have, 1.0, 0.0)
        ray_mask = col[:, 3:4]
        space = spacing[p] * valid
        zd = exp_buf[3 * rays : 4 * rays, :] - 1.0
        density = jnp.maximum(zd, 0.0) + jnp.log1p(jnp.exp(-jnp.abs(zd)))
        tau = density * space
        inclusive = lane_scan(tau, lane1)
        exclusive = inclusive - tau
        beyond = jnp.exp(-inclusive)
        weights = jnp.exp(-exclusive) - beyond
        weighted = jnp.zeros_like(tau)
        sums = jnp.zeros((rays, 1), F32)
        for c in range(3):
            sig = jax.nn.sigmoid(exp_buf[c * rays : (c + 1) * rays, :])
            rgb = 1.002 * sig - 0.001
            color = jnp.sum(weights * rgb, axis=1, keepdims=True)
            error = color - col[:, c : c + 1]
            sums = sums + error * error
            color_grad = share * (2.0 / 3.0) * error * ray_mask
            weighted = weighted + color_grad * rgb
            grad_buf[c * rays : (c + 1) * rays, :] = weights * color_grad * 1.002 * sig * (1.0 - sig)
        product = weighted * weights
        scanned = lane_scan(product, lane1)
        after = jnp.sum(product, axis=1, keepdims=True) - scanned
        grad_buf[3 * rays : 4 * rays, :] = (beyond * weighted - after) * space * jax.nn.sigmoid(zd)
        loss = loss + share * jnp.sum(sums * (1.0 / 3.0) * ray_mask)

        def pack_back(r, offset):
            here = grad_buf[pl.ds(r, 8, stride=rays), :]
            o = offset % LANES
            t = pl.multiple_of(offset - o, LANES)
            turned = pltpu.roll(here, o, 1)
            gs[:, pl.ds(t, LANES)] = jnp.where(lane8 >= o, turned, gs[:, pl.ds(t, LANES)])
            gs[:, pl.ds(t + LANES, LANES)] = jnp.where(lane8 < o, turned, 0.0)
            return offset + counts[p, r]

        lax.fori_loop(0, rays, pack_back, jnp.int32(0))

        def backward(i, carry):
            at = pl.ds(pl.multiple_of(i * BLOCK, BLOCK), BLOCK)
            dz = gs[:, at].astype(BF16)
            dzw = dz.astype(F32)
            part = dzw[:, 0:LANES]
            for k in range(1, per):
                part = part + dzw[:, k * LANES : (k + 1) * LANES]
            g_sum[...] += part
            dz = jnp.concatenate([dzw, jnp.zeros_like(dzw)], axis=0).astype(BF16)
            dzf = (dot_nn(wr[...], dz) * feat_slope[:, at]).astype(BF16)
            both = jnp.concatenate([dzf, dz], axis=0)
            g_head[...] += dot_nt(both, hidden[2, 0:256, at])
            s_ray[...] += dot_nt(dzf, one_hot[:, at])
            g_rgb[...] += dot_nt(dz, feat[:, at])
            up = dot_nn(whd[...], both)
            for k in (1, 0):
                dzk = (up * slope[k + 1, :, at]).astype(BF16)
                g_mid[k] += dot_nt(hidden[k, :, at], dzk)
                up = dot_nn(wm[k], dzk)
            dz0 = (up * slope[0, :, at]).astype(BF16)
            g_in[...] += dot_nt(enc[:, at], dz0)
            return carry

        lax.fori_loop(0, blocks, backward, 0)
        return loss

    loss = lax.fori_loop(0, 2, one_pass, jnp.zeros((), F32))

    for h in range(2):
        for c in range(3):
            for k in range(2):
                tall[pl.ds(96 * h + 48 * k + c, 16, stride=3), :] = g_in[
                    48 * k + 16 * c : 48 * k + 16 * c + 16, 128 * h : 128 * h + 128
                ]
        packed[0:96, 128 * h : 128 * h + 128] = tall[96 * h : 96 * h + 96, :]
    for k in range(2):
        packed[96 + 256 * k : 352 + 256 * k, :] = g_mid[k, 0:256, :]
    packed[608:736, :] = g_head[0:128, :]
    rays_sum = s_ray[...]
    packed[736:768, :] = jnp.zeros((32, 256), F32)
    packed[736:737, :] = g_in[96:97, :]
    packed[737:738, :] = g_mid[0, 256:257, :]
    packed[738:739, :] = g_mid[1, 256:257, :]
    packed[739:740, :] = g_head[131:132, :]
    feat_b = jnp.sum(rays_sum, axis=1, keepdims=True)
    packed[740:741, 0:128] = jnp.broadcast_to(feat_b, (128, 128)).T[0:1, :]
    small = jnp.sum(g_sum[...], axis=1, keepdims=True)
    lane1r = lax.broadcasted_iota(jnp.int32, (1, LANES), 1)
    line = jnp.zeros((1, LANES), F32)
    for k in range(4):
        line = line + jnp.where(lane1r == k, jnp.broadcast_to(small[k : k + 1, :], (1, LANES)), 0.0)
    line = line + jnp.where(lane1r == 4, loss, 0.0)
    line = line + jnp.where(lane1r == 5, jnp.sum(mask[...].astype(F32)), 0.0)
    packed[740:741, 128:256] = line
    packed[741:744, 0:128] = g_rgb[0:3, :]
    view_grad = jnp.zeros((32, 128), F32)
    for piece in split_three(rays_sum):
        view_grad = view_grad + dot_nt(venc[...], piece)
    packed[744:760, 0:128] = view_grad[0:16, :]
    packed[744:760, 128:256] = view_grad[16:32, :]
    for q in range(4):
        for ref, which in ((keep, 0), (send, 1)):
            source = pl.multiple_of((place[which] ^ q) * PART, 8)
            ref[q * PART : (q + 1) * PART, :] = packed[pl.ds(source, PART), :]


def field_gradients(place, means, variances, spacing, dirs, target, counts, mask, params):
    w_in, w_mid, w_head, w_rgb, vec = params
    rays = dirs.shape[1]
    most = 3 * rays * LANES // 4
    room = most + BLOCK
    vmem = pl.BlockSpec(memory_space=pltpu.VMEM)
    smem = pl.BlockSpec(memory_space=pltpu.SMEM)
    hbm = pl.BlockSpec(memory_space=pl.ANY)
    scratch = [
        pltpu.VMEM((2 * 8 * rays, LANES), F32),
        pltpu.VMEM((8, room), F32),
        pltpu.VMEM((8, room), F32),
        pltpu.VMEM((8, room), F32),
        pltpu.VMEM((128, room), BF16),
        pltpu.VMEM((3, 272, room), BF16),
        pltpu.VMEM((3, 256, room), F32),
        pltpu.VMEM((128, room), BF16),
        pltpu.VMEM((128, room), F32),
        pltpu.VMEM((rays, room), BF16),
        pltpu.VMEM((8 * rays, LANES), F32),
        pltpu.VMEM((8 * rays, LANES), F32),
        pltpu.VMEM((8, LANES), F32),
        pltpu.VMEM((128, 256), F32),
        pltpu.VMEM((192, LANES), F32),
        pltpu.VMEM((256, 128), BF16),
        pltpu.VMEM((2, 256, 256), BF16),
        pltpu.VMEM((2, 256, 256), BF16),
        pltpu.VMEM((144, 256), BF16),
        pltpu.VMEM((256, 144), BF16),
        pltpu.VMEM((16, 128), BF16),
        pltpu.VMEM((128, 16), BF16),
        pltpu.VMEM((2, 256, 128), F32),
        pltpu.VMEM((144, 3 * rays), BF16),
        pltpu.VMEM((32, rays), BF16),
        pltpu.VMEM((128, 256), F32),
        pltpu.VMEM((2, 272, 256), F32),
        pltpu.VMEM((144, 256), F32),
        pltpu.VMEM((16, 128), F32),
        pltpu.VMEM((128, rays), F32),
        pltpu.VMEM((8, LANES), F32),
        pltpu.VMEM((8 * PART, 256), F32),
        pltpu.SemaphoreType.DMA((4,)),
    ]
    return pl.pallas_call(
        field_kernel,
        out_shape=[jax.ShapeDtypeStruct((4 * PART, 256), F32)] * 2,
        in_specs=[smem, smem, hbm, hbm] + [vmem] * 10,
        out_specs=[vmem, vmem],
        scratch_shapes=scratch,
        compiler_params=pltpu.CompilerParams(vmem_limit_bytes=56 << 20),
    )(
        counts,
        place,
        means.reshape(2, 3 * rays, LANES),
        variances.reshape(2, 3 * rays, LANES),
        spacing,
        dirs,
        target,
        mask.reshape(1, rays),
        counts,
        w_in,
        w_mid,
        w_head,
        w_rgb,
        jnp.pad(vec, (0, 16 * LANES - vec.shape[0])).reshape(16, LANES),
    )


def adamw(weight, grad, first, second):
    first = BETA_ONE * first + (1.0 - BETA_ONE) * grad
    second = BETA_TWO * second + (1.0 - BETA_TWO) * grad * grad
    first_hat = first * (1.0 / (1.0 - BETA_ONE**STEP))
    second_hat = second * (1.0 / (1.0 - BETA_TWO**STEP))
    fresh = weight - LEARN_RATE * (first_hat / (jnp.sqrt(second_hat) + EPSILON) + DECAY * weight)
    return first, second, fresh


def update_kernel(place, own, near, pair, other, *refs):
    weights, firsts, seconds = refs[0:5], refs[5:10], refs[10:15]
    loss, count = refs[15], refs[16]
    outs = refs[17:32]
    packed, rgb_t = refs[32:]
    row = 0
    for ref, base in ((own, 0), (near, 1), (pair, 2), (other, 4)):
        for k in range(ref.shape[0] // PART):
            position = base + k
            block = (place[0] ^ position) if position < 4 else (place[1] ^ (position - 4))
            packed[pl.ds(pl.multiple_of(block * PART, 8), PART), :] = ref[k * PART : (k + 1) * PART, :]
    line = packed[740:741, 128:256]
    loss[0] = line[0, 4]
    count[0] = line[0, 5]
    scale = 1.0 / line[0:1, 5:6]

    def apply(group, at, grad):
        made = adamw(weights[group][at], grad * scale, firsts[group][at], seconds[group][at])
        for k in range(3):
            outs[3 * group + k][at] = made[k]

    everything = slice(None)
    apply(0, (everything, everything), packed[0:96, :])
    for k in range(2):
        apply(1, (k, everything, everything), packed[96 + 256 * k : 352 + 256 * k, :])
    apply(2, (slice(0, 256), everything), packed[608:736, :].T)
    apply(2, (slice(256, 272), everything), packed[744:760, 0:128])
    apply(2, (slice(272, 283), everything), packed[744:755, 128:256])
    rgb_t[...] = jnp.zeros_like(rgb_t)
    rgb_t[0:3, :] = packed[741:744, 0:128]
    apply(3, (everything, everything), rgb_t[...].T[:, 0:3])
    for k in range(5):
        apply(4, (slice(2 * k, 2 * k + 1), everything), packed[736 + k : 737 + k, 0:128])
        apply(4, (slice(2 * k + 1, 2 * k + 2), everything), packed[736 + k : 737 + k, 128:256])


def update(place, pieces, params, firsts, seconds):
    vmem = pl.BlockSpec(memory_space=pltpu.VMEM)
    smem = pl.BlockSpec(memory_space=pltpu.SMEM)
    shapes = [jax.ShapeDtypeStruct((1,), F32)] * 2
    for array in params:
        shapes += [jax.ShapeDtypeStruct(array.shape, F32)] * 3
    return pl.pallas_call(
        update_kernel,
        out_shape=shapes,
        in_specs=[smem] + [vmem] * 19,
        out_specs=[smem, smem] + [vmem] * 15,
        scratch_shapes=[pltpu.VMEM((8 * PART, 256), F32), pltpu.VMEM((8, LANES), F32)],
        compiler_params=pltpu.CompilerParams(vmem_limit_bytes=32 << 20),
    )(place, *pieces, *params, *firsts, *seconds)


def xor_pairs(total, mask_of):
    return [(i, i ^ mask_of(i)) for i in range(total)]


def reduce_small(keep, send, axes):
    core = xor_pairs(32, lambda i: 1)
    one = xor_pairs(32, lambda i: 4 if i & 1 else 2)
    two = xor_pairs(32, lambda i: 2 if i & 1 else 4)
    z_one = xor_pairs(32, lambda i: 16 if i & 1 else 8)
    z_two = xor_pairs(32, lambda i: 8 if i & 1 else 16)

    def swap(value, pairs):
        return lax.ppermute(value, axes, pairs)

    now = keep + swap(send, core)
    now = now[: 2 * PART] + swap(now[2 * PART :], one)
    own = now[:PART] + swap(now[PART:], two)
    own = own + swap(own, z_one)
    own = own + swap(own, z_two)
    near = swap(own, two)
    half = jnp.concatenate([own, near], axis=0)
    pair = swap(half, one)
    other = swap(jnp.concatenate([half, pair], axis=0), core)
    return own, near, pair, other


def on_device(
    small_mesh,
    sample_means,
    sample_vars,
    sample_spacing,
    view_dirs,
    target_rgb,
    sample_counts,
    ray_mask,
    w_in,
    w_mid,
    w_head,
    w_rgb,
    vectors,
    first_in,
    first_mid,
    first_head,
    first_rgb,
    first_vec,
    second_in,
    second_mid,
    second_head,
    second_rgb,
    second_vec,
):
    def rows(vector):
        return jnp.pad(vector, (0, 10 * LANES - vector.shape[0])).reshape(10, LANES)

    axes = ("rays", "rep")
    if small_mesh:
        index = lax.axis_index(axes)
        core, x, y = index & 1, (index >> 1) & 1, (index >> 2) & 1
        place = jnp.stack([core * 4 + jnp.where(core == 0, 2 * x + y, 2 * y + x), (1 - core) * 4 + jnp.where(core == 0, 2 * y + x, 2 * x + y)])
    else:
        place = jnp.array([0, 4], jnp.int32)
    place = place.astype(jnp.int32)
    params = (w_in, w_mid, w_head, w_rgb, vectors)
    keep, send = field_gradients(
        place, sample_means, sample_vars, sample_spacing, view_dirs, target_rgb, sample_counts, ray_mask, params
    )
    if small_mesh:
        pieces = reduce_small(keep, send, axes)
    else:
        whole = lax.psum(jnp.concatenate([keep, send], axis=0), axes)
        pieces = (whole[:PART], whole[PART : 2 * PART], whole[2 * PART : 4 * PART], whole[4 * PART :])
    outs = update(
        place,
        pieces,
        (w_in, w_mid, w_head, w_rgb, rows(vectors)),
        (first_in, first_mid, first_head, first_rgb, rows(first_vec)),
        (second_in, second_mid, second_head, second_rgb, rows(second_vec)),
    )
    flat = [out.reshape(-1)[: vectors.shape[0]] for out in outs[14:17]]
    return (outs[0].reshape(()), outs[1].reshape(()), *outs[2:14], *flat)


def solution(mesh):
    rays = ("rays", "rep")
    in_specs = (
        P(None, None, rays, None),
        P(None, None, rays, None),
        P(None, rays, None),
        P(None, rays),
        P(None, rays),
        P(None, rays),
        P(rays),
    ) + (P(),) * 15
    small_mesh = mesh.shape["rays"] == 8 and mesh.shape["rep"] == 4

    def step(*args):
        return on_device(small_mesh, *args)

    return jax.shard_map(step, mesh=mesh, in_specs=in_specs, out_specs=(P(),) * 17, check_vma=False)
```

time: 1710 us -> 112 us (0.07)
  loops' own time: 853 us -> 0 us
  local copies, waits for them, and re-layouts: 454 us -> 4.95 us
  matrix products: 114 us -> 0 us
  other arithmetic: 72.3 us -> 2.48 us
  Pallas kernels: 0 us -> 66.3 us
  waiting for transfers between devices: 88 us -> 29.4 us
  blocking collectives: 54.2 us -> 0 us
  starting transfers between devices: 33.3 us -> 7.97 us
  between operations: 24.8 us -> 0.9 us
    another operation x17 -> x0, loops' own time: 853 us -> none  [the longest x4 504 us: compact_rays(): buffer = lax.fori_loop(0, counts.shape[0], place, buffer)]
    dynamic_slice x690 -> x0, local copies, waits for them, and re-layouts: 256 us -> none  [the longest x256 151 us: place(): offsets[ray_index]]
    dynamic_update_slice x436 -> x0, local copies, waits for them, and re-layouts: 120 us -> none  [the longest x256 76 us: place(): lax.dynamic_update_slice_in_dim(current, piece, offsets[ray_index], 1)]
    dot_general x230 -> x0, matrix products: 114 us -> none  [the longest x100 62 us: contract_rows(): lax.dot_general(left, right, (((0,), (0,)), ((), ())), preferred_element_...]
    psum x1 -> x0, waiting for transfers between devices: 88 us -> none  [on_device(): lax.psum((grads[0], grads[1], grads[2], grads[3], grads[4], loss_sum, cou...]
    pallas_call x0 -> x2, Pallas kernels: none -> 66.3 us  [the longest x1 63.6 us: field_gradients(): pl.pallas_call(field_kernel, out_shape=[jax.ShapeDtypeStruct((4 * PART, 2...]
    psum x1 -> x0, blocking collectives: 41.2 us -> none  [on_device(): lax.psum((grads[0], grads[1], grads[2], grads[3], grads[4], loss_sum, cou...]
    all_to_all x6 -> x0, starting transfers between devices: 33.2 us -> none  [the longest x2 12 us: on_device(): lax.all_to_all(laid_out, 'rays', split_axis=2, concat_axis=2, tiled=True)]
  transfers between devices with their start and end apart: 7 -> 8, of which waited for: 1 -> 8; matrix products, arithmetic and copies ran while one was open for 14% -> 0% of each run, Pallas kernels for 0% -> 0%
where the time goes in v1:
time: 112 us
  Pallas kernels  66.3 us (59%)
  waiting for transfers between devices  29.4 us (26%)
  starting transfers between devices  7.97 us (7%)
  local copies, waits for them, and re-layouts  4.95 us (4%)
  other arithmetic  2.48 us (2%)
    pallas_call x1, Pallas kernels, field_gradients(): pl.pallas_call(field_kernel, out_shape=[jax.ShapeDtypeStruct((4 * PART, 2...  63.6 us
    ppermute x8, waiting for transfers between devices, swap(): return lax.ppermute(value, axes, pairs)  29.4 us
    ppermute x8, starting transfers between devices, swap(): return lax.ppermute(value, axes, pairs)  7.97 us
    unnamed x40, local copies, waits for them, and re-layouts  4.32 us
    pallas_call x1, Pallas kernels, update(): pl.pallas_call(update_kernel, out_shape=shapes, in_specs=[smem] + [vmem]...  2.68 us
  transfers between devices with their start and end apart: 8, of which 8 were waited for; matrix products, arithmetic and copies ran while one was open for 0% of the time, Pallas kernels for 0%

profile of v1, /device:TPU:0, one launch (start us, length us, event | category | flops | bytes accessed | tf_op | source)
XLA Modules:
  0.0 112.1 jit_solution(16921956735897269907)
XLA Ops:
  0.7 0.0 copy-start.11
  0.7 0.7 copy-done.11
  1.4 0.0 copy-start.14
  1.4 0.6 pad_bitcast_fusion.3.vec
  2.0 0.1 copy-done.14
  2.0 0.7 copy.39.w_rgb.refs_3_
  2.8 0.6 pad_add_fusion.place
  3.4 63.6 %shard_map.341 = (f32[384,256]{1,0:T(8,128)}, f32[384,256]{1,0:T(8,128)}) custom-call(s32[2,64]{1,0:T(2,128)} %counts_vec.1, s32[2]{0:T(128)} %pad_add_fusion.place, f32[2,192,128]{2,1,0:T(8,128)} %bitcast.21, f32[2,192,128]{2,1,0:T(8,128)} %bitcast.22, f32[2,64,128]{2,1,0:T(8,128)} %spacing.1, f32[3,64]{1,0:T(4,128)} %dirs.1, f32[3,64]{1,0:T(4,128)} %target.1, ...), custom_call_target="tpu_custom_call" | custom-call | tf_op jit(solution)/shard_map/pallas_call | solution.py:440
  67.0 0.1 collective-permute-start
  67.1 1.9 %collective-permute-done = f32[384,256]{1,0:T(8,128)S(1)} collective-permute-done((f32[384,256]{1,0:T(8,128)}, f32[384,256]{1,0:T(8,128)S(1)}, u32[]{:S(2)}, u32[]{:S(2)}) %collective-permute-start) | collective-permute-done | bytes 393248 | tf_op jit(solution)/shard_map/ppermute | solution.py:538
  69.0 1.0 add.45
  70.1 0.1 collective-permute-start.1
  70.2 5.7 %collective-permute-done.1 = f32[192,256]{1,0:T(8,128)S(1)} collective-permute-done((f32[192,256]{1,0:T(8,128)S(1)}, f32[192,256]{1,0:T(8,128)S(1)}, u32[]{:S(2)}, u32[]{:S(2)}) %collective-permute-start.1) | collective-permute-done | bytes 196640 | tf_op jit(solution)/shard_map/ppermute | solution.py:538
  75.9 0.0 copy-start.8
  75.9 0.0 copy-start.9
  75.9 0.1 collective-permute-start.2
  76.0 4.6 %collective-permute-done.2 = f32[96,256]{1,0:T(8,128)S(1)} collective-permute-done((f32[96,256]{1,0:T(8,128)S(1)}, f32[96,256]{1,0:T(8,128)S(1)}, u32[]{:S(2)}, u32[]{:S(2)}) %collective-permute-start.2) | collective-permute-done | bytes 98336 | tf_op jit(solution)/shard_map/ppermute | solution.py:538
  80.6 0.0 copy-start.6
  80.6 0.0 copy-start.7
  80.6 2.1 %collective-permute-start.3 = (f32[96,256]{1,0:T(8,128)S(1)}, f32[96,256]{1,0:T(8,128)S(1)}, u32[]{:S(2)}, u32[]{:S(2)}) collective-permute-start(f32[96,256]{1,0:T(8,128)S(1)} %slice_add_fusion.1), channel_id=1, source_target_pairs={{0,8},{1,17},{2,10},{3,19},{4,12},{5,21},{6,14},{7,23},{8,0},{9,25... | collective-permute-start | bytes 294920 | tf_op jit(solution)/shard_map/ppermute | solution.py:538
  82.7 3.0 %collective-permute-done.3 = f32[96,256]{1,0:T(8,128)S(1)} collective-permute-done((f32[96,256]{1,0:T(8,128)S(1)}, f32[96,256]{1,0:T(8,128)S(1)}, u32[]{:S(2)}, u32[]{:S(2)}) %collective-permute-start.3) | collective-permute-done | bytes 98336 | tf_op jit(solution)/shard_map/ppermute | solution.py:538
  85.7 0.0 copy-start.4
  85.7 3.2 %collective-permute-start.4 = (f32[96,256]{1,0:T(8,128)S(1)}, f32[96,256]{1,0:T(8,128)S(1)}, u32[]{:S(2)}, u32[]{:S(2)}) collective-permute-start(f32[96,256]{1,0:T(8,128)S(1)} %add.48), channel_id=1, source_target_pairs={{0,16},{1,9},{2,18},{3,11},{4,20},{5,13},{6,22},{7,15},{8,24},{9,1... | collective-permute-start | bytes 294920 | tf_op jit(solution)/shard_map/ppermute | solution.py:538
  88.9 3.6 %collective-permute-done.4 = f32[96,256]{1,0:T(8,128)S(1)} collective-permute-done((f32[96,256]{1,0:T(8,128)S(1)}, f32[96,256]{1,0:T(8,128)S(1)}, u32[]{:S(2)}, u32[]{:S(2)}) %collective-permute-start.4) | collective-permute-done | bytes 98336 | tf_op jit(solution)/shard_map/ppermute | solution.py:538
  92.5 0.0 copy-start.12
  92.5 0.0 copy-start.13
  92.6 0.4 collective-permute-start.5
  93.0 5.3 %collective-permute-done.5.near = f32[96,256]{1,0:T(8,128)S(1)} collective-permute-done((f32[96,256]{1,0:T(8,128)S(1)}, f32[96,256]{1,0:T(8,128)S(1)}, u32[]{:S(2)}, u32[]{:S(2)}) %collective-permute-start.5) | collective-permute-done | bytes 98336 | tf_op jit(solution)/shard_map/ppermute | solution.py:538
  98.3 0.0 copy-start.3
  98.3 0.0 copy-start.15
  98.3 0.0 copy-start
  98.3 2.1 %collective-permute-start.6 = (f32[192,256]{1,0:T(8,128)S(1)}, f32[192,256]{1,0:T(8,128)S(1)}, u32[]{:S(2)}, u32[]{:S(2)}) collective-permute-start(f32[192,256]{1,0:T(8,128)S(1)} %pad_maximum_fusion.1), channel_id=1, source_target_pairs={{0,2},{1,5},{2,0},{3,7},{4,6},{5,1},{6,4},{7,3},{8,10},{9,13},{10,... | collective-permute-start | bytes 589832 | tf_op jit(solution)/shard_map/ppermute | solution.py:538
  100.4 3.6 %collective-permute-done.6.pair = f32[192,256]{1,0:T(8,128)S(1)} collective-permute-done((f32[192,256]{1,0:T(8,128)S(1)}, f32[192,256]{1,0:T(8,128)S(1)}, u32[]{:S(2)}, u32[]{:S(2)}) %collective-permute-start.6) | collective-permute-done | bytes 196640 | tf_op jit(solution)/shard_map/ppermute | solution.py:538
  104.0 0.0 copy-start.16
  104.0 0.0 copy-start.2
  104.0 0.0 copy-start.5
  104.1 0.8 pad_maximum_fusion
  104.8 0.0 copy-start.1
  104.8 0.0 collective-permute-start.7
  104.8 0.0 copy-done.15
  104.8 0.1 copy.41.refs_8_
  104.9 0.0 copy-done.16
  104.9 0.1 copy.42.refs_13_
  105.1 0.0 copy-done.12
  105.1 0.0 copy-done.13
  105.1 1.7 %collective-permute-done.7.other = f32[384,256]{1,0:T(8,128)S(1)} collective-permute-done((f32[384,256]{1,0:T(8,128)}, f32[384,256]{1,0:T(8,128)S(1)}, u32[]{:S(2)}, u32[]{:S(2)}) %collective-permute-start.7) | collective-permute-done | bytes 393248 | tf_op jit(solution)/shard_map/ppermute | solution.py:538
  106.8 0.0 copy-start.10
  106.8 0.0 copy-done.8
  106.8 0.0 copy-done.9
  106.8 0.0 copy-done.6
  106.8 0.0 copy-done.7
  106.8 0.0 copy-done.4
  106.8 0.0 copy-done.3
  106.8 0.0 copy-done
  106.8 0.0 copy-done.2
  106.8 0.0 copy-done.5
  106.8 0.0 copy-done.1
  106.8 0.6 copy-done.10
  107.4 2.7 %shard_map.342 = (f32[1]{0:T(128)}, f32[1]{0:T(128)}, f32[96,256]{1,0:T(8,128)}, f32[96,256]{1,0:T(8,128)}, f32[96,256]{1,0:T(8,128)}, /*index=5*/f32[2,256,256]...) custom-call(s32[2]{0:T(128)S(1)} %copy-done.10, ...), custom_call_target="tpu_custom_call" | custom-call | tf_op jit(solution)/shard_map/pallas_call | solution.py:516
  110.1 0.7 copy.43
  110.8 0.7 copy.44
  111.4 0.7 copy.45
  (9 shorter events, 0.1 us)
Async XLA Ops:
  0.7 0.7 copy-start.11
  1.4 0.7 copy-start.14
  67.0 2.0 %collective-permute-start = (f32[384,256]{1,0:T(8,128)}, f32[384,256]{1,0:T(8,128)S(1)}, u32[]{:S(2)}, u32[]{:S(2)}) collective-permute-start(f32[384,256]{1,0:T(8,128)} %get-tuple-element.37), channel_id=1, source_target_pairs={{0,1},{1,0},{2,3},{3,2},{4,5},{5,4},{6,7},{7,6},{8,9},{9,8},{10,11... | collective-permute-start | bytes 1179656 | tf_op jit(solution)/shard_map/ppermute | solution.py:538
  70.1 5.7 %collective-permute-start.1 = (f32[192,256]{1,0:T(8,128)S(1)}, f32[192,256]{1,0:T(8,128)S(1)}, u32[]{:S(2)}, u32[]{:S(2)}) collective-permute-start(f32[192,256]{1,0:T(8,128)S(1)} %slice.29), channel_id=1, source_target_pairs={{0,2},{1,5},{2,0},{3,7},{4,6},{5,1},{6,4},{7,3},{8,10},{9,13},{10,... | collective-permute-start | bytes 589832 | tf_op jit(solution)/shard_map/ppermute | solution.py:538
  75.9 30.9 %copy-start.8 = (f32[96,256]{1,0:T(8,128)S(1)}, f32[96,256]{1,0:T(8,128)}, u32[]{:S(2)}) copy-start(f32[96,256]{1,0:T(8,128)} %refs_5_.1) | copy-start | bytes 294916
  75.9 30.9 %copy-start.9 = (f32[96,256]{1,0:T(8,128)S(1)}, f32[96,256]{1,0:T(8,128)}, u32[]{:S(2)}) copy-start(f32[96,256]{1,0:T(8,128)} %refs_10_.1) | copy-start | bytes 294916
  75.9 4.7 %collective-permute-start.2 = (f32[96,256]{1,0:T(8,128)S(1)}, f32[96,256]{1,0:T(8,128)S(1)}, u32[]{:S(2)}, u32[]{:S(2)}) collective-permute-start(f32[96,256]{1,0:T(8,128)S(1)} %slice.31), channel_id=1, source_target_pairs={{0,4},{1,3},{2,6},{3,1},{4,0},{5,7},{6,2},{7,5},{8,12},{9,11},{10,... | collective-permute-start | bytes 294920 | tf_op jit(solution)/shard_map/ppermute | solution.py:538
  80.6 26.2 %copy-start.6 = (f32[283,128]{1,0:T(8,128)S(1)}, f32[283,128]{1,0:T(8,128)}, u32[]{:S(2)}) copy-start(f32[283,128]{1,0:T(8,128)} %refs_7_.1) | copy-start | bytes 434692
  80.6 26.2 %copy-start.7 = (f32[283,128]{1,0:T(8,128)S(1)}, f32[283,128]{1,0:T(8,128)}, u32[]{:S(2)}) copy-start(f32[283,128]{1,0:T(8,128)} %refs_12_.1) | copy-start | bytes 434692
  80.6 5.1 %collective-permute-start.3 = (f32[96,256]{1,0:T(8,128)S(1)}, f32[96,256]{1,0:T(8,128)S(1)}, u32[]{:S(2)}, u32[]{:S(2)}) collective-permute-start(f32[96,256]{1,0:T(8,128)S(1)} %slice_add_fusion.1), channel_id=1, source_target_pairs={{0,8},{1,17},{2,10},{3,19},{4,12},{5,21},{6,14},{7,23},{8,0},{9,25... | collective-permute-start | bytes 294920 | tf_op jit(solution)/shard_map/ppermute | solution.py:538
  85.7 21.1 %copy-start.4 = (f32[2,256,256]{2,1,0:T(8,128)S(1)}, f32[2,256,256]{2,1,0:T(8,128)}, u32[]{:S(2)}) copy-start(f32[2,256,256]{2,1,0:T(8,128)} %refs_11_.1) | copy-start | bytes 1572868
  85.7 6.8 %collective-permute-start.4 = (f32[96,256]{1,0:T(8,128)S(1)}, f32[96,256]{1,0:T(8,128)S(1)}, u32[]{:S(2)}, u32[]{:S(2)}) collective-permute-start(f32[96,256]{1,0:T(8,128)S(1)} %add.48), channel_id=1, source_target_pairs={{0,16},{1,9},{2,18},{3,11},{4,20},{5,13},{6,22},{7,15},{8,24},{9,1... | collective-permute-start | bytes 294920 | tf_op jit(solution)/shard_map/ppermute | solution.py:538
  92.5 12.5 %copy-start.12 = (f32[1156]{0:T(1024)S(1)}, f32[1156]{0:T(1024)}, u32[]{:S(2)}) copy-start(f32[1156]{0:T(1024)} %param.43) | copy-start | bytes 13876
  92.5 12.5 %copy-start.13 = (f32[1156]{0:T(1024)S(1)}, f32[1156]{0:T(1024)}, u32[]{:S(2)}) copy-start(f32[1156]{0:T(1024)} %param.38) | copy-start | bytes 13876
  92.6 5.7 %collective-permute-start.5 = (f32[96,256]{1,0:T(8,128)S(1)}, f32[96,256]{1,0:T(8,128)S(1)}, u32[]{:S(2)}, u32[]{:S(2)}) collective-permute-start(f32[96,256]{1,0:T(8,128)S(1)} %add.49.own), channel_id=1, source_target_pairs={{0,4},{1,3},{2,6},{3,1},{4,0},{5,7},{6,2},{7,5},{8,12},{9,11},{10,... | collective-permute-start | bytes 294920 | tf_op jit(solution)/shard_map/ppermute | solution.py:538
  98.3 8.5 %copy-start.3 = (f32[2,256,256]{2,1,0:T(8,128)S(1)}, f32[2,256,256]{2,1,0:T(8,128)}, u32[]{:S(2)}) copy-start(f32[2,256,256]{2,1,0:T(8,128)} %refs_6_.1) | copy-start | bytes 1572868
  98.3 6.6 %copy-start.15 = (f32[128,3]{0,1:T(4,128)S(1)}, f32[128,3]{0,1:T(4,128)}, u32[]{:S(2)}) copy-start(f32[128,3]{0,1:T(4,128)} %param.37) | copy-start | bytes 4612
  98.3 8.5 %copy-start = (f32[2,256,256]{2,1,0:T(8,128)S(1)}, f32[2,256,256]{2,1,0:T(8,128)}, u32[]{:S(2)}) copy-start(f32[2,256,256]{2,1,0:T(8,128)} %refs_1_.1) | copy-start | bytes 1572868
  98.3 5.7 %collective-permute-start.6 = (f32[192,256]{1,0:T(8,128)S(1)}, f32[192,256]{1,0:T(8,128)S(1)}, u32[]{:S(2)}, u32[]{:S(2)}) collective-permute-start(f32[192,256]{1,0:T(8,128)S(1)} %pad_maximum_fusion.1), channel_id=1, source_target_pairs={{0,2},{1,5},{2,0},{3,7},{4,6},{5,1},{6,4},{7,3},{8,10},{9,13},{10,... | collective-permute-start | bytes 589832 | tf_op jit(solution)/shard_map/ppermute | solution.py:538
  104.0 0.9 copy-start.16
  104.0 2.8 %copy-start.2 = (f32[128,3]{1,0:T(8,128)S(1)}, f32[128,3]{1,0:T(8,128)}, u32[]{:S(2)}) copy-start(f32[128,3]{1,0:T(8,128)} %copy.39.w_rgb.refs_3_) | copy-start | bytes 4612
  104.0 2.8 %copy-start.5 = (f32[96,256]{1,0:T(8,128)S(1)}, f32[96,256]{1,0:T(8,128)}, u32[]{:S(2)}) copy-start(f32[96,256]{1,0:T(8,128)} %refs_0_.1) | copy-start | bytes 294916
  104.8 2.0 %copy-start.1 = (f32[283,128]{1,0:T(8,128)S(1)}, f32[283,128]{1,0:T(8,128)}, u32[]{:S(2)}) copy-start(f32[283,128]{1,0:T(8,128)} %refs_2_.1) | copy-start | bytes 434692
  104.8 1.9 %collective-permute-start.7 = (f32[384,256]{1,0:T(8,128)}, f32[384,256]{1,0:T(8,128)S(1)}, u32[]{:S(2)}, u32[]{:S(2)}) collective-permute-start(f32[384,256]{1,0:T(8,128)} %pad_maximum_fusion), channel_id=1, source_target_pairs={{0,1},{1,0},{2,3},{3,2},{4,5},{5,4},{6,7},{7,6},{8,9},{9,8},{10,11... | collective-permute-start | bytes 1179656 | tf_op jit(solution)/shard_map/ppermute | solution.py:538
  106.8 0.7 copy-start.10

commit v2 on v1

v2 whole, which is shorter than its diff:
```python
import math

import jax
import jax.numpy as jnp
from jax import lax
from jax.experimental import pallas as pl
from jax.experimental.pallas import tpu as pltpu
from jax.sharding import PartitionSpec as P

L_POS = 16
L_DIR = 4
STEP = 7
LEARN_RATE = 0.05
BETA_ONE = 0.9
BETA_TWO = 0.999
EPSILON = 1e-08
DECAY = 0.01
COARSE_SHARE = 0.1

BLOCK = 1024
REST = 512
LANES = 128
PART = 96

TURN_HEAD = 0.1591796875
TURN_REST = 1.0 / (2.0 * math.pi) - TURN_HEAD
SIN_POLY = (3.1415926343, -5.1677091056, 2.5500551036, -0.5981303017, 0.0773037189)
COS_POLY = (0.9999999314, -4.9347894708, 4.0583337486, -1.3313191807, 0.2184639082)

F32 = jnp.float32
BF16 = jnp.bfloat16


def split_three(values):
    head = values.astype(BF16)
    rest = values - head.astype(F32)
    middle = rest.astype(BF16)
    tail = (rest - middle.astype(F32)).astype(BF16)
    return head, middle, tail


def dot_nt(left, right):
    return lax.dot_general(left, right, (((1,), (1,)), ((), ())), preferred_element_type=F32)


def dot_nn(left, right):
    return jnp.dot(left, right, preferred_element_type=F32)


def poly(coefficients, square):
    total = jnp.full_like(square, coefficients[-1])
    for c in coefficients[-2::-1]:
        total = total * square + c
    return total


def sin_cos_turns(r):
    square = r * r
    s = r * poly(SIN_POLY, square)
    c = poly(COS_POLY, square)
    return (s + s) * c, 1.0 - (s + s) * s


def field_kernel(
    counts,
    counts_two,
    place,
    means,
    means_two,
    variances,
    variances_two,
    spacing,
    spacing_two,
    dirs,
    dirs_two,
    target,
    target_two,
    mask,
    mask_two,
    w_in,
    w_mid,
    w_head,
    w_rgb_t,
    vec,
    keep,
    send,
    pk,
    xs,
    x_planes,
    z_planes,
    g_planes,
    enc,
    hidden,
    pre,
    feat,
    feat_pre,
    one_hot,
    rows,
    wide,
    w0t,
    wmt,
    wm,
    wht,
    whd,
    wrt,
    wr,
    bias_b,
    view_t,
    venc,
    g_in,
    g_mid,
    g_head,
    g_rgb,
    s_ray,
    g_sum,
    packed,
    sem,
):
    rays = dirs.shape[1]
    own = rays // 2
    tiles = z_planes.shape[0] // 8
    copies = []
    for p in range(2):
        for k, pair in enumerate((means, means_two, variances, variances_two)):
            first, base = (0, 0) if k % 2 == 0 else (own, own)
            for c in range(3):
                to = (p * 8 + 4 * (k // 2) + c) * rays + base
                copies.append((pair.at[p, c, pl.ds(first, own)], pk.at[pl.ds(to, own)]))
        for k, pair in enumerate((spacing, spacing_two)):
            copies.append((pair.at[p, pl.ds(k * own, own)], pk.at[pl.ds((p * 8 + 7) * rays + k * own, own)]))
    copies = [pltpu.make_async_copy(a, b, sem.at[k]) for k, (a, b) in enumerate(copies)]
    for copy in copies:
        copy.start()

    half = 0.5
    rows[...] = jnp.zeros_like(rows)
    for k in range(9):
        rows[k : k + 1, :] = vec[pl.ds(k * LANES, LANES)].reshape(1, LANES)
    rows[9:10, 0:4] = vec[pl.ds(9 * LANES, 4)].reshape(1, 4)
    vec_t = rows[0:16, :].T
    wide[0:128, :] = jnp.zeros((128, 256), F32)
    rounded = w_in[...].astype(BF16).astype(F32) * half
    for a in range(4):
        for d in range(4):
            for k in range(2):
                to, at = 64 * k + 16 * d + 4 * a, 48 * k + 12 * a + 3 * d
                wide[to : to + 3, :] = rounded[at : at + 3, :]
    b0 = jnp.concatenate([rows[0:1, :], rows[1:2, :]], axis=1) * half
    for a, piece in enumerate(split_three(b0)):
        wide[67 + 4 * a : 68 + 4 * a, :] = piece.astype(F32)
    w0t[...] = wide[0:128, :].T.astype(BF16)
    for k in range(2):
        rounded = w_mid[k].astype(BF16).astype(F32) * half
        wm[k] = rounded.astype(BF16)
        wmt[k] = rounded.T.astype(BF16)
        bias_b[k, 0:128, :] = jnp.broadcast_to(vec_t[:, 2 + 2 * k : 3 + 2 * k], (128, 128)) * half
        bias_b[k, 128:256, :] = jnp.broadcast_to(vec_t[:, 3 + 2 * k : 4 + 2 * k], (128, 128)) * half
    top = (w_head[0:256, :].astype(BF16).astype(F32) * half).T
    u_row = jnp.concatenate([rows[6:7, :], rows[7:8, :]], axis=1).astype(BF16).astype(F32)
    row16 = lax.broadcasted_iota(jnp.int32, (16, 256), 0)
    last = jnp.where(row16 == 3, u_row, 0.0)
    wht[0:128, :] = top.astype(BF16)
    wht[128:144, :] = last.astype(BF16)
    whd[...] = jnp.concatenate([top, last * half], axis=0).T.astype(BF16)
    wide[0:16, 0:128] = jnp.zeros((16, 128), F32)
    wide[0:3, 0:128] = w_rgb_t[...].astype(BF16).astype(F32)
    wrt[...] = wide[0:16, 0:128].astype(BF16)
    wr[...] = (wide[0:16, 0:128].T * half).astype(BF16)

    def both_halves(at, one, two):
        wide[at : at + one.shape[0], 0:own] = one[:, 0:own].astype(F32)
        wide[at : at + one.shape[0], own:rays] = two[:, own:rays].astype(F32)

    wide[0:32, 0:128] = jnp.zeros((32, 128), F32)
    both_halves(0, dirs, dirs_two)
    d = wide[0:3, 0:rays]
    for l in range(L_DIR):
        wide[3 + 3 * l : 6 + 3 * l, 0:rays] = jnp.sin(d * (2.0**l))
        wide[15 + 3 * l : 18 + 3 * l, 0:rays] = jnp.cos(d * (2.0**l))
    venc[...] = wide[0:32, 0:rays].astype(BF16)
    wide[0:32, 128:256] = jnp.zeros((32, 128), F32)
    wide[0:27, 128:256] = w_head[256:283, :].astype(BF16).astype(F32)
    view = lax.dot_general(
        wide[0:32, 128:256].astype(BF16), venc[...], (((0,), (0,)), ((), ())), preferred_element_type=F32
    )
    view = (view + vec_t[:, 8:9]) * half
    wide[0:16, 0:128] = jnp.zeros((16, 128), F32)
    wide[0:4, 0:rays] = jnp.broadcast_to(vec_t[0:4, 9:10], (4, rays))
    both_halves(4, target, target_two)
    both_halves(7, mask, mask_two)
    count_here = jnp.sum(wide[7:8, 0:128])
    view_t[...] = jnp.concatenate(split_three(jnp.concatenate([view, wide[0:16, 0:rays]], axis=0)), axis=1)

    one_row = (lax.broadcasted_iota(jnp.int32, (16, LANES), 0) == 0).astype(BF16)

    def fill(t, carry):
        s = pl.multiple_of(t * LANES, LANES)
        for k in range(2):
            hidden[k, 256:272, pl.ds(s, LANES)] = one_row
        return carry

    lax.fori_loop(0, tiles, fill, 0)
    for ref in (g_planes, g_in, g_mid, g_head, g_rgb, s_ray, g_sum):
        ref[...] = jnp.zeros_like(ref)

    lane8 = lax.broadcasted_iota(jnp.int32, (8, LANES), 1)
    sub8 = lax.broadcasted_iota(jnp.int32, (8, LANES), 0)
    sub16 = lax.broadcasted_iota(jnp.int32, (16, LANES), 0)
    anchor = (jnp.int32(1) << (4 * (sub16 // 4))).astype(F32)
    decay_rate = anchor * anchor * (-0.5)

    for copy in copies:
        copy.wait()

    def count_of(p, r):
        return jnp.where(r < own, counts[p, r], counts_two[p, r])

    def forward_block(start, size):
        at = pl.ds(pl.multiple_of(start, LANES), size)
        per = size // LANES

        def wide_of(tile):
            return jnp.concatenate([tile] * per, axis=1)

        def activate(y, pre_ref, h_ref):
            pre_ref[...] = y
            h = (y * (1.0 + jnp.tanh(y))).astype(BF16)
            h_ref[...] = h
            return h

        x = xs[:, at]
        tile_at = start // LANES
        for k in range(per):
            x_planes[pl.ds(tile_at + k, 8, stride=tiles), :] = x[:, k * LANES : (k + 1) * LANES]
        sub = lax.broadcasted_iota(jnp.int32, (8, size), 0)
        turned = pltpu.roll(x, 4, 0)
        low = sub < 4
        used = sub % 4 < 3
        mean = jnp.where(used, jnp.where(low, x, turned), 0.0)
        var = jnp.where(used, jnp.where(low, turned, x), 0.0)
        m1 = jnp.round(mean * 2.0**11) * 2.0**-11
        p1 = m1 * TURN_HEAD
        p2 = m1 * TURN_REST + (mean - m1) * (TURN_HEAD + TURN_REST)
        hi = jnp.round((p1 + p2) * 2.0**20) * 2.0**-20
        lo = (p1 - hi) + p2
        pw = wide_of(anchor)
        a = jnp.concatenate([hi, hi], axis=0) * pw
        a = (a - jnp.round(a)) + jnp.concatenate([lo, lo], axis=0) * pw
        s, c = sin_cos_turns(a)
        var = jnp.concatenate([var, var], axis=0) * wide_of(decay_rate)
        for d in range(4):
            damp = jnp.exp(var * (4.0**d))
            enc[16 * d : 16 * d + 16, at] = (s * damp).astype(BF16)
            enc[64 + 16 * d : 80 + 16 * d, at] = (c * damp).astype(BF16)
            twice = s + s
            s, c = twice * c, 1.0 - twice * s
        item = x[3:4, :]
        ray = jnp.where(item >= rays, item - rays, item)
        hit = jnp.broadcast_to(ray, (rays, size)) == lax.broadcasted_iota(jnp.int32, (rays, size), 0).astype(F32)
        hot = jnp.where(hit, 1.0, 0.0).astype(BF16)
        one_hot[:, at] = hot
        h = activate(dot_nn(w0t[...], enc[:, at]), pre.at[0, :, at], hidden.at[0, 0:256, at])
        for k in range(2):
            y = dot_nn(wmt[k], h) + wide_of(bias_b[k])
            h = activate(y, pre.at[k + 1, :, at], hidden.at[k + 1, 0:256, at])
        y = dot_nn(wht[...], h) + dot_nn(view_t[...], jnp.concatenate([hot, hot, hot], axis=0))
        f = activate(y[0:128, :], feat_pre.at[:, at], feat.at[:, at])
        z = dot_nn(wrt[...], f)[0:8, :] + y[128:136, :]
        for k in range(per):
            z_planes[pl.ds(tile_at + k, 8, stride=tiles), :] = z[:, k * LANES : (k + 1) * LANES]

    def backward_block(start, size):
        at = pl.ds(pl.multiple_of(start, LANES), size)
        per = size // LANES
        tile_at = start // LANES

        def slope(y):
            a = jnp.tanh(y)
            return (1.0 + a) * (1.0 + y * (1.0 - a))

        dz = jnp.concatenate([g_planes[pl.ds(tile_at + k, 8, stride=tiles), :] for k in range(per)], axis=1)
        dzw = dz.astype(BF16).astype(F32)
        part = dzw[:, 0:LANES]
        for k in range(1, per):
            part = part + dzw[:, k * LANES : (k + 1) * LANES]
        g_sum[...] += part
        dz = jnp.concatenate([dzw, jnp.zeros_like(dzw)], axis=0).astype(BF16)
        dzf = (dot_nn(wr[...], dz) * slope(feat_pre[:, at])).astype(BF16)
        both = jnp.concatenate([dzf, dz], axis=0)
        g_head[...] += dot_nt(both, hidden[2, 0:256, at])
        s_ray[...] += dot_nt(dzf, one_hot[:, at])
        g_rgb[...] += dot_nt(dz, feat[:, at])
        up = dot_nn(whd[...], both)
        for k in (1, 0):
            dzk = (up * slope(pre[k + 1, :, at])).astype(BF16)
            g_mid[k] += dot_nt(hidden[k, :, at], dzk)
            up = dot_nn(wm[k], dzk)
        dz0 = (up * slope(pre[0, :, at])).astype(BF16)
        g_in[...] += dot_nt(enc[:, at], dz0)

    def over_blocks(block, total):
        large = (total + (BLOCK - REST - 1)) // BLOCK
        small = jnp.where(total > large * BLOCK, 1, 0)

        def at_large(i, carry):
            block(i * BLOCK, BLOCK)
            return carry

        def at_small(i, carry):
            block(large * BLOCK, REST)
            return carry

        lax.fori_loop(0, large, at_large, 0)
        lax.fori_loop(0, small, at_small, 0)

    group = 8

    def chunk(first, items, loss):
        xs[...] = jnp.where(lax.broadcasted_iota(jnp.int32, xs.shape, 0) == 3, -1.0, 0.0)
        x_planes[...] = jnp.full_like(x_planes, -1.0)

        def pack(g, offset):
            base = first + g * group
            p = base // rays
            r0 = base - p * rays
            moved = []
            for j in range(group):
                count = count_of(p, r0 + j)
                here = pk[pl.ds(p * 8 * rays + r0 + j, 8, stride=rays), :]
                item = jnp.where(lane8 < count, (base + j).astype(F32), -1.0)
                here = jnp.where(sub8 == 3, item, here)
                o = offset % LANES
                moved.append((pltpu.roll(here, o, 1), o, pl.multiple_of(offset - o, LANES)))
                offset = offset + count
            for turned, o, t in moved:
                keep_low = lane8 >= o
                pltpu.store(xs.at[:, pl.ds(t, LANES)], turned, mask=keep_low)
                pltpu.store(xs.at[:, pl.ds(t + LANES, LANES)], turned, mask=jnp.logical_not(keep_low))
            return offset

        total = lax.fori_loop(0, items // group, pack, jnp.int32(0))
        over_blocks(forward_block, total)

        def plane(ref, k):
            return ref[k * tiles : (k + 1) * tiles, :]

        lane = lax.broadcasted_iota(jnp.int32, (tiles, LANES), 1)
        row = lax.broadcasted_iota(jnp.int32, (tiles, LANES), 0)
        item = plane(x_planes, 3)
        valid = item >= 0.0
        steps = (1, 2, 4, 8, 16, 32, 64)
        back = [jnp.logical_and(lane >= k, pltpu.roll(item, k, 1) == item) for k in steps]
        ahead = [jnp.logical_and(lane < LANES - k, pltpu.roll(item, LANES - k, 1) == item) for k in steps]
        end_before = jnp.broadcast_to(pltpu.roll(item[:, LANES - 1 : LANES], 1, 0), (tiles, LANES))
        start_after = jnp.broadcast_to(pltpu.roll(item[:, 0:1], tiles - 1, 0), (tiles, LANES))
        from_before = jnp.logical_and(row > 0, end_before == item)
        from_after = jnp.logical_and(row < tiles - 1, start_after == item)

        def scan(values):
            for k, near in zip(steps, back):
                values = values + jnp.where(near, pltpu.roll(values, k, 1), 0.0)
            carry = jnp.broadcast_to(pltpu.roll(values[:, LANES - 1 : LANES], 1, 0), (tiles, LANES))
            return values + jnp.where(from_before, carry, 0.0)

        def scan_back(values):
            for k, near in zip(steps, ahead):
                values = values + jnp.where(near, pltpu.roll(values, LANES - k, 1), 0.0)
            carry = jnp.broadcast_to(pltpu.roll(values[:, 0:1], tiles - 1, 0), (tiles, LANES))
            return values + jnp.where(from_after, carry, 0.0)

        def z_plane(k):
            return jnp.where(valid, plane(z_planes, k), 0.0)

        share = jnp.where(item >= rays, 1.0, COARSE_SHARE) * z_plane(7)
        space = jnp.where(valid, plane(x_planes, 7), 0.0)
        zd = z_plane(3) - 1.0
        density = jnp.maximum(zd, 0.0) + jnp.log1p(jnp.exp(-jnp.abs(zd)))
        tau = density * space
        inclusive = scan(tau)
        exclusive = inclusive - tau
        beyond = jnp.exp(-inclusive)
        weights = jnp.exp(-exclusive) - beyond
        weighted = jnp.zeros_like(tau)
        sums = jnp.zeros_like(tau)
        for c in range(3):
            sig = jax.nn.sigmoid(z_plane(c))
            rgb = 1.002 * sig - 0.001
            part = weights * rgb
            color = scan(part) + (scan_back(part) - part)
            error = color - z_plane(4 + c)
            sums = sums + error * error
            color_grad = (2.0 / 3.0) * share * error
            weighted = weighted + color_grad * rgb
            d_color = weights * color_grad * 1.002 * sig * (1.0 - sig)
            g_planes[c * tiles : (c + 1) * tiles, :] = jnp.where(valid, d_color, 0.0)
        product = jnp.where(valid, weighted * weights, 0.0)
        after = scan_back(product) - product
        d_density = (beyond * weighted - after) * space * jax.nn.sigmoid(zd)
        g_planes[3 * tiles : 4 * tiles, :] = jnp.where(valid, d_density, 0.0)
        previous = jnp.where(lane >= 1, pltpu.roll(item, 1, 1), jnp.where(row > 0, end_before, -2.0))
        begins = jnp.logical_and(previous != item, valid)
        loss = loss + jnp.sum(jnp.where(begins, sums * share, 0.0)) * (1.0 / 3.0)

        over_blocks(backward_block, total)
        return loss

    def add_counts(r, total):
        return total + count_of(0, r) + count_of(1, r)

    everything = lax.fori_loop(0, rays, add_counts, jnp.int32(0), unroll=8)
    at_once = everything <= tiles * LANES
    chunks = jnp.where(at_once, 1, 2)
    items = jnp.where(at_once, 2 * rays, rays)
    loss = lax.fori_loop(0, chunks, lambda i, loss: chunk(i * rays, items, loss), jnp.zeros((), F32))

    for a in range(4):
        for d in range(4):
            for k in range(2):
                at, to = 64 * k + 16 * d + 4 * a, 48 * k + 12 * a + 3 * d
                packed[to : to + 3, :] = g_in[at : at + 3, :]
    for k in range(2):
        packed[96 + 256 * k : 352 + 256 * k, :] = g_mid[k, 0:256, :]
    packed[608:736, :] = g_head[0:128, :]
    rays_sum = s_ray[...]
    packed[736:768, :] = jnp.zeros((32, 256), F32)
    packed[736:737, :] = g_in[67:68, :]
    packed[737:738, :] = g_mid[0, 256:257, :]
    packed[738:739, :] = g_mid[1, 256:257, :]
    packed[739:740, :] = g_head[131:132, :]
    feat_b = jnp.sum(rays_sum, axis=1, keepdims=True)
    packed[740:741, 0:128] = jnp.broadcast_to(feat_b, (128, 128)).T[0:1, :]
    small = jnp.sum(g_sum[...], axis=1, keepdims=True)
    lane1 = lax.broadcasted_iota(jnp.int32, (1, LANES), 1)
    line = jnp.zeros((1, LANES), F32)
    for k in range(4):
        line = line + jnp.where(lane1 == k, jnp.broadcast_to(small[k : k + 1, :], (1, LANES)), 0.0)
    line = line + jnp.where(lane1 == 4, loss, 0.0)
    line = line + jnp.where(lane1 == 5, count_here, 0.0)
    packed[740:741, 128:256] = line
    packed[741:744, 0:128] = g_rgb[0:3, :]
    view_grad = jnp.zeros((32, 128), F32)
    for piece in split_three(rays_sum):
        view_grad = view_grad + dot_nt(venc[...], piece)
    packed[744:760, 0:128] = view_grad[0:16, :]
    packed[744:760, 128:256] = view_grad[16:32, :]
    for q in range(4):
        for ref, which in ((keep, 0), (send, 1)):
            source = pl.multiple_of((place[which] ^ q) * PART, 8)
            ref[q * PART : (q + 1) * PART, :] = packed[pl.ds(source, PART), :]


def field_gradients(place, local, other, params):
    means, variances, spacing, dirs, target, counts, mask = local
    w_in, w_mid, w_head, w_rgb, vec = params
    rays = dirs.shape[1]
    room = rays * LANES
    vmem = pl.BlockSpec(memory_space=pltpu.VMEM)
    smem = pl.BlockSpec(memory_space=pltpu.SMEM)
    hbm = pl.BlockSpec(memory_space=pl.ANY)
    scratch = [
        pltpu.VMEM((2 * 8 * rays, LANES), F32),
        pltpu.VMEM((8, room + 2 * LANES), F32),
        pltpu.VMEM((8 * rays, LANES), F32),
        pltpu.VMEM((8 * rays, LANES), F32),
        pltpu.VMEM((8 * rays, LANES), F32),
        pltpu.VMEM((128, room), BF16),
        pltpu.VMEM((3, 272, room), BF16),
        pltpu.VMEM((3, 256, room), F32),
        pltpu.VMEM((128, room), BF16),
        pltpu.VMEM((128, room), F32),
        pltpu.VMEM((rays, room), BF16),
        pltpu.VMEM((16, LANES), F32),
        pltpu.VMEM((128, 256), F32),
        pltpu.VMEM((256, 128), BF16),
        pltpu.VMEM((2, 256, 256), BF16),
        pltpu.VMEM((2, 256, 256), BF16),
        pltpu.VMEM((144, 256), BF16),
        pltpu.VMEM((256, 144), BF16),
        pltpu.VMEM((16, 128), BF16),
        pltpu.VMEM((128, 16), BF16),
        pltpu.VMEM((2, 256, 128), F32),
        pltpu.VMEM((144, 3 * rays), BF16),
        pltpu.VMEM((32, rays), BF16),
        pltpu.VMEM((128, 256), F32),
        pltpu.VMEM((2, 272, 256), F32),
        pltpu.VMEM((144, 256), F32),
        pltpu.VMEM((16, 128), F32),
        pltpu.VMEM((128, rays), F32),
        pltpu.VMEM((8, LANES), F32),
        pltpu.VMEM((8 * PART, 256), F32),
        pltpu.SemaphoreType.DMA((28,)),
    ]
    pairs = []
    for k in (0, 1, 2, 3, 4):
        pairs += [local[k], other[k]]
    pairs += [mask.reshape(1, rays), other[6].reshape(1, rays)]
    return pl.pallas_call(
        field_kernel,
        out_shape=[jax.ShapeDtypeStruct((4 * PART, 256), F32)] * 2,
        in_specs=[smem] * 3 + [hbm] * 6 + [vmem] * 11,
        out_specs=[vmem, vmem],
        scratch_shapes=scratch,
        compiler_params=pltpu.CompilerParams(vmem_limit_bytes=62 << 20),
    )(counts, other[5], place, *pairs, w_in, w_mid, w_head, w_rgb.T, vec)


def adamw(weight, grad, first, second):
    first = BETA_ONE * first + (1.0 - BETA_ONE) * grad
    second = BETA_TWO * second + (1.0 - BETA_TWO) * grad * grad
    first_hat = first * (1.0 / (1.0 - BETA_ONE**STEP))
    second_hat = second * (1.0 / (1.0 - BETA_TWO**STEP))
    fresh = weight - LEARN_RATE * (first_hat / (jnp.sqrt(second_hat) + EPSILON) + DECAY * weight)
    return first, second, fresh


def update_kernel(place, own, near, pair, other, *refs):
    weights, firsts, seconds = refs[0:5], refs[5:10], refs[10:15]
    loss, count = refs[15], refs[16]
    outs = refs[17:32]
    packed = refs[32]
    for ref, base in ((own, 0), (near, 1), (pair, 2), (other, 4)):
        for k in range(ref.shape[0] // PART):
            position = base + k
            block = (place[0] ^ position) if position < 4 else (place[1] ^ (position - 4))
            packed[pl.ds(pl.multiple_of(block * PART, 8), PART), :] = ref[k * PART : (k + 1) * PART, :]
    line = packed[740:741, 128:256]
    loss[0] = line[0, 4]
    count[0] = line[0, 5]
    scale = 1.0 / line[0:1, 5:6]

    def apply(group, at, grad):
        step = scale.reshape(1) if grad.ndim == 1 else scale
        made = adamw(weights[group][at], grad * step, firsts[group][at], seconds[group][at])
        for k in range(3):
            outs[3 * group + k][at] = made[k]

    everything = slice(None)
    apply(0, (everything, everything), packed[0:96, :])
    for k in range(2):
        apply(1, (k, everything, everything), packed[96 + 256 * k : 352 + 256 * k, :])
    apply(2, (slice(0, 256), everything), packed[608:736, :].T)
    apply(2, (slice(256, 272), everything), packed[744:760, 0:128])
    apply(2, (slice(272, 283), everything), packed[744:755, 128:256])
    apply(3, (everything, everything), packed[741:744, 0:128])
    for k in range(9):
        line = packed[736 + k // 2 : 737 + k // 2, 128 * (k % 2) : 128 * (k % 2) + 128]
        apply(4, (pl.ds(128 * k, 128),), line.reshape(128))
    apply(4, (pl.ds(1152, 4),), packed[740:741, 128:132].reshape(4))


def update(place, pieces, params, firsts, seconds):
    vmem = pl.BlockSpec(memory_space=pltpu.VMEM)
    smem = pl.BlockSpec(memory_space=pltpu.SMEM)
    shapes = [jax.ShapeDtypeStruct((1,), F32)] * 2
    for array in params:
        shapes += [jax.ShapeDtypeStruct(array.shape, F32)] * 3
    return pl.pallas_call(
        update_kernel,
        out_shape=shapes,
        in_specs=[smem] + [vmem] * 19,
        out_specs=[smem, smem] + [vmem] * 15,
        scratch_shapes=[pltpu.VMEM((8 * PART, 256), F32)],
        compiler_params=pltpu.CompilerParams(vmem_limit_bytes=32 << 20),
    )(place, *pieces, *params, *firsts, *seconds)


def xor_pairs(total, mask_of):
    return [(i, i ^ mask_of(i)) for i in range(total)]


def reduce_small(keep, send, axes):
    core = xor_pairs(32, lambda i: 1)
    one = xor_pairs(32, lambda i: 4 if i & 1 else 2)
    two = xor_pairs(32, lambda i: 2 if i & 1 else 4)
    z_one = xor_pairs(32, lambda i: 16 if i & 1 else 8)
    z_two = xor_pairs(32, lambda i: 8 if i & 1 else 16)

    def swap(value, pairs):
        return lax.ppermute(value, axes, pairs)

    now = keep + swap(send, core)
    now = now[: 2 * PART] + swap(now[2 * PART :], one)
    own = now[:PART] + swap(now[PART:], two)
    own = own + swap(own, z_one)
    own = own + swap(own, z_two)
    near = swap(own, two)
    half = jnp.concatenate([own, near], axis=0)
    pair = swap(half, one)
    other = swap(jnp.concatenate([half, pair], axis=0), core)
    return own, near, pair, other


def on_device(
    small_mesh,
    sample_means,
    sample_vars,
    sample_spacing,
    view_dirs,
    target_rgb,
    sample_counts,
    ray_mask,
    w_in,
    w_mid,
    w_head,
    w_rgb,
    vectors,
    first_in,
    first_mid,
    first_head,
    first_rgb,
    first_vec,
    second_in,
    second_mid,
    second_head,
    second_rgb,
    second_vec,
):
    axes = ("rays", "rep")
    if small_mesh:
        index = lax.axis_index(axes)
        core, x, y = index & 1, (index >> 1) & 1, (index >> 2) & 1
        place = jnp.stack([core * 4 + jnp.where(core == 0, 2 * x + y, 2 * y + x), (1 - core) * 4 + jnp.where(core == 0, 2 * y + x, 2 * x + y)])
    else:
        place = jnp.array([0, 4], jnp.int32)
    place = place.astype(jnp.int32)
    params = (w_in, w_mid, w_head, w_rgb, vectors)
    local = (sample_means, sample_vars, sample_spacing, view_dirs, target_rgb, sample_counts, ray_mask)
    other = local
    if small_mesh:
        core_pairs = xor_pairs(32, lambda i: 1)
        other = tuple(lax.ppermute(array, axes, core_pairs) for array in local)
    keep, send = field_gradients(place, local, other, params)
    if small_mesh:
        pieces = reduce_small(keep, send, axes)
    else:
        whole = lax.psum(jnp.concatenate([keep, send], axis=0), axes)
        pieces = (whole[:PART], whole[PART : 2 * PART], whole[2 * PART : 4 * PART], whole[4 * PART :])
    outs = update(
        place,
        pieces,
        (w_in, w_mid, w_head, w_rgb.T, vectors),
        (first_in, first_mid, first_head, first_rgb.T, first_vec),
        (second_in, second_mid, second_head, second_rgb.T, second_vec),
    )
    rgb = [out.T for out in outs[11:14]]
    return (outs[0].reshape(()), outs[1].reshape(()), *outs[2:11], *rgb, *outs[14:17])


def solution(mesh):
    rays = ("rays", "rep")
    in_specs = (
        P(None, None, rays, None),
        P(None, None, rays, None),
        P(None, rays, None),
        P(None, rays),
        P(None, rays),
        P(None, rays),
        P(rays),
    ) + (P(),) * 15
    small_mesh = mesh.shape["rays"] == 8 and mesh.shape["rep"] == 4

    def step(*args):
        return on_device(small_mesh, *args)

    return jax.shard_map(step, mesh=mesh, in_specs=in_specs, out_specs=(P(),) * 17, check_vma=False)
```

time: 112 us -> 76.7 us (0.68)
  Pallas kernels: 66.3 us -> 31.2 us
  starting transfers between devices: 7.97 us -> 17.1 us
  waiting for transfers between devices: 29.4 us -> 23.5 us
  local copies, waits for them, and re-layouts: 4.95 us -> 1.71 us
    pallas_call x1, Pallas kernels: 63.6 us -> 28.6 us  [field_gradients(): pl.pallas_call(field_kernel, out_shape=[jax.ShapeDtypeStruct((4 * PART, 2...]
    ppermute x8, starting transfers between devices: 7.97 us -> 15.1 us  [swap(): return lax.ppermute(value, axes, pairs)]
    ppermute x8, waiting for transfers between devices: 29.4 us -> 22.5 us  [swap(): return lax.ppermute(value, axes, pairs)]
    unnamed x40 -> x48, local copies, waits for them, and re-layouts: 4.32 us -> 1.69 us
    ppermute x0 -> x7, starting transfers between devices: none -> 2.05 us  [on_device(): other = tuple((lax.ppermute(array, axes, core_pairs) for array in local))]
  transfers between devices with their start and end apart: 8 -> 15, of which waited for: 8 -> 10; matrix products, arithmetic and copies ran while one was open for 0% -> 1% of each run, Pallas kernels for 0% -> 0%
where the time goes in v2:
time: 76.7 us; the launch traced here: 76.2 us
  Pallas kernels  31.2 us (41%)
  waiting for transfers between devices  23.5 us (31%)
  starting transfers between devices  17.1 us (22%)
  other arithmetic  1.74 us (2%)
  local copies, waits for them, and re-layouts  1.71 us (2%)
  between operations  0.92 us (1%)
    pallas_call x1, Pallas kernels, field_gradients(): pl.pallas_call(field_kernel, out_shape=[jax.ShapeDtypeStruct((4 * PART, 2...  28.6 us
    ppermute x8, waiting for transfers between devices, swap(): return lax.ppermute(value, axes, pairs)  22.5 us
    ppermute x8, starting transfers between devices, swap(): return lax.ppermute(value, axes, pairs)  15.1 us
    pallas_call x1, Pallas kernels, update(): pl.pallas_call(update_kernel, out_shape=shapes, in_specs=[smem] + [vmem]...  2.67 us
    ppermute x7, starting transfers between devices, on_device(): other = tuple((lax.ppermute(array, axes, core_pairs) for array in local))  2.05 us
    unnamed x48, local copies, waits for them, and re-layouts  1.69 us
  transfers between devices with their start and end apart: 15, of which 10 were waited for; matrix products, arithmetic and copies ran while one was open for 1% of the time, Pallas kernels for 0%

profile of v2, /device:TPU:0, one launch (start us, length us, event | category | flops | bytes accessed | tf_op | source)
XLA Modules:
  0.0 76.2 jit_solution(8025029306610473752)
XLA Ops:
  0.7 0.5 collective-permute-start.1
  1.2 0.1 collective-permute-start.2
  1.3 0.4 collective-permute-start.6
  1.7 0.1 collective-permute-start
  1.8 0.4 collective-permute-start.4
  2.2 0.6 collective-permute-done.6
  2.8 0.1 copy-done.19
  2.9 0.2 collective-permute-start.5
  3.1 0.0 collective-permute-done.counts_two
  3.1 0.3 collective-permute-start.3
  3.4 0.0 copy-done.23
  3.4 0.3 copy-done.22
  3.7 0.6 pad_add_fusion.place
  4.3 0.0 collective-permute-done.4.dirs_two
  4.3 0.0 collective-permute-done.5.target_two
  4.3 0.0 copy-start.21
  4.3 0.3 collective-permute-done.3.spacing_two
  4.6 0.0 collective-permute-done.1.means_two
  4.6 0.0 collective-permute-done.2.variances_two
  4.6 0.0 copy-start.17
  4.6 0.2 copy-done.20
  4.8 0.0 copy-done.21
  4.9 0.4 copy-done.18
  5.2 0.1 copy-done.16
  5.3 0.1 copy-done.17
  5.3 28.6 %shard_map.341 = (f32[384,256]{1,0:T(8,128)}, f32[384,256]{1,0:T(8,128)}) custom-call(s32[2,64]{1,0:T(2,128)} %counts.1, s32[2,64]{1,0:T(2,128)} %copy-done.22, s32[2]{0:T(128)} %pad_add_fusion.place, f32[2,3,64,128]{3,2,1,0:T(8,128)} %means.1, f32[2,3,64,128]{3,2,1,0:T(8,128)} %copy-done.16, f32[2,3,64,128]{3,2,1,0:T(8,128)} %variances.1, ...), custom_call_target="tpu_custom_call" | custom-call | tf_op jit(solution)/shard_map/pallas_call | solution.py:497
  33.9 0.4 collective-permute-start.7
  34.3 1.6 %collective-permute-done.7 = f32[384,256]{1,0:T(8,128)S(1)} collective-permute-done((f32[384,256]{1,0:T(8,128)}, f32[384,256]{1,0:T(8,128)S(1)}, u32[]{:S(2)}, u32[]{:S(2)}) %collective-permute-start.7) | collective-permute-done | bytes 393248 | tf_op jit(solution)/shard_map/ppermute | solution.py:579
  35.9 1.0 %add.37 = f32[384,256]{1,0:T(8,128)S(1)} add(f32[384,256]{1,0:T(8,128)} %get-tuple-element.36, f32[384,256]{1,0:T(8,128)S(1)} %collective-permute-done.7) | non-fusion elementwise | flops 98304 | bytes 1179648 | tf_op jit(solution)/shard_map/add | solution.py:581
  37.0 2.8 %collective-permute-start.8 = (f32[192,256]{1,0:T(8,128)S(1)}, f32[192,256]{1,0:T(8,128)S(1)}, u32[]{:S(2)}, u32[]{:S(2)}) collective-permute-start(f32[192,256]{1,0:T(8,128)S(1)} %slice.17), channel_id=1, source_target_pairs={{0,2},{1,5},{2,0},{3,7},{4,6},{5,1},{6,4},{7,3},{8,10},{9,13},{10,... | collective-permute-start | bytes 589832 | tf_op jit(solution)/shard_map/ppermute | solution.py:579
  39.8 3.6 %collective-permute-done.8 = f32[192,256]{1,0:T(8,128)S(1)} collective-permute-done((f32[192,256]{1,0:T(8,128)S(1)}, f32[192,256]{1,0:T(8,128)S(1)}, u32[]{:S(2)}, u32[]{:S(2)}) %collective-permute-start.8) | collective-permute-done | bytes 196640 | tf_op jit(solution)/shard_map/ppermute | solution.py:579
  43.5 0.0 copy-start.6
  43.5 0.0 copy-start.9
  43.5 0.0 copy-start.10
  43.5 0.0 copy-start.11
  43.6 0.0 copy-start.13
  43.6 0.0 copy-start.14
  43.6 1.6 %collective-permute-start.9 = (f32[96,256]{1,0:T(8,128)S(1)}, f32[96,256]{1,0:T(8,128)S(1)}, u32[]{:S(2)}, u32[]{:S(2)}) collective-permute-start(f32[96,256]{1,0:T(8,128)S(1)} %slice.19), channel_id=1, source_target_pairs={{0,4},{1,3},{2,6},{3,1},{4,0},{5,7},{6,2},{7,5},{8,12},{9,11},{10,... | collective-permute-start | bytes 294920 | tf_op jit(solution)/shard_map/ppermute | solution.py:579
  45.2 3.1 %collective-permute-done.9 = f32[96,256]{1,0:T(8,128)S(1)} collective-permute-done((f32[96,256]{1,0:T(8,128)S(1)}, f32[96,256]{1,0:T(8,128)S(1)}, u32[]{:S(2)}, u32[]{:S(2)}) %collective-permute-start.9) | collective-permute-done | bytes 98336 | tf_op jit(solution)/shard_map/ppermute | solution.py:579
  48.3 2.2 %collective-permute-start.10 = (f32[96,256]{1,0:T(8,128)S(1)}, f32[96,256]{1,0:T(8,128)S(1)}, u32[]{:S(2)}, u32[]{:S(2)}) collective-permute-start(f32[96,256]{1,0:T(8,128)S(1)} %slice_add_fusion.1), channel_id=1, source_target_pairs={{0,8},{1,17},{2,10},{3,19},{4,12},{5,21},{6,14},{7,23},{8,0},{9,25... | collective-permute-start | bytes 294920 | tf_op jit(solution)/shard_map/ppermute | solution.py:579
  50.5 2.6 %collective-permute-done.10 = f32[96,256]{1,0:T(8,128)S(1)} collective-permute-done((f32[96,256]{1,0:T(8,128)S(1)}, f32[96,256]{1,0:T(8,128)S(1)}, u32[]{:S(2)}, u32[]{:S(2)}) %collective-permute-start.10) | collective-permute-done | bytes 98336 | tf_op jit(solution)/shard_map/ppermute | solution.py:579
  53.1 3.1 %collective-permute-start.11 = (f32[96,256]{1,0:T(8,128)S(1)}, f32[96,256]{1,0:T(8,128)S(1)}, u32[]{:S(2)}, u32[]{:S(2)}) collective-permute-start(f32[96,256]{1,0:T(8,128)S(1)} %add.40), channel_id=1, source_target_pairs={{0,16},{1,9},{2,18},{3,11},{4,20},{5,13},{6,22},{7,15},{8,24},{9,1... | collective-permute-start | bytes 294920 | tf_op jit(solution)/shard_map/ppermute | solution.py:579
  56.2 2.6 %collective-permute-done.11 = f32[96,256]{1,0:T(8,128)S(1)} collective-permute-done((f32[96,256]{1,0:T(8,128)S(1)}, f32[96,256]{1,0:T(8,128)S(1)}, u32[]{:S(2)}, u32[]{:S(2)}) %collective-permute-start.11) | collective-permute-done | bytes 98336 | tf_op jit(solution)/shard_map/ppermute | solution.py:579
  58.8 0.0 copy-start
  58.8 2.5 %collective-permute-start.12 = (f32[96,256]{1,0:T(8,128)S(1)}, f32[96,256]{1,0:T(8,128)S(1)}, u32[]{:S(2)}, u32[]{:S(2)}) collective-permute-start(f32[96,256]{1,0:T(8,128)S(1)} %add.41.own), channel_id=1, source_target_pairs={{0,4},{1,3},{2,6},{3,1},{4,0},{5,7},{6,2},{7,5},{8,12},{9,11},{10,... | collective-permute-start | bytes 294920 | tf_op jit(solution)/shard_map/ppermute | solution.py:579
  61.3 3.6 %collective-permute-done.12.near = f32[96,256]{1,0:T(8,128)S(1)} collective-permute-done((f32[96,256]{1,0:T(8,128)S(1)}, f32[96,256]{1,0:T(8,128)S(1)}, u32[]{:S(2)}, u32[]{:S(2)}) %collective-permute-start.12) | collective-permute-done | bytes 98336 | tf_op jit(solution)/shard_map/ppermute | solution.py:579
  64.9 0.0 copy-start.1
  64.9 2.5 %collective-permute-start.13 = (f32[192,256]{1,0:T(8,128)S(1)}, f32[192,256]{1,0:T(8,128)S(1)}, u32[]{:S(2)}, u32[]{:S(2)}) collective-permute-start(f32[192,256]{1,0:T(8,128)S(1)} %pad_maximum_fusion.1), channel_id=1, source_target_pairs={{0,2},{1,5},{2,0},{3,7},{4,6},{5,1},{6,4},{7,3},{8,10},{9,13},{10,... | collective-permute-start | bytes 589832 | tf_op jit(solution)/shard_map/ppermute | solution.py:579
  67.4 3.6 %collective-permute-done.13.pair = f32[192,256]{1,0:T(8,128)S(1)} collective-permute-done((f32[192,256]{1,0:T(8,128)S(1)}, f32[192,256]{1,0:T(8,128)S(1)}, u32[]{:S(2)}, u32[]{:S(2)}) %collective-permute-start.13) | collective-permute-done | bytes 196640 | tf_op jit(solution)/shard_map/ppermute | solution.py:579
  71.1 0.0 copy-start.12
  71.1 0.1 collective-permute-start.14
  71.2 1.7 %collective-permute-done.14.other = f32[384,256]{1,0:T(8,128)S(1)} collective-permute-done((f32[384,256]{1,0:T(8,128)S(1)}, f32[384,256]{1,0:T(8,128)S(1)}, u32[]{:S(2)}, u32[]{:S(2)}) %collective-permute-start.14) | collective-permute-done | bytes 393248 | tf_op jit(solution)/shard_map/ppermute | solution.py:579
  72.9 0.0 copy-done.8
  72.9 0.0 copy-done.6
  72.9 0.0 copy-done.9
  72.9 0.0 copy-done.10
  72.9 0.0 copy-done.11
  72.9 0.0 copy-done.13
  72.9 0.0 copy-done.14
  72.9 0.0 copy-done.4
  72.9 0.0 copy-done.5
  72.9 0.0 copy-done.7
  73.0 0.5 copy-done.15
  73.5 2.7 %shard_map.342 = (f32[1]{0:T(128)}, f32[1]{0:T(128)}, f32[96,256]{1,0:T(8,128)}, f32[96,256]{1,0:T(8,128)}, f32[96,256]{1,0:T(8,128)}, /*index=5*/f32[2,256,256]...) custom-call(s32[2]{0:T(128)S(1)} %copy-done.15, ...), custom_call_target="tpu_custom_call" | custom-call | tf_op jit(solution)/shard_map/pallas_call | solution.py:557
  (26 shorter events, 0.2 us)
Async XLA Ops:
  0.7 3.9 %collective-permute-start.1 = (f32[2,3,64,128]{3,2,1,0:T(8,128)}, f32[2,3,64,128]{3,2,1,0:T(8,128)S(1)}, u32[]{:S(2)}, u32[]{:S(2)}) collective-permute-start(f32[2,3,64,128]{3,2,1,0:T(8,128)} %means.1), channel_id=1, source_target_pairs={{0,1},{1,0},{2,3},{3,2},{4,5},{5,4},{6,7},{7,6},{8,9},{9,8},{10,11... | collective-permute-start | bytes 589832 | tf_op jit(solution)/shard_map/ppermute | solution.py:631
  1.2 3.4 %collective-permute-start.2 = (f32[2,3,64,128]{3,2,1,0:T(8,128)}, f32[2,3,64,128]{3,2,1,0:T(8,128)S(1)}, u32[]{:S(2)}, u32[]{:S(2)}) collective-permute-start(f32[2,3,64,128]{3,2,1,0:T(8,128)} %variances.1), channel_id=1, source_target_pairs={{0,1},{1,0},{2,3},{3,2},{4,5},{5,4},{6,7},{7,6},{8,9},{9,8},{10,11... | collective-permute-start | bytes 589832 | tf_op jit(solution)/shard_map/ppermute | solution.py:631
  1.3 1.6 %collective-permute-start.6 = (s32[64]{0:T(128)}, s32[64]{0:T(128)S(1)}, u32[]{:S(2)}, u32[]{:S(2)}) collective-permute-start(s32[64]{0:T(128)} %param.28), channel_id=1, source_target_pairs={{0,1},{1,0},{2,3},{3,2},{4,5},{5,4},{6,7},{7,6},{8,9},{9,8},{10,11... | collective-permute-start | bytes 776 | tf_op jit(solution)/shard_map/ppermute | solution.py:631
  1.7 1.4 %collective-permute-start = (s32[2,64]{1,0:T(2,128)}, s32[2,64]{1,0:T(2,128)S(1)}, u32[]{:S(2)}, u32[]{:S(2)}) collective-permute-start(s32[2,64]{1,0:T(2,128)} %counts.1), channel_id=1, source_target_pairs={{0,1},{1,0},{2,3},{3,2},{4,5},{5,4},{6,7},{7,6},{8,9},{9,8},{10,11... | collective-permute-start | bytes 1544 | tf_op jit(solution)/shard_map/ppermute | solution.py:631
  1.8 2.5 %collective-permute-start.4 = (f32[3,64]{1,0:T(4,128)}, f32[3,64]{1,0:T(4,128)S(1)}, u32[]{:S(2)}, u32[]{:S(2)}) collective-permute-start(f32[3,64]{1,0:T(4,128)} %dirs.1), channel_id=1, source_target_pairs={{0,1},{1,0},{2,3},{3,2},{4,5},{5,4},{6,7},{7,6},{8,9},{9,8},{10,11... | collective-permute-start | bytes 2312 | tf_op jit(solution)/shard_map/ppermute | solution.py:631
  2.2 0.7 copy-start.19
  2.9 0.5 copy-start.23
  2.9 1.4 %collective-permute-start.5 = (f32[3,64]{1,0:T(4,128)S(1)}, f32[3,64]{1,0:T(4,128)S(1)}, u32[]{:S(2)}, u32[]{:S(2)}) collective-permute-start(f32[3,64]{1,0:T(4,128)S(1)} %copy-done.19), channel_id=1, source_target_pairs={{0,1},{1,0},{2,3},{3,2},{4,5},{5,4},{6,7},{7,6},{8,9},{9,8},{10,11... | collective-permute-start | bytes 2312 | tf_op jit(solution)/shard_map/ppermute | solution.py:631
  3.1 0.6 copy-start.22
  3.1 1.5 %collective-permute-start.3 = (f32[2,64,128]{2,1,0:T(8,128)}, f32[2,64,128]{2,1,0:T(8,128)S(1)}, u32[]{:S(2)}, u32[]{:S(2)}) collective-permute-start(f32[2,64,128]{2,1,0:T(8,128)} %spacing.1), channel_id=1, source_target_pairs={{0,1},{1,0},{2,3},{3,2},{4,5},{5,4},{6,7},{7,6},{8,9},{9,8},{10,11... | collective-permute-start | bytes 196616 | tf_op jit(solution)/shard_map/ppermute | solution.py:631
  4.3 0.6 copy-start.20
  4.3 0.6 copy-start.21
  4.6 0.6 copy-start.18
  4.6 0.7 copy-start.16
  4.6 0.7 copy-start.17
  33.9 2.0 %collective-permute-start.7 = (f32[384,256]{1,0:T(8,128)}, f32[384,256]{1,0:T(8,128)S(1)}, u32[]{:S(2)}, u32[]{:S(2)}) collective-permute-start(f32[384,256]{1,0:T(8,128)} %get-tuple-element.37), channel_id=1, source_target_pairs={{0,1},{1,0},{2,3},{3,2},{4,5},{5,4},{6,7},{7,6},{8,9},{9,8},{10,11... | collective-permute-start | bytes 1179656 | tf_op jit(solution)/shard_map/ppermute | solution.py:579
  37.0 6.5 %collective-permute-start.8 = (f32[192,256]{1,0:T(8,128)S(1)}, f32[192,256]{1,0:T(8,128)S(1)}, u32[]{:S(2)}, u32[]{:S(2)}) collective-permute-start(f32[192,256]{1,0:T(8,128)S(1)} %slice.17), channel_id=1, source_target_pairs={{0,2},{1,5},{2,0},{3,7},{4,6},{5,1},{6,4},{7,3},{8,10},{9,13},{10,... | collective-permute-start | bytes 589832 | tf_op jit(solution)/shard_map/ppermute | solution.py:579
  43.5 29.4 %copy-start.8 = (f32[96,256]{1,0:T(8,128)S(1)}, f32[96,256]{1,0:T(8,128)}, u32[]{:S(2)}) copy-start(f32[96,256]{1,0:T(8,128)} %refs_10_.1) | copy-start | bytes 294916
  43.5 29.4 %copy-start.6 = (f32[283,128]{1,0:T(8,128)S(1)}, f32[283,128]{1,0:T(8,128)}, u32[]{:S(2)}) copy-start(f32[283,128]{1,0:T(8,128)} %refs_12_.1) | copy-start | bytes 434692
  43.5 29.4 %copy-start.9 = (f32[1156]{0:T(1024)S(1)}, f32[1156]{0:T(1024)}, u32[]{:S(2)}) copy-start(f32[1156]{0:T(1024)} %refs_4_.1) | copy-start | bytes 13876
  43.5 29.4 %copy-start.10 = (f32[1156]{0:T(1024)S(1)}, f32[1156]{0:T(1024)}, u32[]{:S(2)}) copy-start(f32[1156]{0:T(1024)} %refs_9_.1) | copy-start | bytes 13876
  43.5 29.4 %copy-start.11 = (f32[1156]{0:T(1024)S(1)}, f32[1156]{0:T(1024)}, u32[]{:S(2)}) copy-start(f32[1156]{0:T(1024)} %refs_14_.1) | copy-start | bytes 13876
  43.6 29.4 %copy-start.13 = (f32[128,3]{0,1:T(4,128)S(1)}, f32[128,3]{0,1:T(4,128)}, u32[]{:S(2)}) copy-start(f32[128,3]{0,1:T(4,128)} %param.37) | copy-start | bytes 4612
  43.6 29.4 %copy-start.14 = (f32[128,3]{0,1:T(4,128)S(1)}, f32[128,3]{0,1:T(4,128)}, u32[]{:S(2)}) copy-start(f32[128,3]{0,1:T(4,128)} %param.42) | copy-start | bytes 4612
  43.6 4.7 %collective-permute-start.9 = (f32[96,256]{1,0:T(8,128)S(1)}, f32[96,256]{1,0:T(8,128)S(1)}, u32[]{:S(2)}, u32[]{:S(2)}) collective-permute-start(f32[96,256]{1,0:T(8,128)S(1)} %slice.19), channel_id=1, source_target_pairs={{0,4},{1,3},{2,6},{3,1},{4,0},{5,7},{6,2},{7,5},{8,12},{9,11},{10,... | collective-permute-start | bytes 294920 | tf_op jit(solution)/shard_map/ppermute | solution.py:579
  48.3 24.6 %copy-start.4 = (f32[96,256]{1,0:T(8,128)S(1)}, f32[96,256]{1,0:T(8,128)}, u32[]{:S(2)}) copy-start(f32[96,256]{1,0:T(8,128)} %refs_0_.1) | copy-start | bytes 294916
  48.3 24.7 %copy-start.5 = (f32[283,128]{1,0:T(8,128)S(1)}, f32[283,128]{1,0:T(8,128)}, u32[]{:S(2)}) copy-start(f32[283,128]{1,0:T(8,128)} %refs_7_.1) | copy-start | bytes 434692
  48.3 24.7 %copy-start.7 = (f32[96,256]{1,0:T(8,128)S(1)}, f32[96,256]{1,0:T(8,128)}, u32[]{:S(2)}) copy-start(f32[96,256]{1,0:T(8,128)} %refs_5_.1) | copy-start | bytes 294916
  48.3 4.8 %collective-permute-start.10 = (f32[96,256]{1,0:T(8,128)S(1)}, f32[96,256]{1,0:T(8,128)S(1)}, u32[]{:S(2)}, u32[]{:S(2)}) collective-permute-start(f32[96,256]{1,0:T(8,128)S(1)} %slice_add_fusion.1), channel_id=1, source_target_pairs={{0,8},{1,17},{2,10},{3,19},{4,12},{5,21},{6,14},{7,23},{8,0},{9,25... | collective-permute-start | bytes 294920 | tf_op jit(solution)/shard_map/ppermute | solution.py:579
  53.1 19.9 %copy-start.3 = (f32[2,256,256]{2,1,0:T(8,128)S(1)}, f32[2,256,256]{2,1,0:T(8,128)}, u32[]{:S(2)}) copy-start(f32[2,256,256]{2,1,0:T(8,128)} %refs_11_.1) | copy-start | bytes 1572868
  53.1 5.7 %collective-permute-start.11 = (f32[96,256]{1,0:T(8,128)S(1)}, f32[96,256]{1,0:T(8,128)S(1)}, u32[]{:S(2)}, u32[]{:S(2)}) collective-permute-start(f32[96,256]{1,0:T(8,128)S(1)} %add.40), channel_id=1, source_target_pairs={{0,16},{1,9},{2,18},{3,11},{4,20},{5,13},{6,22},{7,15},{8,24},{9,1... | collective-permute-start | bytes 294920 | tf_op jit(solution)/shard_map/ppermute | solution.py:579
  58.8 14.2 %copy-start.2 = (f32[2,256,256]{2,1,0:T(8,128)S(1)}, f32[2,256,256]{2,1,0:T(8,128)}, u32[]{:S(2)}) copy-start(f32[2,256,256]{2,1,0:T(8,128)} %refs_6_.1) | copy-start | bytes 1572868
  58.8 14.2 %copy-start = (f32[2,256,256]{2,1,0:T(8,128)S(1)}, f32[2,256,256]{2,1,0:T(8,128)}, u32[]{:S(2)}) copy-start(f32[2,256,256]{2,1,0:T(8,128)} %refs_1_.1) | copy-start | bytes 1572868
  58.8 6.1 %collective-permute-start.12 = (f32[96,256]{1,0:T(8,128)S(1)}, f32[96,256]{1,0:T(8,128)S(1)}, u32[]{:S(2)}, u32[]{:S(2)}) collective-permute-start(f32[96,256]{1,0:T(8,128)S(1)} %add.41.own), channel_id=1, source_target_pairs={{0,4},{1,3},{2,6},{3,1},{4,0},{5,7},{6,2},{7,5},{8,12},{9,11},{10,... | collective-permute-start | bytes 294920 | tf_op jit(solution)/shard_map/ppermute | solution.py:579
  64.9 8.1 %copy-start.1 = (f32[283,128]{1,0:T(8,128)S(1)}, f32[283,128]{1,0:T(8,128)}, u32[]{:S(2)}) copy-start(f32[283,128]{1,0:T(8,128)} %refs_2_.1) | copy-start | bytes 434692
  64.9 6.1 %collective-permute-start.13 = (f32[192,256]{1,0:T(8,128)S(1)}, f32[192,256]{1,0:T(8,128)S(1)}, u32[]{:S(2)}, u32[]{:S(2)}) collective-permute-start(f32[192,256]{1,0:T(8,128)S(1)} %pad_maximum_fusion.1), channel_id=1, source_target_pairs={{0,2},{1,5},{2,0},{3,7},{4,6},{5,1},{6,4},{7,3},{8,10},{9,13},{10,... | collective-permute-start | bytes 589832 | tf_op jit(solution)/shard_map/ppermute | solution.py:579
  71.1 1.9 %copy-start.12 = (f32[128,3]{0,1:T(4,128)S(1)}, f32[128,3]{0,1:T(4,128)}, u32[]{:S(2)}) copy-start(f32[128,3]{0,1:T(4,128)} %param.32) | copy-start | bytes 4612
  71.1 1.8 %collective-permute-start.14 = (f32[384,256]{1,0:T(8,128)S(1)}, f32[384,256]{1,0:T(8,128)S(1)}, u32[]{:S(2)}, u32[]{:S(2)}) collective-permute-start(f32[384,256]{1,0:T(8,128)S(1)} %pad_maximum_fusion), channel_id=1, source_target_pairs={{0,1},{1,0},{2,3},{3,2},{4,5},{5,4},{6,7},{7,6},{8,9},{9,8},{10,11... | collective-permute-start | bytes 1179656 | tf_op jit(solution)/shard_map/ppermute | solution.py:579
  72.9 0.7 copy-start.15

commit v3 on v2

--- a/solution.py
+++ b/solution.py
@@ -1,3 +1,4 @@
+import functools
 import math
 
 import jax
@@ -17,8 +18,8 @@
 DECAY = 0.01
 COARSE_SHARE = 0.1
 
-BLOCK = 1024
-REST = 512
+BLOCK = 512
+BACK = 1024
 LANES = 128
 PART = 96
 
@@ -62,21 +63,17 @@
 
 
 def field_kernel(
+    find_place,
     counts,
     counts_two,
-    place,
+    other,
     means,
-    means_two,
     variances,
-    variances_two,
     spacing,
-    spacing_two,
     dirs,
-    dirs_two,
     target,
-    target_two,
     mask,
-    mask_two,
+    counts_vec,
     w_in,
     w_mid,
     w_head,
@@ -90,11 +87,17 @@
     z_planes,
     g_planes,
     enc,
-    hidden,
-    pre,
+    hidden_a,
+    hidden_b,
+    hidden_c,
+    pre_a,
+    pre_b,
+    pre_c,
     feat,
     feat_pre,
     one_hot,
+    dz_c,
+    small_two,
     rows,
     wide,
     w0t,
@@ -116,18 +119,23 @@
     packed,
     sem,
 ):
+    place = find_place()
     rays = dirs.shape[1]
     own = rays // 2
-    tiles = z_planes.shape[0] // 8
+    tiles = rays
+    pitch = z_planes.shape[0] // 8
     copies = []
     for p in range(2):
-        for k, pair in enumerate((means, means_two, variances, variances_two)):
-            first, base = (0, 0) if k % 2 == 0 else (own, own)
+        for k, source in enumerate((means, variances)):
             for c in range(3):
-                to = (p * 8 + 4 * (k // 2) + c) * rays + base
-                copies.append((pair.at[p, c, pl.ds(first, own)], pk.at[pl.ds(to, own)]))
-        for k, pair in enumerate((spacing, spacing_two)):
-            copies.append((pair.at[p, pl.ds(k * own, own)], pk.at[pl.ds((p * 8 + 7) * rays + k * own, own)]))
+                to = (p * 8 + 4 * k + c) * pitch
+                copies.append((source.at[p, c, pl.ds(0, own)], pk.at[pl.ds(to, own)]))
+                row = (6 * k + 3 * p + c) * own
+                copies.append((other.at[pl.ds(row, own)], pk.at[pl.ds(to + own, own)]))
+        to = (p * 8 + 7) * pitch
+        copies.append((spacing.at[p, pl.ds(0, own)], pk.at[pl.ds(to, own)]))
+        copies.append((other.at[pl.ds((12 + p) * own, own)], pk.at[pl.ds(to + own, own)]))
+    copies.append((other.at[pl.ds(14 * own, 16)], small_two))
     copies = [pltpu.make_async_copy(a, b, sem.at[k]) for k, (a, b) in enumerate(copies)]
     for copy in copies:
         copy.start()
@@ -167,12 +175,15 @@
     wrt[...] = wide[0:16, 0:128].astype(BF16)
     wr[...] = (wide[0:16, 0:128].T * half).astype(BF16)
 
-    def both_halves(at, one, two):
-        wide[at : at + one.shape[0], 0:own] = one[:, 0:own].astype(F32)
-        wide[at : at + one.shape[0], own:rays] = two[:, own:rays].astype(F32)
+    copies[-1].wait()
+
+    def both_halves(at, one, row):
+        n = one.shape[0]
+        wide[at : at + n, 0:own] = one[:, 0:own].astype(F32)
+        wide[at : at + n, own:rays] = small_two[row : row + n, own:rays]
 
     wide[0:32, 0:128] = jnp.zeros((32, 128), F32)
-    both_halves(0, dirs, dirs_two)
+    both_halves(0, dirs, 0)
     d = wide[0:3, 0:rays]
     for l in range(L_DIR):
         wide[3 + 3 * l : 6 + 3 * l, 0:rays] = jnp.sin(d * (2.0**l))
@@ -186,20 +197,14 @@
     view = (view + vec_t[:, 8:9]) * half
     wide[0:16, 0:128] = jnp.zeros((16, 128), F32)
     wide[0:4, 0:rays] = jnp.broadcast_to(vec_t[0:4, 9:10], (4, rays))
-    both_halves(4, target, target_two)
-    both_halves(7, mask, mask_two)
+    both_halves(4, target, 3)
+    both_halves(7, mask, 6)
     count_here = jnp.sum(wide[7:8, 0:128])
     view_t[...] = jnp.concatenate(split_three(jnp.concatenate([view, wide[0:16, 0:rays]], axis=0)), axis=1)
 
-    one_row = (lax.broadcasted_iota(jnp.int32, (16, LANES), 0) == 0).astype(BF16)
-
-    def fill(t, carry):
-        s = pl.multiple_of(t * LANES, LANES)
-        for k in range(2):
-            hidden[k, 256:272, pl.ds(s, LANES)] = one_row
-        return carry
-
-    lax.fori_loop(0, tiles, fill, 0)
+    one_row = (lax.broadcasted_iota(jnp.int32, (16, hidden_a.shape[1]), 0) == 0).astype(BF16)
+    hidden_a[256:272, :] = one_row
+    hidden_b[256:272, :] = one_row
     for ref in (g_planes, g_in, g_mid, g_head, g_rgb, s_ray, g_sum):
         ref[...] = jnp.zeros_like(ref)
 
@@ -209,29 +214,23 @@
     anchor = (jnp.int32(1) << (4 * (sub16 // 4))).astype(F32)
     decay_rate = anchor * anchor * (-0.5)
 
-    for copy in copies:
+    for copy in copies[:-1]:
         copy.wait()
 
-    def count_of(p, r):
-        return jnp.where(r < own, counts[p, r], counts_two[p, r])
-
-    def forward_block(start, size):
-        at = pl.ds(pl.multiple_of(start, LANES), size)
-        per = size // LANES
-
-        def wide_of(tile):
-            return jnp.concatenate([tile] * per, axis=1)
-
-        def activate(y, pre_ref, h_ref):
-            pre_ref[...] = y
-            h = (y * (1.0 + jnp.tanh(y))).astype(BF16)
-            h_ref[...] = h
-            return h
-
+    size = BLOCK
+    per = size // LANES
+
+    def wide_of(tile):
+        return jnp.concatenate([tile] * per, axis=1)
+
+    def place_of(i):
+        return pl.ds(pl.multiple_of(i * size, LANES), size)
+
+    def encode(i):
+        at = place_of(i)
         x = xs[:, at]
-        tile_at = start // LANES
         for k in range(per):
-            x_planes[pl.ds(tile_at + k, 8, stride=tiles), :] = x[:, k * LANES : (k + 1) * LANES]
+            x_planes[pl.ds(i * per + k, 8, stride=pitch), :] = x[:, k * LANES : (k + 1) * LANES]
         sub = lax.broadcasted_iota(jnp.int32, (8, size), 0)
         turned = pltpu.roll(x, 4, 0)
         low = sub < 4
@@ -257,79 +256,85 @@
         item = x[3:4, :]
         ray = jnp.where(item >= rays, item - rays, item)
         hit = jnp.broadcast_to(ray, (rays, size)) == lax.broadcasted_iota(jnp.int32, (rays, size), 0).astype(F32)
-        hot = jnp.where(hit, 1.0, 0.0).astype(BF16)
-        one_hot[:, at] = hot
-        h = activate(dot_nn(w0t[...], enc[:, at]), pre.at[0, :, at], hidden.at[0, 0:256, at])
-        for k in range(2):
-            y = dot_nn(wmt[k], h) + wide_of(bias_b[k])
-            h = activate(y, pre.at[k + 1, :, at], hidden.at[k + 1, 0:256, at])
-        y = dot_nn(wht[...], h) + dot_nn(view_t[...], jnp.concatenate([hot, hot, hot], axis=0))
-        f = activate(y[0:128, :], feat_pre.at[:, at], feat.at[:, at])
-        z = dot_nn(wrt[...], f)[0:8, :] + y[128:136, :]
-        for k in range(per):
-            z_planes[pl.ds(tile_at + k, 8, stride=tiles), :] = z[:, k * LANES : (k + 1) * LANES]
-
-    def backward_block(start, size):
-        at = pl.ds(pl.multiple_of(start, LANES), size)
+        one_hot[:, at] = jnp.where(hit, 1.0, 0.0).astype(BF16)
+
+    def activate(y, pre_ref, h_ref):
+        pre_ref[...] = y
+        h = (y * (1.0 + jnp.tanh(y))).astype(BF16)
+        h_ref[...] = h
+        return h
+
+    def slope(y):
+        a = jnp.tanh(y)
+        return (1.0 + a) * (1.0 + y * (1.0 - a))
+
+    def forward_all(blocks):
+        def step(i, carry):
+            first, second, third = (place_of(jnp.clip(i - k, 0, blocks - 1)) for k in range(3))
+            hot = one_hot[:, third]
+            y_head = dot_nn(wht[...], hidden_c[:, third]) + dot_nn(view_t[...], jnp.concatenate([hot, hot, hot], axis=0))
+            y_two = dot_nn(wmt[0], hidden_a[0:256, second]) + wide_of(bias_b[0])
+            encode(jnp.minimum(i, blocks - 1))
+            f = activate(y_head[0:128, :], feat_pre.at[:, third], feat.at[:, third])
+            h = activate(y_two, pre_b.at[:, second], hidden_b.at[0:256, second])
+            y_one = dot_nn(w0t[...], enc[:, first])
+            y_color = dot_nn(wrt[...], f)[0:8, :] + y_head[128:136, :]
+            y_three = dot_nn(wmt[1], h) + wide_of(bias_b[1])
+            activate(y_one, pre_a.at[:, first], hidden_a.at[0:256, first])
+            tile_at = jnp.clip(i - 2, 0, blocks - 1) * per
+            for k in range(per):
+                z_planes[pl.ds(tile_at + k, 8, stride=pitch), :] = y_color[:, k * LANES : (k + 1) * LANES]
+            activate(y_three, pre_c.at[:, second], hidden_c.at[:, second])
+            return carry
+
+        lax.fori_loop(0, blocks + 2, step, 0)
+
+    def backward_all(blocks):
+        size = BACK
         per = size // LANES
-        tile_at = start // LANES
-
-        def slope(y):
-            a = jnp.tanh(y)
-            return (1.0 + a) * (1.0 + y * (1.0 - a))
-
-        dz = jnp.concatenate([g_planes[pl.ds(tile_at + k, 8, stride=tiles), :] for k in range(per)], axis=1)
-        dzw = dz.astype(BF16).astype(F32)
-        part = dzw[:, 0:LANES]
-        for k in range(1, per):
-            part = part + dzw[:, k * LANES : (k + 1) * LANES]
-        g_sum[...] += part
-        dz = jnp.concatenate([dzw, jnp.zeros_like(dzw)], axis=0).astype(BF16)
-        dzf = (dot_nn(wr[...], dz) * slope(feat_pre[:, at])).astype(BF16)
-        both = jnp.concatenate([dzf, dz], axis=0)
-        g_head[...] += dot_nt(both, hidden[2, 0:256, at])
-        s_ray[...] += dot_nt(dzf, one_hot[:, at])
-        g_rgb[...] += dot_nt(dz, feat[:, at])
-        up = dot_nn(whd[...], both)
-        for k in (1, 0):
-            dzk = (up * slope(pre[k + 1, :, at])).astype(BF16)
-            g_mid[k] += dot_nt(hidden[k, :, at], dzk)
-            up = dot_nn(wm[k], dzk)
-        dz0 = (up * slope(pre[0, :, at])).astype(BF16)
-        g_in[...] += dot_nt(enc[:, at], dz0)
-
-    def over_blocks(block, total):
-        large = (total + (BLOCK - REST - 1)) // BLOCK
-        small = jnp.where(total > large * BLOCK, 1, 0)
-
-        def at_large(i, carry):
-            block(i * BLOCK, BLOCK)
+
+        def step(i, carry):
+            at = pl.ds(pl.multiple_of(i * size, LANES), size)
+            dz = jnp.concatenate([g_planes[pl.ds(i * per + k, 8, stride=pitch), :] for k in range(per)], axis=1)
+            dzw = dz.astype(BF16).astype(F32)
+            part = dzw[:, 0:LANES]
+            for k in range(1, per):
+                part = part + dzw[:, k * LANES : (k + 1) * LANES]
+            g_sum[...] += part
+            dz = jnp.concatenate([dzw, jnp.zeros_like(dzw)], axis=0).astype(BF16)
+            dz_f = (dot_nn(wr[...], dz) * slope(feat_pre[:, at])).astype(BF16)
+            both = jnp.concatenate([dz_f, dz], axis=0)
+            up = dot_nn(whd[...], both)
+            g_head[...] += dot_nt(both, hidden_c[:, at])
+            s_ray[...] += dot_nt(dz_f, one_hot[:, at])
+            g_rgb[...] += dot_nt(dz, feat[:, at])
+            dz = (up * slope(pre_c[:, at])).astype(BF16)
+            up = dot_nn(wm[1], dz)
+            g_mid[1] += dot_nt(hidden_b[:, at], dz)
+            dz = (up * slope(pre_b[:, at])).astype(BF16)
+            up = dot_nn(wm[0], dz)
+            g_mid[0] += dot_nt(hidden_a[:, at], dz)
+            dz = (up * slope(pre_a[:, at])).astype(BF16)
+            g_in[...] += dot_nt(enc[:, at], dz)
             return carry
 
-        def at_small(i, carry):
-            block(large * BLOCK, REST)
-            return carry
-
-        lax.fori_loop(0, large, at_large, 0)
-        lax.fori_loop(0, small, at_small, 0)
+        lax.fori_loop(0, (blocks + BACK // BLOCK - 1) // (BACK // BLOCK), step, 0)
 
     group = 8
 
-    def chunk(first, items, loss):
+    def chunk(first, passes, loss):
         xs[...] = jnp.where(lax.broadcasted_iota(jnp.int32, xs.shape, 0) == 3, -1.0, 0.0)
         x_planes[...] = jnp.full_like(x_planes, -1.0)
 
-        def pack(g, offset):
-            base = first + g * group
-            p = base // rays
-            r0 = base - p * rays
+        def pack(p, part, g, offset):
+            r0 = part * own + g * group
             moved = []
             for j in range(group):
-                count = count_of(p, r0 + j)
-                here = pk[pl.ds(p * 8 * rays + r0 + j, 8, stride=rays), :]
-                item = jnp.where(lane8 < count, (base + j).astype(F32), -1.0)
+                count = (counts, counts_two)[part][p, r0 + j]
+                here = pk[pl.ds(p * 8 * pitch + r0 + j, 8, stride=pitch), :]
+                item = jnp.where(lane8 < count, (p * rays + r0 + j).astype(F32), -1.0)
                 here = jnp.where(sub8 == 3, item, here)
-                o = offset % LANES
+                o = offset & (LANES - 1)
                 moved.append((pltpu.roll(here, o, 1), o, pl.multiple_of(offset - o, LANES)))
                 offset = offset + count
             for turned, o, t in moved:
@@ -338,11 +343,17 @@
                 pltpu.store(xs.at[:, pl.ds(t + LANES, LANES)], turned, mask=jnp.logical_not(keep_low))
             return offset
 
-        total = lax.fori_loop(0, items // group, pack, jnp.int32(0))
-        over_blocks(forward_block, total)
+        def pack_pass(p, offset):
+            for part in range(2):
+                offset = lax.fori_loop(0, own // group, lambda g, o: pack(p, part, g, o), offset)
+            return offset
+
+        total = lax.fori_loop(first, first + passes, pack_pass, jnp.int32(0))
+        blocks = (total + BACK - 1) // BACK * (BACK // BLOCK)
+        forward_all(blocks)
 
         def plane(ref, k):
-            return ref[k * tiles : (k + 1) * tiles, :]
+            return ref[k * pitch : k * pitch + tiles, :]
 
         lane = lax.broadcasted_iota(jnp.int32, (tiles, LANES), 1)
         row = lax.broadcasted_iota(jnp.int32, (tiles, LANES), 0)
@@ -392,26 +403,25 @@
             color_grad = (2.0 / 3.0) * share * error
             weighted = weighted + color_grad * rgb
             d_color = weights * color_grad * 1.002 * sig * (1.0 - sig)
-            g_planes[c * tiles : (c + 1) * tiles, :] = jnp.where(valid, d_color, 0.0)
+            g_planes[c * pitch : c * pitch + tiles, :] = jnp.where(valid, d_color, 0.0)
         product = jnp.where(valid, weighted * weights, 0.0)
         after = scan_back(product) - product
         d_density = (beyond * weighted - after) * space * jax.nn.sigmoid(zd)
-        g_planes[3 * tiles : 4 * tiles, :] = jnp.where(valid, d_density, 0.0)
+        g_planes[3 * pitch : 3 * pitch + tiles, :] = jnp.where(valid, d_density, 0.0)
         previous = jnp.where(lane >= 1, pltpu.roll(item, 1, 1), jnp.where(row > 0, end_before, -2.0))
         begins = jnp.logical_and(previous != item, valid)
         loss = loss + jnp.sum(jnp.where(begins, sums * share, 0.0)) * (1.0 / 3.0)
 
-        over_blocks(backward_block, total)
+        backward_all(blocks)
         return loss
 
-    def add_counts(r, total):
-        return total + count_of(0, r) + count_of(1, r)
-
-    everything = lax.fori_loop(0, rays, add_counts, jnp.int32(0), unroll=8)
-    at_once = everything <= tiles * LANES
+    wide[0:2, 0:own] = counts_vec[:, 0:own].astype(F32)
+    wide[0:2, own:rays] = small_two[7:9, own:rays]
+    everything = jnp.sum(wide[0:2, 0:rays])
+    at_once = everything <= 1.0 * tiles * LANES
     chunks = jnp.where(at_once, 1, 2)
-    items = jnp.where(at_once, 2 * rays, rays)
-    loss = lax.fori_loop(0, chunks, lambda i, loss: chunk(i * rays, items, loss), jnp.zeros((), F32))
+    passes = jnp.where(at_once, 2, 1)
+    loss = lax.fori_loop(0, chunks, lambda i, loss: chunk(i, passes, loss), jnp.zeros((), F32))
 
     for a in range(4):
         for d in range(4):
@@ -444,31 +454,38 @@
     packed[744:760, 0:128] = view_grad[0:16, :]
     packed[744:760, 128:256] = view_grad[16:32, :]
     for q in range(4):
-        for ref, which in ((keep, 0), (send, 1)):
-            source = pl.multiple_of((place[which] ^ q) * PART, 8)
+        for ref, which in ((keep, place[0]), (send, place[1])):
+            source = pl.multiple_of((which ^ q) * PART, 8)
             ref[q * PART : (q + 1) * PART, :] = packed[pl.ds(source, PART), :]
 
 
-def field_gradients(place, local, other, params):
+def field_gradients(find_place, local, other, other_counts, params):
     means, variances, spacing, dirs, target, counts, mask = local
     w_in, w_mid, w_head, w_rgb, vec = params
     rays = dirs.shape[1]
-    room = rays * LANES
+    room = rays * LANES + LANES
+    pitch = rays + 8
     vmem = pl.BlockSpec(memory_space=pltpu.VMEM)
     smem = pl.BlockSpec(memory_space=pltpu.SMEM)
     hbm = pl.BlockSpec(memory_space=pl.ANY)
     scratch = [
-        pltpu.VMEM((2 * 8 * rays, LANES), F32),
-        pltpu.VMEM((8, room + 2 * LANES), F32),
-        pltpu.VMEM((8 * rays, LANES), F32),
-        pltpu.VMEM((8 * rays, LANES), F32),
-        pltpu.VMEM((8 * rays, LANES), F32),
+        pltpu.VMEM((2 * 8 * pitch, LANES), F32),
+        pltpu.VMEM((8, room + LANES), F32),
+        pltpu.VMEM((8 * pitch, LANES), F32),
+        pltpu.VMEM((8 * pitch, LANES), F32),
+        pltpu.VMEM((8 * pitch, LANES), F32),
         pltpu.VMEM((128, room), BF16),
-        pltpu.VMEM((3, 272, room), BF16),
-        pltpu.VMEM((3, 256, room), F32),
+        pltpu.VMEM((272, room), BF16),
+        pltpu.VMEM((272, room), BF16),
+        pltpu.VMEM((256, room), BF16),
+        pltpu.VMEM((256, room), F32),
+        pltpu.VMEM((256, room), F32),
+        pltpu.VMEM((256, room), F32),
         pltpu.VMEM((128, room), BF16),
         pltpu.VMEM((128, room), F32),
         pltpu.VMEM((rays, room), BF16),
+        pltpu.VMEM((256, BLOCK + LANES), BF16),
+        pltpu.VMEM((16, LANES), F32),
         pltpu.VMEM((16, LANES), F32),
         pltpu.VMEM((128, 256), F32),
         pltpu.VMEM((256, 128), BF16),
@@ -488,20 +505,49 @@
         pltpu.VMEM((128, rays), F32),
         pltpu.VMEM((8, LANES), F32),
         pltpu.VMEM((8 * PART, 256), F32),
-        pltpu.SemaphoreType.DMA((28,)),
+        pltpu.SemaphoreType.DMA((29,)),
     ]
-    pairs = []
-    for k in (0, 1, 2, 3, 4):
-        pairs += [local[k], other[k]]
-    pairs += [mask.reshape(1, rays), other[6].reshape(1, rays)]
     return pl.pallas_call(
-        field_kernel,
+        functools.partial(field_kernel, find_place),
         out_shape=[jax.ShapeDtypeStruct((4 * PART, 256), F32)] * 2,
-        in_specs=[smem] * 3 + [hbm] * 6 + [vmem] * 11,
+        in_specs=[smem] * 2 + [hbm] * 4 + [vmem] * 9,
         out_specs=[vmem, vmem],
         scratch_shapes=scratch,
         compiler_params=pltpu.CompilerParams(vmem_limit_bytes=62 << 20),
-    )(counts, other[5], place, *pairs, w_in, w_mid, w_head, w_rgb.T, vec)
+    )(
+        counts,
+        other_counts,
+        other,
+        means,
+        variances,
+        spacing,
+        dirs,
+        target,
+        mask.reshape(1, rays),
+        counts,
+        w_in,
+        w_mid,
+        w_head,
+        w_rgb.T,
+        vec,
+    )
+
+
+def second_half(local):
+    means, variances, spacing, dirs, target, counts, mask = local
+    rays = dirs.shape[1]
+    own = rays // 2
+    small = jnp.concatenate([dirs, target, mask[None].astype(F32), counts.astype(F32)], axis=0)
+    small = jnp.pad(small, ((0, 16 - small.shape[0]), (0, LANES - rays)))
+    return jnp.concatenate(
+        [
+            means[:, :, own:].reshape(6 * own, LANES),
+            variances[:, :, own:].reshape(6 * own, LANES),
+            spacing[:, own:].reshape(2 * own, LANES),
+            small,
+        ],
+        axis=0,
+    )
 
 
 def adamw(weight, grad, first, second):
@@ -513,16 +559,16 @@
     return first, second, fresh
 
 
-def update_kernel(place, own, near, pair, other, *refs):
+def update_kernel(find_place, *refs):
+    place = find_place()
+    pieces, refs = refs[0:8], refs[8:]
     weights, firsts, seconds = refs[0:5], refs[5:10], refs[10:15]
     loss, count = refs[15], refs[16]
     outs = refs[17:32]
     packed = refs[32]
-    for ref, base in ((own, 0), (near, 1), (pair, 2), (other, 4)):
-        for k in range(ref.shape[0] // PART):
-            position = base + k
-            block = (place[0] ^ position) if position < 4 else (place[1] ^ (position - 4))
-            packed[pl.ds(pl.multiple_of(block * PART, 8), PART), :] = ref[k * PART : (k + 1) * PART, :]
+    for k, ref in enumerate(pieces):
+        block = place[k // 4] ^ (k % 4)
+        packed[pl.ds(pl.multiple_of(block * PART, 8), PART), :] = ref[...]
     line = packed[740:741, 128:256]
     loss[0] = line[0, 4]
     count[0] = line[0, 5]
@@ -548,46 +594,56 @@
     apply(4, (pl.ds(1152, 4),), packed[740:741, 128:132].reshape(4))
 
 
-def update(place, pieces, params, firsts, seconds):
+def update(find_place, pieces, params, firsts, seconds):
     vmem = pl.BlockSpec(memory_space=pltpu.VMEM)
     smem = pl.BlockSpec(memory_space=pltpu.SMEM)
     shapes = [jax.ShapeDtypeStruct((1,), F32)] * 2
     for array in params:
         shapes += [jax.ShapeDtypeStruct(array.shape, F32)] * 3
     return pl.pallas_call(
-        update_kernel,
+        functools.partial(update_kernel, find_place),
         out_shape=shapes,
-        in_specs=[smem] + [vmem] * 19,
+        in_specs=[vmem] * 23,
         out_specs=[smem, smem] + [vmem] * 15,
         scratch_shapes=[pltpu.VMEM((8 * PART, 256), F32)],
         compiler_params=pltpu.CompilerParams(vmem_limit_bytes=32 << 20),
-    )(place, *pieces, *params, *firsts, *seconds)
+    )(*pieces, *params, *firsts, *seconds)
 
 
 def xor_pairs(total, mask_of):
     return [(i, i ^ mask_of(i)) for i in range(total)]
+
+
+def place_small():
+    ray = lax.axis_index("rays")
+    rep = lax.axis_index("rep")
+    y, x, core = ray % 2, rep // 2, rep % 2
+    xy, yx = 2 * x + y, 2 * y + x
+    return (
+        jnp.where(core == 0, xy, 4 + yx),
+        jnp.where(core == 0, 4 + yx, xy),
+    )
 
 
 def reduce_small(keep, send, axes):
     core = xor_pairs(32, lambda i: 1)
     one = xor_pairs(32, lambda i: 4 if i & 1 else 2)
     two = xor_pairs(32, lambda i: 2 if i & 1 else 4)
+    both = xor_pairs(32, lambda i: 6)
     z_one = xor_pairs(32, lambda i: 16 if i & 1 else 8)
     z_two = xor_pairs(32, lambda i: 8 if i & 1 else 16)
 
     def swap(value, pairs):
         return lax.ppermute(value, axes, pairs)
 
+    square = (two, one, both)
     now = keep + swap(send, core)
-    now = now[: 2 * PART] + swap(now[2 * PART :], one)
-    own = now[:PART] + swap(now[PART:], two)
+    got = [swap(now[PART * (k + 1) : PART * (k + 2)], pairs) for k, pairs in enumerate(square)]
+    own = (now[:PART] + got[0]) + (got[1] + got[2])
     own = own + swap(own, z_one)
     own = own + swap(own, z_two)
-    near = swap(own, two)
-    half = jnp.concatenate([own, near], axis=0)
-    pair = swap(half, one)
-    other = swap(jnp.concatenate([half, pair], axis=0), core)
-    return own, near, pair, other
+    parts = [own] + [swap(own, pairs) for pairs in square]
+    return parts + [swap(part, core) for part in parts]
 
 
 def on_device(
@@ -616,27 +672,21 @@
     second_vec,
 ):
     axes = ("rays", "rep")
-    if small_mesh:
-        index = lax.axis_index(axes)
-        core, x, y = index & 1, (index >> 1) & 1, (index >> 2) & 1
-        place = jnp.stack([core * 4 + jnp.where(core == 0, 2 * x + y, 2 * y + x), (1 - core) * 4 + jnp.where(core == 0, 2 * y + x, 2 * x + y)])
-    else:
-        place = jnp.array([0, 4], jnp.int32)
-    place = place.astype(jnp.int32)
+    find_place = place_small if small_mesh else lambda: (0, 4)
     params = (w_in, w_mid, w_head, w_rgb, vectors)
     local = (sample_means, sample_vars, sample_spacing, view_dirs, target_rgb, sample_counts, ray_mask)
-    other = local
+    other, other_counts = second_half(local), sample_counts
     if small_mesh:
         core_pairs = xor_pairs(32, lambda i: 1)
-        other = tuple(lax.ppermute(array, axes, core_pairs) for array in local)
-    keep, send = field_gradients(place, local, other, params)
+        other, other_counts = (lax.ppermute(array, axes, core_pairs) for array in (other, other_counts))
+    keep, send = field_gradients(find_place, local, other, other_counts, params)
     if small_mesh:
         pieces = reduce_small(keep, send, axes)
     else:
         whole = lax.psum(jnp.concatenate([keep, send], axis=0), axes)
-        pieces = (whole[:PART], whole[PART : 2 * PART], whole[2 * PART : 4 * PART], whole[4 * PART :])
+        pieces = [whole[PART * k : PART * (k + 1)] for k in range(8)]
     outs = update(
-        place,
+        find_place,
         pieces,
         (w_in, w_mid, w_head, w_rgb.T, vectors),
         (first_in, first_mid, first_head, first_rgb.T, first_vec),

time: 76.7 us -> 82.1 us (1.070)
  Pallas kernels: 31.2 us -> 44 us
  starting transfers between devices: 17.1 us -> 11 us
  waiting for transfers between devices: 23.5 us -> 22.4 us
    pallas_call x2, Pallas kernels: 31.2 us -> 44 us  [the longest x1 41.8 us: field_gradients(): pl.pallas_call(functools.partial(field_kernel, find_place), out_shape=[ja...]
    ppermute x8 -> x13, starting transfers between devices: 15.1 us -> 10.4 us  [swap(): return lax.ppermute(value, axes, pairs)]
    ppermute x7 -> x2, starting transfers between devices: 2.05 us -> 0.6 us  [on_device(): lax.ppermute(array, axes, core_pairs)]
    ppermute x8 -> x13, waiting for transfers between devices: 22.5 us -> 21.3 us  [swap(): return lax.ppermute(value, axes, pairs)]
    unnamed x48 -> x40, local copies, waits for them, and re-layouts: 1.69 us -> 1.43 us
  transfers between devices with their start and end apart: 15 -> 15, of which waited for: 10 -> 11; matrix products, arithmetic and copies ran while one was open for 1% -> 0% of each run, Pallas kernels for 0% -> 0%
where the time goes in v3:
time: 82.1 us; the launch traced here: 81.9 us
  Pallas kernels  44 us (54%)
  waiting for transfers between devices  22.4 us (27%)
  starting transfers between devices  11 us (13%)
  other arithmetic  1.86 us (2%)
  local copies, waits for them, and re-layouts  1.74 us (2%)
  between operations  0.95 us (1%)
    pallas_call x1, Pallas kernels, field_gradients(): pl.pallas_call(functools.partial(field_kernel, find_place), out_shape=[ja...  41.8 us
    ppermute x13, waiting for transfers between devices, swap(): return lax.ppermute(value, axes, pairs)  21.3 us
    ppermute x13, starting transfers between devices, swap(): return lax.ppermute(value, axes, pairs)  10.4 us
    pallas_call x1, Pallas kernels, update(): pl.pallas_call(functools.partial(update_kernel, find_place), out_shape=sh...  2.2 us
  transfers between devices with their start and end apart: 15, of which 11 were waited for; matrix products, arithmetic and copies ran while one was open for 0% of the time, Pallas kernels for 0%

profile of v3, /device:TPU:0, one launch (start us, length us, event | category | flops | bytes accessed | tf_op | source)
XLA Modules:
  0.0 81.9 jit_solution(8744527688616353862)
XLA Ops:
  0.7 0.0 copy-start.16
  0.7 0.7 convert_bitcast_fusion
  1.3 0.0 copy-done.16
  1.4 0.0 slice-start.2
  1.4 0.0 slice-start
  1.4 0.0 slice-start.1
  1.4 0.6 copy-done.17
  2.0 0.0 copy-done.18
  2.1 0.1 slice-done.2
  2.1 0.2 slice-done
  2.3 0.0 slice-done.1
  2.3 0.5 collective-permute-start.1
  2.9 0.1 collective-permute-start
  2.9 1.1 %collective-permute-done.counts_two = s32[2,64]{1,0:T(2,128)S(1)} collective-permute-done((s32[2,64]{1,0:T(2,128)S(1)}, s32[2,64]{1,0:T(2,128)S(1)}, u32[]{:S(2)}, u32[]{:S(2)}) %collective-permute-start) | collective-permute-done | bytes 544 | tf_op jit(solution)/shard_map/ppermute | solution.py:681
  4.0 0.0 collective-permute-done.1.other
  4.0 0.6 copy-done.19
  4.6 0.1 copy-done.15
  4.7 41.8 %shard_map.341 = (f32[384,256]{1,0:T(8,128)}, f32[384,256]{1,0:T(8,128)}) custom-call(s32[2,64]{1,0:T(2,128)} %counts_vec.1, s32[2,64]{1,0:T(2,128)} %copy-done.19, f32[464,128]{1,0:T(8,128)} %copy-done.15, f32[2,3,64,128]{3,2,1,0:T(8,128)} %means.1, f32[2,3,64,128]{3,2,1,0:T(8,128)} %variances.1, f32[2,64,128]{2,1,0:T(8,128)} %spacing.1, f32[3,64]{1,0:T(4,128)} %dirs.1, ...), custom_call_target="tpu_custom_call" | custom-call | tf_op jit(solution)/shard_map/pallas_call | solution.py:510
  46.5 3.1 %collective-permute-start.2 = (f32[384,256]{1,0:T(8,128)}, f32[384,256]{1,0:T(8,128)S(1)}, u32[]{:S(2)}, u32[]{:S(2)}) collective-permute-start(f32[384,256]{1,0:T(8,128)} %get-tuple-element.37), channel_id=1, source_target_pairs={{0,1},{1,0},{2,3},{3,2},{4,5},{5,4},{6,7},{7,6},{8,9},{9,8},{10,11... | collective-permute-start | bytes 1179656 | tf_op jit(solution)/shard_map/ppermute | solution.py:637
  49.6 1.6 %collective-permute-done.2 = f32[384,256]{1,0:T(8,128)S(1)} collective-permute-done((f32[384,256]{1,0:T(8,128)}, f32[384,256]{1,0:T(8,128)S(1)}, u32[]{:S(2)}, u32[]{:S(2)}) %collective-permute-start.2) | collective-permute-done | bytes 393248 | tf_op jit(solution)/shard_map/ppermute | solution.py:637
  51.2 1.1 %add.20 = f32[384,256]{1,0:T(8,128)S(1)} add(f32[384,256]{1,0:T(8,128)} %get-tuple-element.36, f32[384,256]{1,0:T(8,128)S(1)} %collective-permute-done.2) | non-fusion elementwise | flops 98304 | bytes 1179648 | tf_op jit(solution)/shard_map/add | solution.py:640
  52.3 0.0 copy-start.2
  52.3 0.0 copy-start.11
  52.4 0.1 collective-permute-start.5
  52.5 0.0 copy-start.14
  52.5 0.1 collective-permute-start.4
  52.6 0.0 copy-start.13
  52.6 0.0 copy-start
  52.6 3.4 %collective-permute-start.3 = (f32[96,256]{1,0:T(8,128)S(1)}, f32[96,256]{1,0:T(8,128)S(1)}, u32[]{:S(2)}, u32[]{:S(2)}) collective-permute-start(f32[96,256]{1,0:T(8,128)S(1)} %get-tuple-element.57), channel_id=1, source_target_pairs={{0,4},{1,3},{2,6},{3,1},{4,0},{5,7},{6,2},{7,5},{8,12},{9,11},{10,... | collective-permute-start | bytes 294920 | tf_op jit(solution)/shard_map/ppermute | solution.py:637
  56.0 3.1 %collective-permute-done.5 = f32[96,256]{1,0:T(8,128)S(1)} collective-permute-done((f32[96,256]{1,0:T(8,128)S(1)}, f32[96,256]{1,0:T(8,128)S(1)}, u32[]{:S(2)}, u32[]{:S(2)}) %collective-permute-start.5) | collective-permute-done | bytes 98336 | tf_op jit(solution)/shard_map/ppermute | solution.py:637
  59.0 0.0 collective-permute-done.4
  59.0 0.7 collective-permute-done.3
  59.8 0.1 collective-permute-start.6
  59.8 4.6 %collective-permute-done.6 = f32[96,256]{1,0:T(8,128)S(1)} collective-permute-done((f32[96,256]{1,0:T(8,128)S(1)}, f32[96,256]{1,0:T(8,128)S(1)}, u32[]{:S(2)}, u32[]{:S(2)}) %collective-permute-start.6) | collective-permute-done | bytes 98336 | tf_op jit(solution)/shard_map/ppermute | solution.py:637
  64.5 0.0 copy-start.1
  64.5 0.0 copy-start.4
  64.5 0.1 collective-permute-start.7
  64.6 6.0 %collective-permute-done.7 = f32[96,256]{1,0:T(8,128)S(1)} collective-permute-done((f32[96,256]{1,0:T(8,128)S(1)}, f32[96,256]{1,0:T(8,128)S(1)}, u32[]{:S(2)}, u32[]{:S(2)}) %collective-permute-start.7) | collective-permute-done | bytes 98336 | tf_op jit(solution)/shard_map/ppermute | solution.py:637
  70.6 0.0 copy-start.12
  70.6 1.5 %collective-permute-start.10 = (f32[96,256]{1,0:T(8,128)S(1)}, f32[96,256]{1,0:T(8,128)S(1)}, u32[]{:S(2)}, u32[]{:S(2)}) collective-permute-start(f32[96,256]{1,0:T(8,128)S(1)} %add.25.refs_0_), channel_id=1, source_target_pairs={{0,6},{1,7},{2,4},{3,5},{4,2},{5,3},{6,0},{7,1},{8,14},{9,15},{10,... | collective-permute-start | bytes 294920 | tf_op jit(solution)/shard_map/ppermute | solution.py:637
  72.1 1.6 %collective-permute-start.9 = (f32[96,256]{1,0:T(8,128)S(1)}, f32[96,256]{1,0:T(8,128)S(1)}, u32[]{:S(2)}, u32[]{:S(2)}) collective-permute-start(f32[96,256]{1,0:T(8,128)S(1)} %add.25.refs_0_), channel_id=1, source_target_pairs={{0,2},{1,5},{2,0},{3,7},{4,6},{5,1},{6,4},{7,3},{8,10},{9,13},{10,... | collective-permute-start | bytes 294920 | tf_op jit(solution)/shard_map/ppermute | solution.py:637
  73.6 0.5 collective-permute-start.8
  74.1 0.0 collective-permute-start.11
  74.1 2.0 %collective-permute-done.10.refs_3_ = f32[96,256]{1,0:T(8,128)S(1)} collective-permute-done((f32[96,256]{1,0:T(8,128)S(1)}, f32[96,256]{1,0:T(8,128)S(1)}, u32[]{:S(2)}, u32[]{:S(2)}) %collective-permute-start.10) | collective-permute-done | bytes 98336 | tf_op jit(solution)/shard_map/ppermute | solution.py:637
  76.2 0.0 collective-permute-start.14
  76.2 1.1 %collective-permute-done.9.refs_2_ = f32[96,256]{1,0:T(8,128)S(1)} collective-permute-done((f32[96,256]{1,0:T(8,128)S(1)}, f32[96,256]{1,0:T(8,128)S(1)}, u32[]{:S(2)}, u32[]{:S(2)}) %collective-permute-start.9) | collective-permute-done | bytes 98336 | tf_op jit(solution)/shard_map/ppermute | solution.py:637
  77.3 0.0 collective-permute-start.13
  77.3 1.0 %collective-permute-done.8.refs_1_ = f32[96,256]{1,0:T(8,128)S(1)} collective-permute-done((f32[96,256]{1,0:T(8,128)S(1)}, f32[96,256]{1,0:T(8,128)S(1)}, u32[]{:S(2)}, u32[]{:S(2)}) %collective-permute-start.8) | collective-permute-done | bytes 98336 | tf_op jit(solution)/shard_map/ppermute | solution.py:637
  78.2 0.0 collective-permute-start.12
  78.2 0.0 collective-permute-done.11.refs_4_
  78.2 0.0 collective-permute-done.14.refs_7_
  78.2 0.3 collective-permute-done.13.refs_6_
  78.6 1.0 %collective-permute-done.12.refs_5_ = f32[96,256]{1,0:T(8,128)S(1)} collective-permute-done((f32[96,256]{1,0:T(8,128)S(1)}, f32[96,256]{1,0:T(8,128)S(1)}, u32[]{:S(2)}, u32[]{:S(2)}) %collective-permute-start.12) | collective-permute-done | bytes 98336 | tf_op jit(solution)/shard_map/ppermute | solution.py:637
  79.5 0.0 copy-done.2
  79.6 0.0 copy-done.11
  79.6 0.0 copy-done.14
  79.6 0.0 copy-done.13
  79.6 0.0 copy-done
  79.6 0.0 copy-done.5
  79.6 0.0 copy-done.6
  79.6 0.0 copy-done.1
  79.6 0.0 copy-done.4
  79.6 0.0 copy-done.9
  79.7 2.2 %shard_map.342 = (f32[1]{0:T(128)}, f32[1]{0:T(128)}, f32[96,256]{1,0:T(8,128)}, f32[96,256]{1,0:T(8,128)}, f32[96,256]{1,0:T(8,128)}, /*index=5*/f32[2,256,256]...) custom-call(f32[96,256]{1,0:T(8,128)S(1)} %add.25.refs_0_, ...), custom_call_target="tpu_custom_call" | custom-call | tf_op jit(solution)/shard_map/pallas_call | solution.py:603
  (23 shorter events, 0.1 us)
Async XLA Ops:
  0.7 0.7 copy-start.16
  1.3 0.7 copy-start.17
  1.3 0.7 copy-start.18
  1.4 0.8 slice-start.2
  1.4 0.9 %slice-start = ((f32[2,3,64,128]{3,2,1,0:T(8,128)}), f32[2,3,32,128]{3,2,1,0:T(8,128)S(1)}, s32[]{:S(2)}) async-start(f32[2,3,64,128]{3,2,1,0:T(8,128)} %variances.1), calls=%async_computation | async-start | bytes 196608 | tf_op jit(solution)/shard_map/slice | solution.py:545
  1.4 1.0 %slice-start.1 = ((f32[2,3,64,128]{3,2,1,0:T(8,128)}), f32[2,3,32,128]{3,2,1,0:T(8,128)S(1)}, s32[]{:S(2)}) async-start(f32[2,3,64,128]{3,2,1,0:T(8,128)} %means.1), calls=%async_computation.1 | async-start | bytes 196608 | tf_op jit(solution)/shard_map/slice | solution.py:544
  2.3 1.7 %collective-permute-start.1 = (f32[464,128]{1,0:T(8,128)S(1)}, f32[464,128]{1,0:T(8,128)S(1)}, u32[]{:S(2)}, u32[]{:S(2)}) collective-permute-start(f32[464,128]{1,0:T(8,128)S(1)} %pad_maximum_fusion), channel_id=1, source_target_pairs={{0,1},{1,0},{2,3},{3,2},{4,5},{5,4},{6,7},{7,6},{8,9},{9,8},{10,11... | collective-permute-start | bytes 712712 | tf_op jit(solution)/shard_map/ppermute | solution.py:681
  2.9 1.1 %collective-permute-start = (s32[2,64]{1,0:T(2,128)S(1)}, s32[2,64]{1,0:T(2,128)S(1)}, u32[]{:S(2)}, u32[]{:S(2)}) collective-permute-start(s32[2,64]{1,0:T(2,128)S(1)} %copy-done.16), channel_id=1, source_target_pairs={{0,1},{1,0},{2,3},{3,2},{4,5},{5,4},{6,7},{7,6},{8,9},{9,8},{10,11... | collective-permute-start | bytes 1544 | tf_op jit(solution)/shard_map/ppermute | solution.py:681
  4.0 0.6 copy-start.19
  4.0 0.7 copy-start.15
  46.5 4.7 %collective-permute-start.2 = (f32[384,256]{1,0:T(8,128)}, f32[384,256]{1,0:T(8,128)S(1)}, u32[]{:S(2)}, u32[]{:S(2)}) collective-permute-start(f32[384,256]{1,0:T(8,128)} %get-tuple-element.37), channel_id=1, source_target_pairs={{0,1},{1,0},{2,3},{3,2},{4,5},{5,4},{6,7},{7,6},{8,9},{9,8},{10,11... | collective-permute-start | bytes 1179656 | tf_op jit(solution)/shard_map/ppermute | solution.py:637
  51.2 28.3 %copy-start.3 = (f32[2,256,256]{2,1,0:T(8,128)S(1)}, f32[2,256,256]{2,1,0:T(8,128)}, u32[]{:S(2)}) copy-start(f32[2,256,256]{2,1,0:T(8,128)} %refs_19_.1) | copy-start | bytes 1572868
  51.2 28.3 %copy-start.7 = (f32[96,256]{1,0:T(8,128)S(1)}, f32[96,256]{1,0:T(8,128)}, u32[]{:S(2)}) copy-start(f32[96,256]{1,0:T(8,128)} %refs_13_.1) | copy-start | bytes 294916
  51.2 28.3 %copy-start.8 = (f32[96,256]{1,0:T(8,128)S(1)}, f32[96,256]{1,0:T(8,128)}, u32[]{:S(2)}) copy-start(f32[96,256]{1,0:T(8,128)} %refs_18_.1) | copy-start | bytes 294916
  52.3 27.2 %copy-start.2 = (f32[2,256,256]{2,1,0:T(8,128)S(1)}, f32[2,256,256]{2,1,0:T(8,128)}, u32[]{:S(2)}) copy-start(f32[2,256,256]{2,1,0:T(8,128)} %refs_14_.1) | copy-start | bytes 1572868
  52.3 27.2 %copy-start.11 = (f32[1156]{0:T(1024)S(1)}, f32[1156]{0:T(1024)}, u32[]{:S(2)}) copy-start(f32[1156]{0:T(1024)} %refs_22_.1) | copy-start | bytes 13876
  52.4 6.6 %collective-permute-start.5 = (f32[96,256]{1,0:T(8,128)S(1)}, f32[96,256]{1,0:T(8,128)S(1)}, u32[]{:S(2)}, u32[]{:S(2)}) collective-permute-start(f32[96,256]{1,0:T(8,128)S(1)} %get-tuple-element.55), channel_id=1, source_target_pairs={{0,6},{1,7},{2,4},{3,5},{4,2},{5,3},{6,0},{7,1},{8,14},{9,15},{10,... | collective-permute-start | bytes 294920 | tf_op jit(solution)/shard_map/ppermute | solution.py:637
  52.5 27.1 %copy-start.14 = (f32[128,3]{0,1:T(4,128)S(1)}, f32[128,3]{0,1:T(4,128)}, u32[]{:S(2)}) copy-start(f32[128,3]{0,1:T(4,128)} %param.42) | copy-start | bytes 4612
  52.5 6.6 %collective-permute-start.4 = (f32[96,256]{1,0:T(8,128)S(1)}, f32[96,256]{1,0:T(8,128)S(1)}, u32[]{:S(2)}, u32[]{:S(2)}) collective-permute-start(f32[96,256]{1,0:T(8,128)S(1)} %get-tuple-element.56), channel_id=1, source_target_pairs={{0,2},{1,5},{2,0},{3,7},{4,6},{5,1},{6,4},{7,3},{8,10},{9,13},{10,... | collective-permute-start | bytes 294920 | tf_op jit(solution)/shard_map/ppermute | solution.py:637
  52.6 27.0 %copy-start.13 = (f32[128,3]{0,1:T(4,128)S(1)}, f32[128,3]{0,1:T(4,128)}, u32[]{:S(2)}) copy-start(f32[128,3]{0,1:T(4,128)} %param.37) | copy-start | bytes 4612
  52.6 27.0 %copy-start = (f32[2,256,256]{2,1,0:T(8,128)S(1)}, f32[2,256,256]{2,1,0:T(8,128)}, u32[]{:S(2)}) copy-start(f32[2,256,256]{2,1,0:T(8,128)} %refs_9_.1) | copy-start | bytes 1572868
  52.6 7.1 %collective-permute-start.3 = (f32[96,256]{1,0:T(8,128)S(1)}, f32[96,256]{1,0:T(8,128)S(1)}, u32[]{:S(2)}, u32[]{:S(2)}) collective-permute-start(f32[96,256]{1,0:T(8,128)S(1)} %get-tuple-element.57), channel_id=1, source_target_pairs={{0,4},{1,3},{2,6},{3,1},{4,0},{5,7},{6,2},{7,5},{8,12},{9,11},{10,... | collective-permute-start | bytes 294920 | tf_op jit(solution)/shard_map/ppermute | solution.py:637
  59.8 4.7 %collective-permute-start.6 = (f32[96,256]{1,0:T(8,128)S(1)}, f32[96,256]{1,0:T(8,128)S(1)}, u32[]{:S(2)}, u32[]{:S(2)}) collective-permute-start(f32[96,256]{1,0:T(8,128)S(1)} %fusion), channel_id=1, source_target_pairs={{0,8},{1,17},{2,10},{3,19},{4,12},{5,21},{6,14},{7,23},{8,0},{9,25... | collective-permute-start | bytes 294920 | tf_op jit(solution)/shard_map/ppermute | solution.py:637
  64.4 15.2 %copy-start.5 = (f32[283,128]{1,0:T(8,128)S(1)}, f32[283,128]{1,0:T(8,128)}, u32[]{:S(2)}) copy-start(f32[283,128]{1,0:T(8,128)} %refs_15_.1) | copy-start | bytes 434692
  64.4 15.2 %copy-start.6 = (f32[283,128]{1,0:T(8,128)S(1)}, f32[283,128]{1,0:T(8,128)}, u32[]{:S(2)}) copy-start(f32[283,128]{1,0:T(8,128)} %refs_20_.1) | copy-start | bytes 434692
  64.5 15.2 %copy-start.1 = (f32[283,128]{1,0:T(8,128)S(1)}, f32[283,128]{1,0:T(8,128)}, u32[]{:S(2)}) copy-start(f32[283,128]{1,0:T(8,128)} %refs_10_.1) | copy-start | bytes 434692
  64.5 15.2 %copy-start.4 = (f32[96,256]{1,0:T(8,128)S(1)}, f32[96,256]{1,0:T(8,128)}, u32[]{:S(2)}) copy-start(f32[96,256]{1,0:T(8,128)} %refs_8_.1) | copy-start | bytes 294916
  64.5 6.1 %collective-permute-start.7 = (f32[96,256]{1,0:T(8,128)S(1)}, f32[96,256]{1,0:T(8,128)S(1)}, u32[]{:S(2)}, u32[]{:S(2)}) collective-permute-start(f32[96,256]{1,0:T(8,128)S(1)} %add.24), channel_id=1, source_target_pairs={{0,16},{1,9},{2,18},{3,11},{4,20},{5,13},{6,22},{7,15},{8,24},{9,1... | collective-permute-start | bytes 294920 | tf_op jit(solution)/shard_map/ppermute | solution.py:637
  70.6 9.1 %copy-start.9 = (f32[1156]{0:T(1024)S(1)}, f32[1156]{0:T(1024)}, u32[]{:S(2)}) copy-start(f32[1156]{0:T(1024)} %refs_12_.1) | copy-start | bytes 13876
  70.6 9.1 %copy-start.10 = (f32[1156]{0:T(1024)S(1)}, f32[1156]{0:T(1024)}, u32[]{:S(2)}) copy-start(f32[1156]{0:T(1024)} %refs_17_.1) | copy-start | bytes 13876
  70.6 9.1 %copy-start.12 = (f32[128,3]{0,1:T(4,128)S(1)}, f32[128,3]{0,1:T(4,128)}, u32[]{:S(2)}) copy-start(f32[128,3]{0,1:T(4,128)} %param.32) | copy-start | bytes 4612
  70.6 5.6 %collective-permute-start.10 = (f32[96,256]{1,0:T(8,128)S(1)}, f32[96,256]{1,0:T(8,128)S(1)}, u32[]{:S(2)}, u32[]{:S(2)}) collective-permute-start(f32[96,256]{1,0:T(8,128)S(1)} %add.25.refs_0_), channel_id=1, source_target_pairs={{0,6},{1,7},{2,4},{3,5},{4,2},{5,3},{6,0},{7,1},{8,14},{9,15},{10,... | collective-permute-start | bytes 294920 | tf_op jit(solution)/shard_map/ppermute | solution.py:637
  72.1 5.2 %collective-permute-start.9 = (f32[96,256]{1,0:T(8,128)S(1)}, f32[96,256]{1,0:T(8,128)S(1)}, u32[]{:S(2)}, u32[]{:S(2)}) collective-permute-start(f32[96,256]{1,0:T(8,128)S(1)} %add.25.refs_0_), channel_id=1, source_target_pairs={{0,2},{1,5},{2,0},{3,7},{4,6},{5,1},{6,4},{7,3},{8,10},{9,13},{10,... | collective-permute-start | bytes 294920 | tf_op jit(solution)/shard_map/ppermute | solution.py:637
  73.6 4.6 %collective-permute-start.8 = (f32[96,256]{1,0:T(8,128)S(1)}, f32[96,256]{1,0:T(8,128)S(1)}, u32[]{:S(2)}, u32[]{:S(2)}) collective-permute-start(f32[96,256]{1,0:T(8,128)S(1)} %add.25.refs_0_), channel_id=1, source_target_pairs={{0,4},{1,3},{2,6},{3,1},{4,0},{5,7},{6,2},{7,5},{8,12},{9,11},{10,... | collective-permute-start | bytes 294920 | tf_op jit(solution)/shard_map/ppermute | solution.py:637
  74.1 4.1 %collective-permute-start.11 = (f32[96,256]{1,0:T(8,128)S(1)}, f32[96,256]{1,0:T(8,128)S(1)}, u32[]{:S(2)}, u32[]{:S(2)}) collective-permute-start(f32[96,256]{1,0:T(8,128)S(1)} %add.25.refs_0_), channel_id=1, source_target_pairs={{0,1},{1,0},{2,3},{3,2},{4,5},{5,4},{6,7},{7,6},{8,9},{9,8},{10,11... | collective-permute-start | bytes 294920 | tf_op jit(solution)/shard_map/ppermute | solution.py:637
  76.2 2.1 %collective-permute-start.14 = (f32[96,256]{1,0:T(8,128)S(1)}, f32[96,256]{1,0:T(8,128)S(1)}, u32[]{:S(2)}, u32[]{:S(2)}) collective-permute-start(f32[96,256]{1,0:T(8,128)S(1)} %collective-permute-done.10.refs_3_), channel_id=1, source_target_pairs={{0,1},{1,0},{2,3},{3,2},{4,5},{5,4},{6,7},{7,6},{8,9},{9,8},{10,11... | collective-permute-start | bytes 294920 | tf_op jit(solution)/shard_map/ppermute | solution.py:637
  77.3 1.3 %collective-permute-start.13 = (f32[96,256]{1,0:T(8,128)S(1)}, f32[96,256]{1,0:T(8,128)S(1)}, u32[]{:S(2)}, u32[]{:S(2)}) collective-permute-start(f32[96,256]{1,0:T(8,128)S(1)} %collective-permute-done.9.refs_2_), channel_id=1, source_target_pairs={{0,1},{1,0},{2,3},{3,2},{4,5},{5,4},{6,7},{7,6},{8,9},{9,8},{10,11... | collective-permute-start | bytes 294920 | tf_op jit(solution)/shard_map/ppermute | solution.py:637
  78.2 1.3 %collective-permute-start.12 = (f32[96,256]{1,0:T(8,128)S(1)}, f32[96,256]{1,0:T(8,128)S(1)}, u32[]{:S(2)}, u32[]{:S(2)}) collective-permute-start(f32[96,256]{1,0:T(8,128)S(1)} %collective-permute-done.8.refs_1_), channel_id=1, source_target_pairs={{0,1},{1,0},{2,3},{3,2},{4,5},{5,4},{6,7},{7,6},{8,9},{9,8},{10,11... | collective-permute-start | bytes 294920 | tf_op jit(solution)/shard_map/ppermute | solution.py:637

commit v4 on v3

--- a/solution.py
+++ b/solution.py
@@ -96,7 +96,6 @@
     feat,
     feat_pre,
     one_hot,
-    dz_c,
     small_two,
     rows,
     wide,
@@ -111,10 +110,8 @@
     view_t,
     venc,
     g_in,
-    g_mid,
-    g_head,
-    g_rgb,
-    s_ray,
+    g_low,
+    g_top,
     g_sum,
     packed,
     sem,
@@ -122,17 +119,19 @@
     place = find_place()
     rays = dirs.shape[1]
     own = rays // 2
-    tiles = rays
     pitch = z_planes.shape[0] // 8
+    pk_pitch = pk.shape[0] // 16
+    capacity = hidden_c.shape[1] - LANES
+    tiles = -(-capacity // (8 * LANES)) * 8
     copies = []
     for p in range(2):
         for k, source in enumerate((means, variances)):
             for c in range(3):
-                to = (p * 8 + 4 * k + c) * pitch
+                to = (p * 8 + 4 * k + c) * pk_pitch
                 copies.append((source.at[p, c, pl.ds(0, own)], pk.at[pl.ds(to, own)]))
                 row = (6 * k + 3 * p + c) * own
                 copies.append((other.at[pl.ds(row, own)], pk.at[pl.ds(to + own, own)]))
-        to = (p * 8 + 7) * pitch
+        to = (p * 8 + 7) * pk_pitch
         copies.append((spacing.at[p, pl.ds(0, own)], pk.at[pl.ds(to, own)]))
         copies.append((other.at[pl.ds((12 + p) * own, own)], pk.at[pl.ds(to + own, own)]))
     copies.append((other.at[pl.ds(14 * own, 16)], small_two))
@@ -205,7 +204,7 @@
     one_row = (lax.broadcasted_iota(jnp.int32, (16, hidden_a.shape[1]), 0) == 0).astype(BF16)
     hidden_a[256:272, :] = one_row
     hidden_b[256:272, :] = one_row
-    for ref in (g_planes, g_in, g_mid, g_head, g_rgb, s_ray, g_sum):
+    for ref in (g_planes, g_in, g_low, g_top, g_sum, packed):
         ref[...] = jnp.zeros_like(ref)
 
     lane8 = lax.broadcasted_iota(jnp.int32, (8, LANES), 1)
@@ -228,9 +227,10 @@
 
     def encode(i):
         at = place_of(i)
-        x = xs[:, at]
+        x = [xs[i * per + k] for k in range(per)]
         for k in range(per):
-            x_planes[pl.ds(i * per + k, 8, stride=pitch), :] = x[:, k * LANES : (k + 1) * LANES]
+            x_planes[pl.ds(i * per + k, 8, stride=pitch), :] = x[k]
+        x = jnp.concatenate(x, axis=1)
         sub = lax.broadcasted_iota(jnp.int32, (8, size), 0)
         turned = pltpu.roll(x, 4, 0)
         low = sub < 4
@@ -290,12 +290,12 @@
         lax.fori_loop(0, blocks + 2, step, 0)
 
     def backward_all(blocks):
-        size = BACK
-        per = size // LANES
-
-        def step(i, carry):
-            at = pl.ds(pl.multiple_of(i * size, LANES), size)
-            dz = jnp.concatenate([g_planes[pl.ds(i * per + k, 8, stride=pitch), :] for k in range(per)], axis=1)
+        def step(start, size):
+            per = size // LANES
+            at = pl.ds(pl.multiple_of(start, LANES), size)
+            dz = jnp.concatenate(
+                [g_planes[pl.ds(start // LANES + k, 8, stride=pitch), :] for k in range(per)], axis=1
+            )
             dzw = dz.astype(BF16).astype(F32)
             part = dzw[:, 0:LANES]
             for k in range(1, per):
@@ -305,42 +305,54 @@
             dz_f = (dot_nn(wr[...], dz) * slope(feat_pre[:, at])).astype(BF16)
             both = jnp.concatenate([dz_f, dz], axis=0)
             up = dot_nn(whd[...], both)
-            g_head[...] += dot_nt(both, hidden_c[:, at])
-            s_ray[...] += dot_nt(dz_f, one_hot[:, at])
-            g_rgb[...] += dot_nt(dz, feat[:, at])
+            g_top[:, 0:144] += dot_nt(jnp.concatenate([hidden_c[:, at], one_hot[:, at], feat[:, at]], axis=0), both)
             dz = (up * slope(pre_c[:, at])).astype(BF16)
             up = dot_nn(wm[1], dz)
-            g_mid[1] += dot_nt(hidden_b[:, at], dz)
+            made = dot_nt(hidden_b[:, at], dz)
+            packed[352:608, :] += made[0:256, :]
+            g_low[1] += made[256:272, :]
             dz = (up * slope(pre_b[:, at])).astype(BF16)
             up = dot_nn(wm[0], dz)
-            g_mid[0] += dot_nt(hidden_a[:, at], dz)
+            made = dot_nt(hidden_a[:, at], dz)
+            packed[96:352, :] += made[0:256, :]
+            g_low[0] += made[256:272, :]
             dz = (up * slope(pre_a[:, at])).astype(BF16)
             g_in[...] += dot_nt(enc[:, at], dz)
+
+        def large(i, carry):
+            step(i * BACK, BACK)
             return carry
 
-        lax.fori_loop(0, (blocks + BACK // BLOCK - 1) // (BACK // BLOCK), step, 0)
+        def small(i, carry):
+            step(i * BLOCK, BLOCK)
+            return carry
+
+        lax.fori_loop(0, blocks // 2, large, 0)
+        lax.fori_loop(blocks // 2 * 2, blocks, small, 0)
 
     group = 8
 
     def chunk(first, passes, loss):
-        xs[...] = jnp.where(lax.broadcasted_iota(jnp.int32, xs.shape, 0) == 3, -1.0, 0.0)
+        xs[...] = jnp.where(lax.broadcasted_iota(jnp.int32, xs.shape, 1) == 3, -1.0, 0.0)
         x_planes[...] = jnp.full_like(x_planes, -1.0)
 
         def pack(p, part, g, offset):
             r0 = part * own + g * group
+            item0 = (p * rays + r0).astype(F32)
+            base = p * 8 * pk_pitch + r0
             moved = []
             for j in range(group):
                 count = (counts, counts_two)[part][p, r0 + j]
-                here = pk[pl.ds(p * 8 * pitch + r0 + j, 8, stride=pitch), :]
-                item = jnp.where(lane8 < count, (p * rays + r0 + j).astype(F32), -1.0)
+                here = pk[pl.ds(base + j, 8, stride=pk_pitch), :]
+                item = jnp.where(lane8 < count, item0 + float(j), -1.0)
                 here = jnp.where(sub8 == 3, item, here)
                 o = offset & (LANES - 1)
-                moved.append((pltpu.roll(here, o, 1), o, pl.multiple_of(offset - o, LANES)))
+                moved.append((pltpu.roll(here, o, 1), o, offset >> 7))
                 offset = offset + count
             for turned, o, t in moved:
                 keep_low = lane8 >= o
-                pltpu.store(xs.at[:, pl.ds(t, LANES)], turned, mask=keep_low)
-                pltpu.store(xs.at[:, pl.ds(t + LANES, LANES)], turned, mask=jnp.logical_not(keep_low))
+                pltpu.store(xs.at[t], turned, mask=keep_low)
+                pltpu.store(xs.at[t + 1], turned, mask=jnp.logical_not(keep_low))
             return offset
 
         def pack_pass(p, offset):
@@ -349,7 +361,7 @@
             return offset
 
         total = lax.fori_loop(first, first + passes, pack_pass, jnp.int32(0))
-        blocks = (total + BACK - 1) // BACK * (BACK // BLOCK)
+        blocks = (total + BLOCK - 1) // BLOCK
         forward_all(blocks)
 
         def plane(ref, k):
@@ -418,7 +430,7 @@
     wide[0:2, 0:own] = counts_vec[:, 0:own].astype(F32)
     wide[0:2, own:rays] = small_two[7:9, own:rays]
     everything = jnp.sum(wide[0:2, 0:rays])
-    at_once = everything <= 1.0 * tiles * LANES
+    at_once = everything <= 1.0 * capacity
     chunks = jnp.where(at_once, 1, 2)
     passes = jnp.where(at_once, 2, 1)
     loss = lax.fori_loop(0, chunks, lambda i, loss: chunk(i, passes, loss), jnp.zeros((), F32))
@@ -428,17 +440,14 @@
             for k in range(2):
                 at, to = 64 * k + 16 * d + 4 * a, 48 * k + 12 * a + 3 * d
                 packed[to : to + 3, :] = g_in[at : at + 3, :]
+    rays_sum = g_top[256 : 256 + rays, 0:128]
+    packed[736:737, :] = g_in[67:68, :]
+    packed[737:738, :] = g_low[0, 0:1, :]
+    packed[738:739, :] = g_low[1, 0:1, :]
     for k in range(2):
-        packed[96 + 256 * k : 352 + 256 * k, :] = g_mid[k, 0:256, :]
-    packed[608:736, :] = g_head[0:128, :]
-    rays_sum = s_ray[...]
-    packed[736:768, :] = jnp.zeros((32, 256), F32)
-    packed[736:737, :] = g_in[67:68, :]
-    packed[737:738, :] = g_mid[0, 256:257, :]
-    packed[738:739, :] = g_mid[1, 256:257, :]
-    packed[739:740, :] = g_head[131:132, :]
-    feat_b = jnp.sum(rays_sum, axis=1, keepdims=True)
-    packed[740:741, 0:128] = jnp.broadcast_to(feat_b, (128, 128)).T[0:1, :]
+        packed[608:736, 128 * k : 128 * k + 128] = g_top[128 * k : 128 * k + 128, 0:128]
+        packed[739:740, 128 * k : 128 * k + 128] = g_top[128 * k : 128 * k + 128, 128:256].T[3:4, :]
+    packed[740:741, 0:128] = jnp.sum(rays_sum, axis=0, keepdims=True)
     small = jnp.sum(g_sum[...], axis=1, keepdims=True)
     lane1 = lax.broadcasted_iota(jnp.int32, (1, LANES), 1)
     line = jnp.zeros((1, LANES), F32)
@@ -447,10 +456,10 @@
     line = line + jnp.where(lane1 == 4, loss, 0.0)
     line = line + jnp.where(lane1 == 5, count_here, 0.0)
     packed[740:741, 128:256] = line
-    packed[741:744, 0:128] = g_rgb[0:3, :]
+    packed[741:744, 0:128] = g_top[256 + rays : 384 + rays, 128:256].T[0:3, :]
     view_grad = jnp.zeros((32, 128), F32)
     for piece in split_three(rays_sum):
-        view_grad = view_grad + dot_nt(venc[...], piece)
+        view_grad = view_grad + dot_nn(venc[...], piece)
     packed[744:760, 0:128] = view_grad[0:16, :]
     packed[744:760, 128:256] = view_grad[16:32, :]
     for q in range(4):
@@ -463,14 +472,15 @@
     means, variances, spacing, dirs, target, counts, mask = local
     w_in, w_mid, w_head, w_rgb, vec = params
     rays = dirs.shape[1]
-    room = rays * LANES + LANES
-    pitch = rays + 8
+    room = 17 * rays * LANES // 16 + LANES
+    tiles = -(-(room - LANES) // (8 * LANES)) * 8
+    pitch = tiles + 8 * (1 - tiles // 8 % 2)
     vmem = pl.BlockSpec(memory_space=pltpu.VMEM)
     smem = pl.BlockSpec(memory_space=pltpu.SMEM)
     hbm = pl.BlockSpec(memory_space=pl.ANY)
     scratch = [
-        pltpu.VMEM((2 * 8 * pitch, LANES), F32),
-        pltpu.VMEM((8, room + LANES), F32),
+        pltpu.VMEM((2 * 8 * (rays + 8), LANES), F32),
+        pltpu.VMEM((room // LANES + 1, 8, LANES), F32),
         pltpu.VMEM((8 * pitch, LANES), F32),
         pltpu.VMEM((8 * pitch, LANES), F32),
         pltpu.VMEM((8 * pitch, LANES), F32),
@@ -484,7 +494,6 @@
         pltpu.VMEM((128, room), BF16),
         pltpu.VMEM((128, room), F32),
         pltpu.VMEM((rays, room), BF16),
-        pltpu.VMEM((256, BLOCK + LANES), BF16),
         pltpu.VMEM((16, LANES), F32),
         pltpu.VMEM((16, LANES), F32),
         pltpu.VMEM((128, 256), F32),
@@ -499,10 +508,8 @@
         pltpu.VMEM((144, 3 * rays), BF16),
         pltpu.VMEM((32, rays), BF16),
         pltpu.VMEM((128, 256), F32),
-        pltpu.VMEM((2, 272, 256), F32),
-        pltpu.VMEM((144, 256), F32),
-        pltpu.VMEM((16, 128), F32),
-        pltpu.VMEM((128, rays), F32),
+        pltpu.VMEM((2, 16, 256), F32),
+        pltpu.VMEM((384 + rays, 256), F32),
         pltpu.VMEM((8, LANES), F32),
         pltpu.VMEM((8 * PART, 256), F32),
         pltpu.SemaphoreType.DMA((29,)),
@@ -513,7 +520,7 @@
         in_specs=[smem] * 2 + [hbm] * 4 + [vmem] * 9,
         out_specs=[vmem, vmem],
         scratch_shapes=scratch,
-        compiler_params=pltpu.CompilerParams(vmem_limit_bytes=62 << 20),
+        compiler_params=pltpu.CompilerParams(vmem_limit_bytes=63 << 20),
     )(
         counts,
         other_counts,
@@ -564,8 +571,8 @@
     pieces, refs = refs[0:8], refs[8:]
     weights, firsts, seconds = refs[0:5], refs[5:10], refs[10:15]
     loss, count = refs[15], refs[16]
-    outs = refs[17:32]
-    packed = refs[32]
+    results, outs = refs[17:32], refs[32:47]
+    packed, sem = refs[47:]
     for k, ref in enumerate(pieces):
         block = place[k // 4] ^ (k % 4)
         packed[pl.ds(pl.multiple_of(block * PART, 8), PART), :] = ref[...]
@@ -580,18 +587,33 @@
         for k in range(3):
             outs[3 * group + k][at] = made[k]
 
+    copies = []
+
+    def give(group):
+        for k in range(3 * group, 3 * group + 3):
+            copies.append(pltpu.make_async_copy(outs[k], results[k], sem.at[k]))
+            copies[-1].start()
+
     everything = slice(None)
     apply(0, (everything, everything), packed[0:96, :])
+    give(0)
     for k in range(2):
         apply(1, (k, everything, everything), packed[96 + 256 * k : 352 + 256 * k, :])
-    apply(2, (slice(0, 256), everything), packed[608:736, :].T)
+    give(1)
+    for k in range(2):
+        apply(2, (slice(128 * k, 128 * k + 128), everything), packed[608:736, 128 * k : 128 * k + 128])
     apply(2, (slice(256, 272), everything), packed[744:760, 0:128])
     apply(2, (slice(272, 283), everything), packed[744:755, 128:256])
+    give(2)
     apply(3, (everything, everything), packed[741:744, 0:128])
+    give(3)
     for k in range(9):
         line = packed[736 + k // 2 : 737 + k // 2, 128 * (k % 2) : 128 * (k % 2) + 128]
         apply(4, (pl.ds(128 * k, 128),), line.reshape(128))
     apply(4, (pl.ds(1152, 4),), packed[740:741, 128:132].reshape(4))
+    give(4)
+    for copy in copies:
+        copy.wait()
 
 
 def update(find_place, pieces, params, firsts, seconds):
@@ -604,8 +626,9 @@
         functools.partial(update_kernel, find_place),
         out_shape=shapes,
         in_specs=[vmem] * 23,
-        out_specs=[smem, smem] + [vmem] * 15,
-        scratch_shapes=[pltpu.VMEM((8 * PART, 256), F32)],
+        out_specs=[smem, smem] + [pl.BlockSpec(memory_space=pl.ANY)] * 15,
+        scratch_shapes=[pltpu.VMEM(shape.shape, F32) for shape in shapes[2:]]
+        + [pltpu.VMEM((8 * PART, 256), F32), pltpu.SemaphoreType.DMA((15,))],
         compiler_params=pltpu.CompilerParams(vmem_limit_bytes=32 << 20),
     )(*pieces, *params, *firsts, *seconds)
 
@@ -637,9 +660,10 @@
         return lax.ppermute(value, axes, pairs)
 
     square = (two, one, both)
-    now = keep + swap(send, core)
-    got = [swap(now[PART * (k + 1) : PART * (k + 2)], pairs) for k, pairs in enumerate(square)]
-    own = (now[:PART] + got[0]) + (got[1] + got[2])
+    came = swap(send, core)
+    now = [keep[PART * k : PART * (k + 1)] + came[PART * k : PART * (k + 1)] for k in range(4)]
+    got = [swap(lax.optimization_barrier(now[k + 1]), square[k]) for k in (2, 1, 0)]
+    own = (now[0] + got[2]) + (got[1] + got[0])
     own = own + swap(own, z_one)
     own = own + swap(own, z_two)
     parts = [own] + [swap(own, pairs) for pairs in square]

time: 82.1 us -> 71.3 us (0.87)
  Pallas kernels: 44 us -> 22.3 us
  starting transfers between devices: 11 us -> 23.6 us
  waiting for transfers between devices: 22.4 us -> 19.5 us
  other arithmetic: 1.86 us -> 2.76 us
    pallas_call x1, Pallas kernels: 41.8 us -> 19.6 us  [field_gradients(): pl.pallas_call(functools.partial(field_kernel, find_place), out_shape=[ja...]
    ppermute x13, starting transfers between devices: 10.4 us -> 23 us  [swap(): return lax.ppermute(value, axes, pairs)]
    ppermute x13, waiting for transfers between devices: 21.3 us -> 18.5 us  [swap(): return lax.ppermute(value, axes, pairs)]
    add x2, other arithmetic: 1.14 us -> 2.04 us  [the longest x1 1.11 us: reduce_small(): keep[PART * k:PART * (k + 1)] + came[PART * k:PART * (k + 1)]]
where the time goes in v4:
time: 71.3 us; the launch traced here: 70.8 us
  starting transfers between devices  23.6 us (33%)
  Pallas kernels  22.3 us (31%)
  waiting for transfers between devices  19.5 us (27%)
  other arithmetic  2.76 us (4%)
  local copies, waits for them, and re-layouts  1.71 us (2%)
  between operations  0.9 us (1%)
    ppermute x13, starting transfers between devices, swap(): return lax.ppermute(value, axes, pairs)  23 us
    pallas_call x1, Pallas kernels, field_gradients(): pl.pallas_call(functools.partial(field_kernel, find_place), out_shape=[ja...  19.6 us
    ppermute x13, waiting for transfers between devices, swap(): return lax.ppermute(value, axes, pairs)  18.5 us
    pallas_call x1, Pallas kernels, update(): pl.pallas_call(functools.partial(update_kernel, find_place), out_shape=sh...  2.75 us
  transfers between devices with their start and end apart: 15, of which 11 were waited for; matrix products, arithmetic and copies ran while one was open for 0% of the time, Pallas kernels for 0%

profile of v4, /device:TPU:0, one launch (start us, length us, event | category | flops | bytes accessed | tf_op | source)
XLA Modules:
  0.0 70.8 jit_solution(8708680804834854101)
XLA Ops:
  0.7 0.0 copy-start.16
  0.7 0.7 convert_bitcast_fusion
  1.3 0.0 copy-done.16
  1.3 0.0 copy-start.18
  1.4 0.0 slice-start.2
  1.4 0.0 slice-start
  1.4 0.0 slice-start.1
  1.4 0.6 copy-done.17
  2.0 0.0 copy-done.18
  2.1 0.1 slice-done.2
  2.1 0.2 slice-done
  2.3 0.0 slice-done.1
  2.3 0.5 collective-permute-start.1
  2.9 0.1 collective-permute-start
  2.9 1.1 %collective-permute-done.counts_two = s32[2,64]{1,0:T(2,128)S(1)} collective-permute-done((s32[2,64]{1,0:T(2,128)S(1)}, s32[2,64]{1,0:T(2,128)S(1)}, u32[]{:S(2)}, u32[]{:S(2)}) %collective-permute-start) | collective-permute-done | bytes 544 | tf_op jit(solution)/shard_map/ppermute | solution.py:705
  4.0 0.0 collective-permute-done.1.other
  4.0 0.6 copy-done.19
  4.6 0.1 copy-done.15
  4.7 0.0 copy-start.12
  4.7 0.0 copy-start.13
  4.7 0.0 copy-start.14
  4.8 19.6 %shard_map.341 = (f32[384,256]{1,0:T(8,128)}, f32[384,256]{1,0:T(8,128)}) custom-call(s32[2,64]{1,0:T(2,128)} %counts_vec.1, s32[2,64]{1,0:T(2,128)} %copy-done.19, f32[464,128]{1,0:T(8,128)} %copy-done.15, f32[2,3,64,128]{3,2,1,0:T(8,128)} %means.1, f32[2,3,64,128]{3,2,1,0:T(8,128)} %variances.1, f32[2,64,128]{2,1,0:T(8,128)} %spacing.1, f32[3,64]{1,0:T(4,128)} %dirs.1, ...), custom_call_target="tpu_custom_call" | custom-call | tf_op jit(solution)/shard_map/pallas_call | solution.py:517
  24.3 2.0 %collective-permute-start.2 = (f32[384,256]{1,0:T(8,128)}, f32[384,256]{1,0:T(8,128)S(1)}, u32[]{:S(2)}, u32[]{:S(2)}) collective-permute-start(f32[384,256]{1,0:T(8,128)} %get-tuple-element.37), channel_id=1, source_target_pairs={{0,1},{1,0},{2,3},{3,2},{4,5},{5,4},{6,7},{7,6},{8,9},{9,8},{10,11... | collective-permute-start | bytes 1179656 | tf_op jit(solution)/shard_map/ppermute | solution.py:660
  26.3 1.6 %collective-permute-done.2 = f32[384,256]{1,0:T(8,128)S(1)} collective-permute-done((f32[384,256]{1,0:T(8,128)}, f32[384,256]{1,0:T(8,128)S(1)}, u32[]{:S(2)}, u32[]{:S(2)}) %collective-permute-start.2) | collective-permute-done | bytes 393248 | tf_op jit(solution)/shard_map/ppermute | solution.py:660
  27.9 1.1 %slice_add_fusion = (f32[96,256]{1,0:T(8,128)S(1)}, f32[96,256]{1,0:T(8,128)S(1)}, f32[96,256]{1,0:T(8,128)S(1)}) fusion(f32[384,256]{1,0:T(8,128)S(1)} %collective-permute-done.2, f32[384,256]{1,0:T(8,128)} %get-tuple-element.36), kind=kLoop, calls=%fused_computation.1 | loop fusion | flops 73728 | bytes 884736 | tf_op jit(solution)/shard_map/add | solution.py:664
  29.0 0.0 copy-start
  29.0 8.3 %collective-permute-start.4 = (f32[96,256]{1,0:T(8,128)S(1)}, f32[96,256]{1,0:T(8,128)S(1)}, u32[]{:S(2)}, u32[]{:S(2)}) collective-permute-start(f32[96,256]{1,0:T(8,128)S(1)} %get-tuple-element.56), channel_id=1, source_target_pairs={{0,2},{1,5},{2,0},{3,7},{4,6},{5,1},{6,4},{7,3},{8,10},{9,13},{10,... | collective-permute-start | bytes 294920 | tf_op jit(solution)/shard_map/ppermute | solution.py:660
  37.3 0.0 collective-permute-start.5
  37.3 1.5 %collective-permute-start.3 = (f32[96,256]{1,0:T(8,128)S(1)}, f32[96,256]{1,0:T(8,128)S(1)}, u32[]{:S(2)}, u32[]{:S(2)}) collective-permute-start(f32[96,256]{1,0:T(8,128)S(1)} %get-tuple-element.57), channel_id=1, source_target_pairs={{0,4},{1,3},{2,6},{3,1},{4,0},{5,7},{6,2},{7,5},{8,12},{9,11},{10,... | collective-permute-start | bytes 294920 | tf_op jit(solution)/shard_map/ppermute | solution.py:660
  38.9 1.7 %collective-permute-done.4 = f32[96,256]{1,0:T(8,128)S(1)} collective-permute-done((f32[96,256]{1,0:T(8,128)S(1)}, f32[96,256]{1,0:T(8,128)S(1)}, u32[]{:S(2)}, u32[]{:S(2)}) %collective-permute-start.4) | collective-permute-done | bytes 98336 | tf_op jit(solution)/shard_map/ppermute | solution.py:660
  40.5 2.5 %collective-permute-done.5 = f32[96,256]{1,0:T(8,128)S(1)} collective-permute-done((f32[96,256]{1,0:T(8,128)S(1)}, f32[96,256]{1,0:T(8,128)S(1)}, u32[]{:S(2)}, u32[]{:S(2)}) %collective-permute-start.5) | collective-permute-done | bytes 98336 | tf_op jit(solution)/shard_map/ppermute | solution.py:660
  43.0 0.0 collective-permute-done.3
  43.0 0.9 %fusion.1 = f32[96,256]{1,0:T(8,128)S(1)} fusion(f32[96,256]{1,0:T(8,128)S(1)} %collective-permute-done.3, f32[384,256]{1,0:T(8,128)S(1)} %collective-permute-done.2, f32[96,256]{1,0:T(8,128)S(1)} %collective-permute-done.4, f32[96,256]{1,0:T(8,128)S(1)} %collective-permute-done.5, f32[384,256]{1,0:T(8,128)} %get-tuple-element.36), kind=kLoop, calls=%fused_computation.6 | loop fusion | flops 98304 | bytes 589824 | tf_op jit(solution)/shard_map/add | solution.py:666
  43.9 0.9 %collective-permute-start.6 = (f32[96,256]{1,0:T(8,128)S(1)}, f32[96,256]{1,0:T(8,128)S(1)}, u32[]{:S(2)}, u32[]{:S(2)}) collective-permute-start(f32[96,256]{1,0:T(8,128)S(1)} %fusion.1), channel_id=1, source_target_pairs={{0,8},{1,17},{2,10},{3,19},{4,12},{5,21},{6,14},{7,23},{8,0},{9,25... | collective-permute-start | bytes 294920 | tf_op jit(solution)/shard_map/ppermute | solution.py:660
  44.8 3.8 %collective-permute-done.6 = f32[96,256]{1,0:T(8,128)S(1)} collective-permute-done((f32[96,256]{1,0:T(8,128)S(1)}, f32[96,256]{1,0:T(8,128)S(1)}, u32[]{:S(2)}, u32[]{:S(2)}) %collective-permute-start.6) | collective-permute-done | bytes 98336 | tf_op jit(solution)/shard_map/ppermute | solution.py:660
  48.6 0.0 copy-start.1
  48.7 0.0 copy-start.4
  48.7 6.3 %collective-permute-start.7 = (f32[96,256]{1,0:T(8,128)S(1)}, f32[96,256]{1,0:T(8,128)S(1)}, u32[]{:S(2)}, u32[]{:S(2)}) collective-permute-start(f32[96,256]{1,0:T(8,128)S(1)} %add.36), channel_id=1, source_target_pairs={{0,16},{1,9},{2,18},{3,11},{4,20},{5,13},{6,22},{7,15},{8,24},{9,1... | collective-permute-start | bytes 294920 | tf_op jit(solution)/shard_map/ppermute | solution.py:660
  54.9 3.1 %collective-permute-done.7 = f32[96,256]{1,0:T(8,128)S(1)} collective-permute-done((f32[96,256]{1,0:T(8,128)S(1)}, f32[96,256]{1,0:T(8,128)S(1)}, u32[]{:S(2)}, u32[]{:S(2)}) %collective-permute-start.7) | collective-permute-done | bytes 98336 | tf_op jit(solution)/shard_map/ppermute | solution.py:660
  58.0 1.6 %collective-permute-start.10 = (f32[96,256]{1,0:T(8,128)S(1)}, f32[96,256]{1,0:T(8,128)S(1)}, u32[]{:S(2)}, u32[]{:S(2)}) collective-permute-start(f32[96,256]{1,0:T(8,128)S(1)} %add.37.refs_0_), channel_id=1, source_target_pairs={{0,6},{1,7},{2,4},{3,5},{4,2},{5,3},{6,0},{7,1},{8,14},{9,15},{10,... | collective-permute-start | bytes 294920 | tf_op jit(solution)/shard_map/ppermute | solution.py:660
  59.6 2.4 %collective-permute-start.9 = (f32[96,256]{1,0:T(8,128)S(1)}, f32[96,256]{1,0:T(8,128)S(1)}, u32[]{:S(2)}, u32[]{:S(2)}) collective-permute-start(f32[96,256]{1,0:T(8,128)S(1)} %add.37.refs_0_), channel_id=1, source_target_pairs={{0,2},{1,5},{2,0},{3,7},{4,6},{5,1},{6,4},{7,3},{8,10},{9,13},{10,... | collective-permute-start | bytes 294920 | tf_op jit(solution)/shard_map/ppermute | solution.py:660
  62.0 0.0 collective-permute-start.8
  62.0 0.0 collective-permute-start.11
  62.0 1.6 %collective-permute-done.10.refs_3_ = f32[96,256]{1,0:T(8,128)S(1)} collective-permute-done((f32[96,256]{1,0:T(8,128)S(1)}, f32[96,256]{1,0:T(8,128)S(1)}, u32[]{:S(2)}, u32[]{:S(2)}) %collective-permute-start.10) | collective-permute-done | bytes 98336 | tf_op jit(solution)/shard_map/ppermute | solution.py:660
  63.6 0.0 collective-permute-start.14
  63.6 2.1 %collective-permute-done.9.refs_2_ = f32[96,256]{1,0:T(8,128)S(1)} collective-permute-done((f32[96,256]{1,0:T(8,128)S(1)}, f32[96,256]{1,0:T(8,128)S(1)}, u32[]{:S(2)}, u32[]{:S(2)}) %collective-permute-start.9) | collective-permute-done | bytes 98336 | tf_op jit(solution)/shard_map/ppermute | solution.py:660
  65.7 0.0 collective-permute-start.13
  65.7 1.0 %collective-permute-done.8.refs_1_ = f32[96,256]{1,0:T(8,128)S(1)} collective-permute-done((f32[96,256]{1,0:T(8,128)S(1)}, f32[96,256]{1,0:T(8,128)S(1)}, u32[]{:S(2)}, u32[]{:S(2)}) %collective-permute-start.8) | collective-permute-done | bytes 98336 | tf_op jit(solution)/shard_map/ppermute | solution.py:660
  66.7 0.0 collective-permute-start.12
  66.7 0.0 collective-permute-done.11.refs_4_
  66.7 0.0 collective-permute-done.14.refs_7_
  66.7 0.3 collective-permute-done.13.refs_6_
  67.0 1.0 %collective-permute-done.12.refs_5_ = f32[96,256]{1,0:T(8,128)S(1)} collective-permute-done((f32[96,256]{1,0:T(8,128)S(1)}, f32[96,256]{1,0:T(8,128)S(1)}, u32[]{:S(2)}, u32[]{:S(2)}) %collective-permute-start.12) | collective-permute-done | bytes 98336 | tf_op jit(solution)/shard_map/ppermute | solution.py:660
  68.0 0.0 copy-done.6
  68.0 0.0 copy-done.8
  68.0 0.0 copy-done.10
  68.0 0.0 copy-done.11
  68.0 0.0 copy-done.12
  68.0 0.0 copy-done.13
  68.0 0.0 copy-done.14
  68.0 0.0 copy-done.2
  68.0 0.0 copy-done.3
  68.0 0.0 copy-done
  68.1 2.8 %shard_map.342 = (f32[1]{0:T(128)}, f32[1]{0:T(128)}, f32[96,256]{1,0:T(8,128)}, f32[96,256]{1,0:T(8,128)}, f32[96,256]{1,0:T(8,128)}, /*index=5*/f32[2,256,256]...) custom-call(f32[96,256]{1,0:T(8,128)S(1)} %add.37.refs_0_, ...), custom_call_target="tpu_custom_call" | custom-call | tf_op jit(solution)/shard_map/pallas_call | solution.py:625
  (22 shorter events, 0.1 us)
Async XLA Ops:
  0.7 0.7 copy-start.16
  1.3 0.7 copy-start.17
  1.3 0.7 copy-start.18
  1.4 0.8 %slice-start.2 = ((f32[2,64,128]{2,1,0:T(8,128)}), f32[2,32,128]{2,1,0:T(8,128)S(1)}, s32[]{:S(2)}) async-start(f32[2,64,128]{2,1,0:T(8,128)} %spacing.1), calls=%async_computation.2 | async-start | bytes 65536 | tf_op jit(solution)/shard_map/slice | solution.py:553
  1.4 0.9 %slice-start = ((f32[2,3,64,128]{3,2,1,0:T(8,128)}), f32[2,3,32,128]{3,2,1,0:T(8,128)S(1)}, s32[]{:S(2)}) async-start(f32[2,3,64,128]{3,2,1,0:T(8,128)} %variances.1), calls=%async_computation | async-start | bytes 196608 | tf_op jit(solution)/shard_map/slice | solution.py:552
  1.4 1.0 %slice-start.1 = ((f32[2,3,64,128]{3,2,1,0:T(8,128)}), f32[2,3,32,128]{3,2,1,0:T(8,128)S(1)}, s32[]{:S(2)}) async-start(f32[2,3,64,128]{3,2,1,0:T(8,128)} %means.1), calls=%async_computation.1 | async-start | bytes 196608 | tf_op jit(solution)/shard_map/slice | solution.py:551
  2.3 1.7 %collective-permute-start.1 = (f32[464,128]{1,0:T(8,128)S(1)}, f32[464,128]{1,0:T(8,128)S(1)}, u32[]{:S(2)}, u32[]{:S(2)}) collective-permute-start(f32[464,128]{1,0:T(8,128)S(1)} %pad_maximum_fusion), channel_id=1, source_target_pairs={{0,1},{1,0},{2,3},{3,2},{4,5},{5,4},{6,7},{7,6},{8,9},{9,8},{10,11... | collective-permute-start | bytes 712712 | tf_op jit(solution)/shard_map/ppermute | solution.py:705
  2.9 1.1 %collective-permute-start = (s32[2,64]{1,0:T(2,128)S(1)}, s32[2,64]{1,0:T(2,128)S(1)}, u32[]{:S(2)}, u32[]{:S(2)}) collective-permute-start(s32[2,64]{1,0:T(2,128)S(1)} %copy-done.16), channel_id=1, source_target_pairs={{0,1},{1,0},{2,3},{3,2},{4,5},{5,4},{6,7},{7,6},{8,9},{9,8},{10,11... | collective-permute-start | bytes 1544 | tf_op jit(solution)/shard_map/ppermute | solution.py:705
  4.0 0.6 copy-start.19
  4.0 0.7 copy-start.15
  4.7 63.3 %copy-start.6 = (f32[283,128]{1,0:T(8,128)S(1)}, f32[283,128]{1,0:T(8,128)}, u32[]{:S(2)}) copy-start(f32[283,128]{1,0:T(8,128)} %refs_20_.1) | copy-start | bytes 434692
  4.7 63.3 %copy-start.8 = (f32[96,256]{1,0:T(8,128)S(1)}, f32[96,256]{1,0:T(8,128)}, u32[]{:S(2)}) copy-start(f32[96,256]{1,0:T(8,128)} %refs_18_.1) | copy-start | bytes 294916
  4.7 63.3 %copy-start.10 = (f32[1156]{0:T(1024)S(1)}, f32[1156]{0:T(1024)}, u32[]{:S(2)}) copy-start(f32[1156]{0:T(1024)} %refs_17_.1) | copy-start | bytes 13876
  4.7 63.3 %copy-start.11 = (f32[1156]{0:T(1024)S(1)}, f32[1156]{0:T(1024)}, u32[]{:S(2)}) copy-start(f32[1156]{0:T(1024)} %refs_22_.1) | copy-start | bytes 13876
  4.7 63.3 %copy-start.12 = (f32[128,3]{0,1:T(4,128)S(1)}, f32[128,3]{0,1:T(4,128)}, u32[]{:S(2)}) copy-start(f32[128,3]{0,1:T(4,128)} %param.32) | copy-start | bytes 4612
  4.7 63.3 %copy-start.13 = (f32[128,3]{0,1:T(4,128)S(1)}, f32[128,3]{0,1:T(4,128)}, u32[]{:S(2)}) copy-start(f32[128,3]{0,1:T(4,128)} %param.37) | copy-start | bytes 4612
  4.7 63.3 %copy-start.14 = (f32[128,3]{0,1:T(4,128)S(1)}, f32[128,3]{0,1:T(4,128)}, u32[]{:S(2)}) copy-start(f32[128,3]{0,1:T(4,128)} %param.42) | copy-start | bytes 4612
  24.3 3.6 %collective-permute-start.2 = (f32[384,256]{1,0:T(8,128)}, f32[384,256]{1,0:T(8,128)S(1)}, u32[]{:S(2)}, u32[]{:S(2)}) collective-permute-start(f32[384,256]{1,0:T(8,128)} %get-tuple-element.37), channel_id=1, source_target_pairs={{0,1},{1,0},{2,3},{3,2},{4,5},{5,4},{6,7},{7,6},{8,9},{9,8},{10,11... | collective-permute-start | bytes 1179656 | tf_op jit(solution)/shard_map/ppermute | solution.py:660
  27.9 40.1 %copy-start.2 = (f32[2,256,256]{2,1,0:T(8,128)S(1)}, f32[2,256,256]{2,1,0:T(8,128)}, u32[]{:S(2)}) copy-start(f32[2,256,256]{2,1,0:T(8,128)} %refs_14_.1) | copy-start | bytes 1572868
  27.9 40.1 %copy-start.3 = (f32[2,256,256]{2,1,0:T(8,128)S(1)}, f32[2,256,256]{2,1,0:T(8,128)}, u32[]{:S(2)}) copy-start(f32[2,256,256]{2,1,0:T(8,128)} %refs_19_.1) | copy-start | bytes 1572868
  29.0 39.0 %copy-start = (f32[2,256,256]{2,1,0:T(8,128)S(1)}, f32[2,256,256]{2,1,0:T(8,128)}, u32[]{:S(2)}) copy-start(f32[2,256,256]{2,1,0:T(8,128)} %refs_9_.1) | copy-start | bytes 1572868
  29.0 11.5 %collective-permute-start.4 = (f32[96,256]{1,0:T(8,128)S(1)}, f32[96,256]{1,0:T(8,128)S(1)}, u32[]{:S(2)}, u32[]{:S(2)}) collective-permute-start(f32[96,256]{1,0:T(8,128)S(1)} %get-tuple-element.56), channel_id=1, source_target_pairs={{0,2},{1,5},{2,0},{3,7},{4,6},{5,1},{6,4},{7,3},{8,10},{9,13},{10,... | collective-permute-start | bytes 294920 | tf_op jit(solution)/shard_map/ppermute | solution.py:660
  37.3 5.7 %collective-permute-start.5 = (f32[96,256]{1,0:T(8,128)S(1)}, f32[96,256]{1,0:T(8,128)S(1)}, u32[]{:S(2)}, u32[]{:S(2)}) collective-permute-start(f32[96,256]{1,0:T(8,128)S(1)} %get-tuple-element.55), channel_id=1, source_target_pairs={{0,6},{1,7},{2,4},{3,5},{4,2},{5,3},{6,0},{7,1},{8,14},{9,15},{10,... | collective-permute-start | bytes 294920 | tf_op jit(solution)/shard_map/ppermute | solution.py:660
  37.3 5.7 %collective-permute-start.3 = (f32[96,256]{1,0:T(8,128)S(1)}, f32[96,256]{1,0:T(8,128)S(1)}, u32[]{:S(2)}, u32[]{:S(2)}) collective-permute-start(f32[96,256]{1,0:T(8,128)S(1)} %get-tuple-element.57), channel_id=1, source_target_pairs={{0,4},{1,3},{2,6},{3,1},{4,0},{5,7},{6,2},{7,5},{8,12},{9,11},{10,... | collective-permute-start | bytes 294920 | tf_op jit(solution)/shard_map/ppermute | solution.py:660
  43.9 4.7 %collective-permute-start.6 = (f32[96,256]{1,0:T(8,128)S(1)}, f32[96,256]{1,0:T(8,128)S(1)}, u32[]{:S(2)}, u32[]{:S(2)}) collective-permute-start(f32[96,256]{1,0:T(8,128)S(1)} %fusion.1), channel_id=1, source_target_pairs={{0,8},{1,17},{2,10},{3,19},{4,12},{5,21},{6,14},{7,23},{8,0},{9,25... | collective-permute-start | bytes 294920 | tf_op jit(solution)/shard_map/ppermute | solution.py:660
  48.6 19.4 %copy-start.5 = (f32[283,128]{1,0:T(8,128)S(1)}, f32[283,128]{1,0:T(8,128)}, u32[]{:S(2)}) copy-start(f32[283,128]{1,0:T(8,128)} %refs_15_.1) | copy-start | bytes 434692
  48.6 19.4 %copy-start.7 = (f32[96,256]{1,0:T(8,128)S(1)}, f32[96,256]{1,0:T(8,128)}, u32[]{:S(2)}) copy-start(f32[96,256]{1,0:T(8,128)} %refs_13_.1) | copy-start | bytes 294916
  48.6 19.4 %copy-start.1 = (f32[283,128]{1,0:T(8,128)S(1)}, f32[283,128]{1,0:T(8,128)}, u32[]{:S(2)}) copy-start(f32[283,128]{1,0:T(8,128)} %refs_10_.1) | copy-start | bytes 434692
  48.7 19.4 %copy-start.4 = (f32[96,256]{1,0:T(8,128)S(1)}, f32[96,256]{1,0:T(8,128)}, u32[]{:S(2)}) copy-start(f32[96,256]{1,0:T(8,128)} %refs_8_.1) | copy-start | bytes 294916
  48.7 9.4 %collective-permute-start.7 = (f32[96,256]{1,0:T(8,128)S(1)}, f32[96,256]{1,0:T(8,128)S(1)}, u32[]{:S(2)}, u32[]{:S(2)}) collective-permute-start(f32[96,256]{1,0:T(8,128)S(1)} %add.36), channel_id=1, source_target_pairs={{0,16},{1,9},{2,18},{3,11},{4,20},{5,13},{6,22},{7,15},{8,24},{9,1... | collective-permute-start | bytes 294920 | tf_op jit(solution)/shard_map/ppermute | solution.py:660
  58.0 10.1 %copy-start.9 = (f32[1156]{0:T(1024)S(1)}, f32[1156]{0:T(1024)}, u32[]{:S(2)}) copy-start(f32[1156]{0:T(1024)} %refs_12_.1) | copy-start | bytes 13876
  58.0 5.6 %collective-permute-start.10 = (f32[96,256]{1,0:T(8,128)S(1)}, f32[96,256]{1,0:T(8,128)S(1)}, u32[]{:S(2)}, u32[]{:S(2)}) collective-permute-start(f32[96,256]{1,0:T(8,128)S(1)} %add.37.refs_0_), channel_id=1, source_target_pairs={{0,6},{1,7},{2,4},{3,5},{4,2},{5,3},{6,0},{7,1},{8,14},{9,15},{10,... | collective-permute-start | bytes 294920 | tf_op jit(solution)/shard_map/ppermute | solution.py:660
  59.6 6.1 %collective-permute-start.9 = (f32[96,256]{1,0:T(8,128)S(1)}, f32[96,256]{1,0:T(8,128)S(1)}, u32[]{:S(2)}, u32[]{:S(2)}) collective-permute-start(f32[96,256]{1,0:T(8,128)S(1)} %add.37.refs_0_), channel_id=1, source_target_pairs={{0,2},{1,5},{2,0},{3,7},{4,6},{5,1},{6,4},{7,3},{8,10},{9,13},{10,... | collective-permute-start | bytes 294920 | tf_op jit(solution)/shard_map/ppermute | solution.py:660
  62.0 4.6 %collective-permute-start.8 = (f32[96,256]{1,0:T(8,128)S(1)}, f32[96,256]{1,0:T(8,128)S(1)}, u32[]{:S(2)}, u32[]{:S(2)}) collective-permute-start(f32[96,256]{1,0:T(8,128)S(1)} %add.37.refs_0_), channel_id=1, source_target_pairs={{0,4},{1,3},{2,6},{3,1},{4,0},{5,7},{6,2},{7,5},{8,12},{9,11},{10,... | collective-permute-start | bytes 294920 | tf_op jit(solution)/shard_map/ppermute | solution.py:660
  62.0 4.6 %collective-permute-start.11 = (f32[96,256]{1,0:T(8,128)S(1)}, f32[96,256]{1,0:T(8,128)S(1)}, u32[]{:S(2)}, u32[]{:S(2)}) collective-permute-start(f32[96,256]{1,0:T(8,128)S(1)} %add.37.refs_0_), channel_id=1, source_target_pairs={{0,1},{1,0},{2,3},{3,2},{4,5},{5,4},{6,7},{7,6},{8,9},{9,8},{10,11... | collective-permute-start | bytes 294920 | tf_op jit(solution)/shard_map/ppermute | solution.py:660
  63.6 3.0 %collective-permute-start.14 = (f32[96,256]{1,0:T(8,128)S(1)}, f32[96,256]{1,0:T(8,128)S(1)}, u32[]{:S(2)}, u32[]{:S(2)}) collective-permute-start(f32[96,256]{1,0:T(8,128)S(1)} %collective-permute-done.10.refs_3_), channel_id=1, source_target_pairs={{0,1},{1,0},{2,3},{3,2},{4,5},{5,4},{6,7},{7,6},{8,9},{9,8},{10,11... | collective-permute-start | bytes 294920 | tf_op jit(solution)/shard_map/ppermute | solution.py:660
  65.7 1.3 %collective-permute-start.13 = (f32[96,256]{1,0:T(8,128)S(1)}, f32[96,256]{1,0:T(8,128)S(1)}, u32[]{:S(2)}, u32[]{:S(2)}) collective-permute-start(f32[96,256]{1,0:T(8,128)S(1)} %collective-permute-done.9.refs_2_), channel_id=1, source_target_pairs={{0,1},{1,0},{2,3},{3,2},{4,5},{5,4},{6,7},{7,6},{8,9},{9,8},{10,11... | collective-permute-start | bytes 294920 | tf_op jit(solution)/shard_map/ppermute | solution.py:660
  66.7 1.3 %collective-permute-start.12 = (f32[96,256]{1,0:T(8,128)S(1)}, f32[96,256]{1,0:T(8,128)S(1)}, u32[]{:S(2)}, u32[]{:S(2)}) collective-permute-start(f32[96,256]{1,0:T(8,128)S(1)} %collective-permute-done.8.refs_1_), channel_id=1, source_target_pairs={{0,1},{1,0},{2,3},{3,2},{4,5},{5,4},{6,7},{7,6},{8,9},{9,8},{10,11... | collective-permute-start | bytes 294920 | tf_op jit(solution)/shard_map/ppermute | solution.py:660

commit v5 on v4

--- a/solution.py
+++ b/solution.py
@@ -66,6 +66,9 @@
     find_place,
     counts,
     counts_two,
+    means_two,
+    variances_two,
+    spacing_two,
     other,
     means,
     variances,
@@ -125,16 +128,15 @@
     tiles = -(-capacity // (8 * LANES)) * 8
     copies = []
     for p in range(2):
-        for k, source in enumerate((means, variances)):
+        for k, sources in enumerate(((means, means_two), (variances, variances_two))):
             for c in range(3):
-                to = (p * 8 + 4 * k + c) * pk_pitch
-                copies.append((source.at[p, c, pl.ds(0, own)], pk.at[pl.ds(to, own)]))
-                row = (6 * k + 3 * p + c) * own
-                copies.append((other.at[pl.ds(row, own)], pk.at[pl.ds(to + own, own)]))
-        to = (p * 8 + 7) * pk_pitch
-        copies.append((spacing.at[p, pl.ds(0, own)], pk.at[pl.ds(to, own)]))
-        copies.append((other.at[pl.ds((12 + p) * own, own)], pk.at[pl.ds(to + own, own)]))
-    copies.append((other.at[pl.ds(14 * own, 16)], small_two))
+                for half, source in enumerate(sources):
+                    to = (p * 8 + 4 * k + c) * pk_pitch + half * own
+                    copies.append((source.at[p, c, pl.ds(half * own, own)], pk.at[pl.ds(to, own)]))
+        for half, source in enumerate((spacing, spacing_two)):
+            to = (p * 8 + 7) * pk_pitch + half * own
+            copies.append((source.at[p, pl.ds(half * own, own)], pk.at[pl.ds(to, own)]))
+    copies.append((other, small_two))
     copies = [pltpu.make_async_copy(a, b, sem.at[k]) for k, (a, b) in enumerate(copies)]
     for copy in copies:
         copy.start()
@@ -468,8 +470,9 @@
             ref[q * PART : (q + 1) * PART, :] = packed[pl.ds(source, PART), :]
 
 
-def field_gradients(find_place, local, other, other_counts, params):
+def field_gradients(find_place, local, other, params):
     means, variances, spacing, dirs, target, counts, mask = local
+    means_two, variances_two, spacing_two, other_counts, other_rows = other
     w_in, w_mid, w_head, w_rgb, vec = params
     rays = dirs.shape[1]
     room = 17 * rays * LANES // 16 + LANES
@@ -517,14 +520,17 @@
     return pl.pallas_call(
         functools.partial(field_kernel, find_place),
         out_shape=[jax.ShapeDtypeStruct((4 * PART, 256), F32)] * 2,
-        in_specs=[smem] * 2 + [hbm] * 4 + [vmem] * 9,
+        in_specs=[smem] * 2 + [hbm] * 7 + [vmem] * 9,
         out_specs=[vmem, vmem],
         scratch_shapes=scratch,
         compiler_params=pltpu.CompilerParams(vmem_limit_bytes=63 << 20),
     )(
         counts,
         other_counts,
-        other,
+        means_two,
+        variances_two,
+        spacing_two,
+        other_rows,
         means,
         variances,
         spacing,
@@ -540,21 +546,10 @@
     )
 
 
-def second_half(local):
-    means, variances, spacing, dirs, target, counts, mask = local
-    rays = dirs.shape[1]
-    own = rays // 2
-    small = jnp.concatenate([dirs, target, mask[None].astype(F32), counts.astype(F32)], axis=0)
-    small = jnp.pad(small, ((0, 16 - small.shape[0]), (0, LANES - rays)))
-    return jnp.concatenate(
-        [
-            means[:, :, own:].reshape(6 * own, LANES),
-            variances[:, :, own:].reshape(6 * own, LANES),
-            spacing[:, own:].reshape(2 * own, LANES),
-            small,
-        ],
-        axis=0,
-    )
+def ray_rows(local):
+    dirs, target, counts, mask = local[3:]
+    rows = jnp.concatenate([dirs, target, mask[None].astype(F32), counts.astype(F32)], axis=0)
+    return jnp.pad(rows, ((0, 16 - rows.shape[0]), (0, LANES - rows.shape[1])))
 
 
 def adamw(weight, grad, first, second):
@@ -571,8 +566,8 @@
     pieces, refs = refs[0:8], refs[8:]
     weights, firsts, seconds = refs[0:5], refs[5:10], refs[10:15]
     loss, count = refs[15], refs[16]
-    results, outs = refs[17:32], refs[32:47]
-    packed, sem = refs[47:]
+    outs = refs[17:32]
+    packed = refs[32]
     for k, ref in enumerate(pieces):
         block = place[k // 4] ^ (k % 4)
         packed[pl.ds(pl.multiple_of(block * PART, 8), PART), :] = ref[...]
@@ -587,33 +582,19 @@
         for k in range(3):
             outs[3 * group + k][at] = made[k]
 
-    copies = []
-
-    def give(group):
-        for k in range(3 * group, 3 * group + 3):
-            copies.append(pltpu.make_async_copy(outs[k], results[k], sem.at[k]))
-            copies[-1].start()
-
     everything = slice(None)
     apply(0, (everything, everything), packed[0:96, :])
-    give(0)
     for k in range(2):
         apply(1, (k, everything, everything), packed[96 + 256 * k : 352 + 256 * k, :])
-    give(1)
     for k in range(2):
         apply(2, (slice(128 * k, 128 * k + 128), everything), packed[608:736, 128 * k : 128 * k + 128])
     apply(2, (slice(256, 272), everything), packed[744:760, 0:128])
     apply(2, (slice(272, 283), everything), packed[744:755, 128:256])
-    give(2)
     apply(3, (everything, everything), packed[741:744, 0:128])
-    give(3)
     for k in range(9):
         line = packed[736 + k // 2 : 737 + k // 2, 128 * (k % 2) : 128 * (k % 2) + 128]
         apply(4, (pl.ds(128 * k, 128),), line.reshape(128))
     apply(4, (pl.ds(1152, 4),), packed[740:741, 128:132].reshape(4))
-    give(4)
-    for copy in copies:
-        copy.wait()
 
 
 def update(find_place, pieces, params, firsts, seconds):
@@ -626,9 +607,8 @@
         functools.partial(update_kernel, find_place),
         out_shape=shapes,
         in_specs=[vmem] * 23,
-        out_specs=[smem, smem] + [pl.BlockSpec(memory_space=pl.ANY)] * 15,
-        scratch_shapes=[pltpu.VMEM(shape.shape, F32) for shape in shapes[2:]]
-        + [pltpu.VMEM((8 * PART, 256), F32), pltpu.SemaphoreType.DMA((15,))],
+        out_specs=[smem, smem] + [vmem] * 15,
+        scratch_shapes=[pltpu.VMEM((8 * PART, 256), F32)],
         compiler_params=pltpu.CompilerParams(vmem_limit_bytes=32 << 20),
     )(*pieces, *params, *firsts, *seconds)
 
@@ -660,10 +640,9 @@
         return lax.ppermute(value, axes, pairs)
 
     square = (two, one, both)
-    came = swap(send, core)
-    now = [keep[PART * k : PART * (k + 1)] + came[PART * k : PART * (k + 1)] for k in range(4)]
-    got = [swap(lax.optimization_barrier(now[k + 1]), square[k]) for k in (2, 1, 0)]
-    own = (now[0] + got[2]) + (got[1] + got[0])
+    now = keep + swap(send, core)
+    got = [swap(now[PART * (k + 1) : PART * (k + 2)], pairs) for k, pairs in enumerate(square)]
+    own = (now[:PART] + got[0]) + (got[1] + got[2])
     own = own + swap(own, z_one)
     own = own + swap(own, z_two)
     parts = [own] + [swap(own, pairs) for pairs in square]
@@ -699,11 +678,11 @@
     find_place = place_small if small_mesh else lambda: (0, 4)
     params = (w_in, w_mid, w_head, w_rgb, vectors)
     local = (sample_means, sample_vars, sample_spacing, view_dirs, target_rgb, sample_counts, ray_mask)
-    other, other_counts = second_half(local), sample_counts
+    other = (sample_means, sample_vars, sample_spacing, sample_counts, ray_rows(local))
     if small_mesh:
         core_pairs = xor_pairs(32, lambda i: 1)
-        other, other_counts = (lax.ppermute(array, axes, core_pairs) for array in (other, other_counts))
-    keep, send = field_gradients(find_place, local, other, other_counts, params)
+        other = tuple(lax.ppermute(array, axes, core_pairs) for array in other)
+    keep, send = field_gradients(find_place, local, other, params)
     if small_mesh:
         pieces = reduce_small(keep, send, axes)
     else:

time: 71.3 us -> 70.2 us (0.985); the launches traced: 70.8 us -> 71.2 us
  waiting for transfers between devices: 19.5 us -> 22.1 us
  local copies, waits for them, and re-layouts: 1.71 us -> 0.82 us
    ppermute x13, waiting for transfers between devices: 18.5 us -> 21.2 us  [swap(): return lax.ppermute(value, axes, pairs)]
    ppermute x13, starting transfers between devices: 23 us -> 21.6 us  [swap(): return lax.ppermute(value, axes, pairs)]
    ppermute x2 -> x5, starting transfers between devices: 0.6 us -> 1.6 us  [on_device(): other = tuple((lax.ppermute(array, axes, core_pairs) for array in other))]
    add x2, other arithmetic: 2.04 us -> 1.14 us  [the longest x1 1.12 us: reduce_small(): now = keep + swap(send, core)]
  transfers between devices with their start and end apart: 15 -> 18, of which waited for: 11 -> 10; matrix products, arithmetic and copies ran while one was open for 0% -> 2% of each run, Pallas kernels for 0% -> 0%
where the time goes in v5:
time: 70.2 us; the launch traced here: 71.2 us
  starting transfers between devices  23.2 us (33%)
  waiting for transfers between devices  22.1 us (31%)
  Pallas kernels  21.7 us (31%)
  other arithmetic  2.53 us (4%)
  between operations  0.92 us (1%)
  local copies, waits for them, and re-layouts  0.82 us (1%)
    ppermute x13, starting transfers between devices, swap(): return lax.ppermute(value, axes, pairs)  21.6 us
    ppermute x13, waiting for transfers between devices, swap(): return lax.ppermute(value, axes, pairs)  21.2 us
    pallas_call x1, Pallas kernels, field_gradients(): pl.pallas_call(functools.partial(field_kernel, find_place), out_shape=[ja...  19.5 us
    pallas_call x1, Pallas kernels, update(): pl.pallas_call(functools.partial(update_kernel, find_place), out_shape=sh...  2.21 us
    ppermute x5, starting transfers between devices, on_device(): other = tuple((lax.ppermute(array, axes, core_pairs) for array in other))  1.6 us
  transfers between devices with their start and end apart: 18, of which 10 were waited for; matrix products, arithmetic and copies ran while one was open for 2% of the time, Pallas kernels for 0%

profile of v5, /device:TPU:0, one launch (start us, length us, event | category | flops | bytes accessed | tf_op | source)
XLA Modules:
  0.0 71.2 jit_solution(6167151707919851313)
XLA Ops:
  0.7 0.0 copy-start.18
  0.7 0.0 copy-start.20
  0.7 0.5 collective-permute-start.3
  1.2 0.1 collective-permute-start.1
  1.3 0.4 collective-permute-start.2
  1.7 0.7 convert_bitcast_fusion
  2.4 0.0 copy-done.18
  2.4 0.0 copy-done.20
  2.4 0.7 select_maximum_fusion
  3.1 0.1 collective-permute-start.4
  3.2 0.4 collective-permute-start
  3.6 0.8 %collective-permute-done.counts_two = s32[2,64]{1,0:T(2,128)S(1)} collective-permute-done((s32[2,64]{1,0:T(2,128)S(1)}, s32[2,64]{1,0:T(2,128)S(1)}, u32[]{:S(2)}, u32[]{:S(2)}) %collective-permute-start) | collective-permute-done | bytes 544 | tf_op jit(solution)/shard_map/ppermute | solution.py:684
  4.5 0.0 collective-permute-done.4.other
  4.5 0.0 collective-permute-done.3.spacing_two
  4.5 0.0 copy-start.17
  4.5 0.0 collective-permute-done.1.means_two
  4.5 0.0 copy-start.15
  4.5 0.0 collective-permute-done.2.variances_two
  4.5 0.0 copy-start.16
  4.5 0.5 copy-done.21
  5.0 0.0 copy-done.19
  5.1 0.0 copy-done.17
  5.1 0.1 copy-done.15
  5.2 0.1 copy-done.16
  5.2 19.5 %shard_map.341 = (f32[384,256]{1,0:T(8,128)}, f32[384,256]{1,0:T(8,128)}) custom-call(s32[2,64]{1,0:T(2,128)} %counts_vec.1, s32[2,64]{1,0:T(2,128)} %copy-done.21, f32[2,3,64,128]{3,2,1,0:T(8,128)} %copy-done.15, f32[2,3,64,128]{3,2,1,0:T(8,128)} %copy-done.16, f32[2,64,128]{2,1,0:T(8,128)} %copy-done.17, f32[16,128]{1,0:T(8,128)} %copy-done.19, ...), custom_call_target="tpu_custom_call" | custom-call | tf_op jit(solution)/shard_map/pallas_call | solution.py:520
  24.7 0.4 collective-permute-start.5
  25.2 1.6 %collective-permute-done.5 = f32[384,256]{1,0:T(8,128)S(1)} collective-permute-done((f32[384,256]{1,0:T(8,128)}, f32[384,256]{1,0:T(8,128)S(1)}, u32[]{:S(2)}, u32[]{:S(2)}) %collective-permute-start.5) | collective-permute-done | bytes 393248 | tf_op jit(solution)/shard_map/ppermute | solution.py:640
  26.7 1.1 %add.20 = f32[384,256]{1,0:T(8,128)S(1)} add(f32[384,256]{1,0:T(8,128)} %get-tuple-element.36, f32[384,256]{1,0:T(8,128)S(1)} %collective-permute-done.5) | non-fusion elementwise | flops 98304 | bytes 1179648 | tf_op jit(solution)/shard_map/add | solution.py:643
  27.8 0.0 copy-start.2
  27.9 0.0 copy-start.11
  27.9 5.5 %collective-permute-start.8 = (f32[96,256]{1,0:T(8,128)S(1)}, f32[96,256]{1,0:T(8,128)S(1)}, u32[]{:S(2)}, u32[]{:S(2)}) collective-permute-start(f32[96,256]{1,0:T(8,128)S(1)} %get-tuple-element.55), channel_id=1, source_target_pairs={{0,6},{1,7},{2,4},{3,5},{4,2},{5,3},{6,0},{7,1},{8,14},{9,15},{10,... | collective-permute-start | bytes 294920 | tf_op jit(solution)/shard_map/ppermute | solution.py:640
  33.4 9.7 %collective-permute-start.7 = (f32[96,256]{1,0:T(8,128)S(1)}, f32[96,256]{1,0:T(8,128)S(1)}, u32[]{:S(2)}, u32[]{:S(2)}) collective-permute-start(f32[96,256]{1,0:T(8,128)S(1)} %get-tuple-element.56), channel_id=1, source_target_pairs={{0,2},{1,5},{2,0},{3,7},{4,6},{5,1},{6,4},{7,3},{8,10},{9,13},{10,... | collective-permute-start | bytes 294920 | tf_op jit(solution)/shard_map/ppermute | solution.py:640
  43.0 1.5 %collective-permute-start.6 = (f32[96,256]{1,0:T(8,128)S(1)}, f32[96,256]{1,0:T(8,128)S(1)}, u32[]{:S(2)}, u32[]{:S(2)}) collective-permute-start(f32[96,256]{1,0:T(8,128)S(1)} %get-tuple-element.57), channel_id=1, source_target_pairs={{0,4},{1,3},{2,6},{3,1},{4,0},{5,7},{6,2},{7,5},{8,12},{9,11},{10,... | collective-permute-start | bytes 294920 | tf_op jit(solution)/shard_map/ppermute | solution.py:640
  44.5 0.0 collective-permute-done.8
  44.5 3.3 %collective-permute-done.7 = f32[96,256]{1,0:T(8,128)S(1)} collective-permute-done((f32[96,256]{1,0:T(8,128)S(1)}, f32[96,256]{1,0:T(8,128)S(1)}, u32[]{:S(2)}, u32[]{:S(2)}) %collective-permute-start.7) | collective-permute-done | bytes 98336 | tf_op jit(solution)/shard_map/ppermute | solution.py:640
  47.8 0.0 collective-permute-done.6
  47.8 0.1 collective-permute-start.9
  47.9 5.7 %collective-permute-done.9 = f32[96,256]{1,0:T(8,128)S(1)} collective-permute-done((f32[96,256]{1,0:T(8,128)S(1)}, f32[96,256]{1,0:T(8,128)S(1)}, u32[]{:S(2)}, u32[]{:S(2)}) %collective-permute-start.9) | collective-permute-done | bytes 98336 | tf_op jit(solution)/shard_map/ppermute | solution.py:640
  53.6 0.0 copy-start.1
  53.6 0.0 copy-start.4
  53.6 0.9 %collective-permute-start.10 = (f32[96,256]{1,0:T(8,128)S(1)}, f32[96,256]{1,0:T(8,128)S(1)}, u32[]{:S(2)}, u32[]{:S(2)}) collective-permute-start(f32[96,256]{1,0:T(8,128)S(1)} %add.24), channel_id=1, source_target_pairs={{0,16},{1,9},{2,18},{3,11},{4,20},{5,13},{6,22},{7,15},{8,24},{9,1... | collective-permute-start | bytes 294920 | tf_op jit(solution)/shard_map/ppermute | solution.py:640
  54.5 4.9 %collective-permute-done.10 = f32[96,256]{1,0:T(8,128)S(1)} collective-permute-done((f32[96,256]{1,0:T(8,128)S(1)}, f32[96,256]{1,0:T(8,128)S(1)}, u32[]{:S(2)}, u32[]{:S(2)}) %collective-permute-start.10) | collective-permute-done | bytes 98336 | tf_op jit(solution)/shard_map/ppermute | solution.py:640
  59.4 0.0 copy-start.12
  59.4 2.6 %collective-permute-start.13 = (f32[96,256]{1,0:T(8,128)S(1)}, f32[96,256]{1,0:T(8,128)S(1)}, u32[]{:S(2)}, u32[]{:S(2)}) collective-permute-start(f32[96,256]{1,0:T(8,128)S(1)} %add.25.refs_0_), channel_id=1, source_target_pairs={{0,6},{1,7},{2,4},{3,5},{4,2},{5,3},{6,0},{7,1},{8,14},{9,15},{10,... | collective-permute-start | bytes 294920 | tf_op jit(solution)/shard_map/ppermute | solution.py:640
  62.1 0.9 %collective-permute-start.12 = (f32[96,256]{1,0:T(8,128)S(1)}, f32[96,256]{1,0:T(8,128)S(1)}, u32[]{:S(2)}, u32[]{:S(2)}) collective-permute-start(f32[96,256]{1,0:T(8,128)S(1)} %add.25.refs_0_), channel_id=1, source_target_pairs={{0,2},{1,5},{2,0},{3,7},{4,6},{5,1},{6,4},{7,3},{8,10},{9,13},{10,... | collective-permute-start | bytes 294920 | tf_op jit(solution)/shard_map/ppermute | solution.py:640
  62.9 0.0 collective-permute-start.11
  63.0 0.0 collective-permute-start.14
  63.0 2.0 %collective-permute-done.13.refs_3_ = f32[96,256]{1,0:T(8,128)S(1)} collective-permute-done((f32[96,256]{1,0:T(8,128)S(1)}, f32[96,256]{1,0:T(8,128)S(1)}, u32[]{:S(2)}, u32[]{:S(2)}) %collective-permute-start.13) | collective-permute-done | bytes 98336 | tf_op jit(solution)/shard_map/ppermute | solution.py:640
  65.0 0.0 collective-permute-start.17
  65.0 1.7 %collective-permute-done.12.refs_2_ = f32[96,256]{1,0:T(8,128)S(1)} collective-permute-done((f32[96,256]{1,0:T(8,128)S(1)}, f32[96,256]{1,0:T(8,128)S(1)}, u32[]{:S(2)}, u32[]{:S(2)}) %collective-permute-start.12) | collective-permute-done | bytes 98336 | tf_op jit(solution)/shard_map/ppermute | solution.py:640
  66.7 0.0 collective-permute-start.16
  66.7 0.9 %collective-permute-done.11.refs_1_ = f32[96,256]{1,0:T(8,128)S(1)} collective-permute-done((f32[96,256]{1,0:T(8,128)S(1)}, f32[96,256]{1,0:T(8,128)S(1)}, u32[]{:S(2)}, u32[]{:S(2)}) %collective-permute-start.11) | collective-permute-done | bytes 98336 | tf_op jit(solution)/shard_map/ppermute | solution.py:640
  67.5 0.0 collective-permute-start.15
  67.6 0.0 collective-permute-done.14.refs_4_
  67.6 0.0 collective-permute-done.17.refs_7_
  67.6 0.4 collective-permute-done.16.refs_6_
  68.0 0.9 %collective-permute-done.15.refs_5_ = f32[96,256]{1,0:T(8,128)S(1)} collective-permute-done((f32[96,256]{1,0:T(8,128)S(1)}, f32[96,256]{1,0:T(8,128)S(1)}, u32[]{:S(2)}, u32[]{:S(2)}) %collective-permute-start.15) | collective-permute-done | bytes 98336 | tf_op jit(solution)/shard_map/ppermute | solution.py:640
  68.9 0.0 copy-done.3
  68.9 0.0 copy-done.7
  68.9 0.0 copy-done.8
  68.9 0.0 copy-done.2
  68.9 0.0 copy-done.11
  68.9 0.0 copy-done.14
  69.0 2.2 %shard_map.342 = (f32[1]{0:T(128)}, f32[1]{0:T(128)}, f32[96,256]{1,0:T(8,128)}, f32[96,256]{1,0:T(8,128)}, f32[96,256]{1,0:T(8,128)}, /*index=5*/f32[2,256,256]...) custom-call(f32[96,256]{1,0:T(8,128)S(1)} %add.25.refs_0_, ...), custom_call_target="tpu_custom_call" | custom-call | tf_op jit(solution)/shard_map/pallas_call | solution.py:606
  (26 shorter events, 0.1 us)
Async XLA Ops:
  0.7 1.7 %copy-start.18 = (s32[2,64]{1,0:T(2,128)S(1)}, s32[2,64]{1,0:T(2,128)}, u32[]{:S(2)}) copy-start(s32[2,64]{1,0:T(2,128)} %counts_vec.1) | copy-start | bytes 1540
  0.7 1.7 %copy-start.20 = (f32[3,64]{1,0:T(4,128)S(1)}, f32[3,64]{1,0:T(4,128)}, u32[]{:S(2)}) copy-start(f32[3,64]{1,0:T(4,128)} %target.1) | copy-start | bytes 2308
  0.7 3.8 %collective-permute-start.3 = (f32[2,64,128]{2,1,0:T(8,128)}, f32[2,64,128]{2,1,0:T(8,128)S(1)}, u32[]{:S(2)}, u32[]{:S(2)}) collective-permute-start(f32[2,64,128]{2,1,0:T(8,128)} %spacing.1), channel_id=1, source_target_pairs={{0,1},{1,0},{2,3},{3,2},{4,5},{5,4},{6,7},{7,6},{8,9},{9,8},{10,11... | collective-permute-start | bytes 196616 | tf_op jit(solution)/shard_map/ppermute | solution.py:684
  1.2 3.3 %collective-permute-start.1 = (f32[2,3,64,128]{3,2,1,0:T(8,128)}, f32[2,3,64,128]{3,2,1,0:T(8,128)S(1)}, u32[]{:S(2)}, u32[]{:S(2)}) collective-permute-start(f32[2,3,64,128]{3,2,1,0:T(8,128)} %means.1), channel_id=1, source_target_pairs={{0,1},{1,0},{2,3},{3,2},{4,5},{5,4},{6,7},{7,6},{8,9},{9,8},{10,11... | collective-permute-start | bytes 589832 | tf_op jit(solution)/shard_map/ppermute | solution.py:684
  1.3 3.2 %collective-permute-start.2 = (f32[2,3,64,128]{3,2,1,0:T(8,128)}, f32[2,3,64,128]{3,2,1,0:T(8,128)S(1)}, u32[]{:S(2)}, u32[]{:S(2)}) collective-permute-start(f32[2,3,64,128]{3,2,1,0:T(8,128)} %variances.1), channel_id=1, source_target_pairs={{0,1},{1,0},{2,3},{3,2},{4,5},{5,4},{6,7},{7,6},{8,9},{9,8},{10,11... | collective-permute-start | bytes 589832 | tf_op jit(solution)/shard_map/ppermute | solution.py:684
  3.1 1.4 %collective-permute-start.4 = (f32[16,128]{1,0:T(8,128)S(1)}, f32[16,128]{1,0:T(8,128)S(1)}, u32[]{:S(2)}, u32[]{:S(2)}) collective-permute-start(f32[16,128]{1,0:T(8,128)S(1)} %select_maximum_fusion), channel_id=1, source_target_pairs={{0,1},{1,0},{2,3},{3,2},{4,5},{5,4},{6,7},{7,6},{8,9},{9,8},{10,11... | collective-permute-start | bytes 24584 | tf_op jit(solution)/shard_map/ppermute | solution.py:684
  3.2 1.2 %collective-permute-start = (s32[2,64]{1,0:T(2,128)S(1)}, s32[2,64]{1,0:T(2,128)S(1)}, u32[]{:S(2)}, u32[]{:S(2)}) collective-permute-start(s32[2,64]{1,0:T(2,128)S(1)} %copy-done.18), channel_id=1, source_target_pairs={{0,1},{1,0},{2,3},{3,2},{4,5},{5,4},{6,7},{7,6},{8,9},{9,8},{10,11... | collective-permute-start | bytes 1544 | tf_op jit(solution)/shard_map/ppermute | solution.py:684
  4.5 0.6 copy-start.21
  4.5 0.6 copy-start.19
  4.5 0.6 copy-start.17
  4.5 0.7 copy-start.15
  4.5 0.7 %copy-start.16 = (f32[2,3,64,128]{3,2,1,0:T(8,128)}, f32[2,3,64,128]{3,2,1,0:T(8,128)S(1)}, u32[]{:S(2)}) copy-start(f32[2,3,64,128]{3,2,1,0:T(8,128)S(1)} %collective-permute-done.2.variances_two) | copy-start | bytes 589828
  24.7 2.0 %collective-permute-start.5 = (f32[384,256]{1,0:T(8,128)}, f32[384,256]{1,0:T(8,128)S(1)}, u32[]{:S(2)}, u32[]{:S(2)}) collective-permute-start(f32[384,256]{1,0:T(8,128)} %get-tuple-element.37), channel_id=1, source_target_pairs={{0,1},{1,0},{2,3},{3,2},{4,5},{5,4},{6,7},{7,6},{8,9},{9,8},{10,11... | collective-permute-start | bytes 1179656 | tf_op jit(solution)/shard_map/ppermute | solution.py:640
  26.7 42.1 %copy-start.3 = (f32[2,256,256]{2,1,0:T(8,128)S(1)}, f32[2,256,256]{2,1,0:T(8,128)}, u32[]{:S(2)}) copy-start(f32[2,256,256]{2,1,0:T(8,128)} %refs_19_.1) | copy-start | bytes 1572868
  26.7 42.1 %copy-start.7 = (f32[96,256]{1,0:T(8,128)S(1)}, f32[96,256]{1,0:T(8,128)}, u32[]{:S(2)}) copy-start(f32[96,256]{1,0:T(8,128)} %refs_13_.1) | copy-start | bytes 294916
  26.7 42.1 %copy-start.8 = (f32[96,256]{1,0:T(8,128)S(1)}, f32[96,256]{1,0:T(8,128)}, u32[]{:S(2)}) copy-start(f32[96,256]{1,0:T(8,128)} %refs_18_.1) | copy-start | bytes 294916
  27.8 41.0 %copy-start.2 = (f32[2,256,256]{2,1,0:T(8,128)S(1)}, f32[2,256,256]{2,1,0:T(8,128)}, u32[]{:S(2)}) copy-start(f32[2,256,256]{2,1,0:T(8,128)} %refs_14_.1) | copy-start | bytes 1572868
  27.9 41.0 %copy-start.11 = (f32[1156]{0:T(1024)S(1)}, f32[1156]{0:T(1024)}, u32[]{:S(2)}) copy-start(f32[1156]{0:T(1024)} %refs_22_.1) | copy-start | bytes 13876
  27.9 16.6 %collective-permute-start.8 = (f32[96,256]{1,0:T(8,128)S(1)}, f32[96,256]{1,0:T(8,128)S(1)}, u32[]{:S(2)}, u32[]{:S(2)}) collective-permute-start(f32[96,256]{1,0:T(8,128)S(1)} %get-tuple-element.55), channel_id=1, source_target_pairs={{0,6},{1,7},{2,4},{3,5},{4,2},{5,3},{6,0},{7,1},{8,14},{9,15},{10,... | collective-permute-start | bytes 294920 | tf_op jit(solution)/shard_map/ppermute | solution.py:640
  33.3 35.5 %copy-start.14 = (f32[128,3]{0,1:T(4,128)S(1)}, f32[128,3]{0,1:T(4,128)}, u32[]{:S(2)}) copy-start(f32[128,3]{0,1:T(4,128)} %param.42) | copy-start | bytes 4612
  33.4 14.4 %collective-permute-start.7 = (f32[96,256]{1,0:T(8,128)S(1)}, f32[96,256]{1,0:T(8,128)S(1)}, u32[]{:S(2)}, u32[]{:S(2)}) collective-permute-start(f32[96,256]{1,0:T(8,128)S(1)} %get-tuple-element.56), channel_id=1, source_target_pairs={{0,2},{1,5},{2,0},{3,7},{4,6},{5,1},{6,4},{7,3},{8,10},{9,13},{10,... | collective-permute-start | bytes 294920 | tf_op jit(solution)/shard_map/ppermute | solution.py:640
  43.0 25.9 %copy-start.13 = (f32[128,3]{0,1:T(4,128)S(1)}, f32[128,3]{0,1:T(4,128)}, u32[]{:S(2)}) copy-start(f32[128,3]{0,1:T(4,128)} %param.37) | copy-start | bytes 4612
  43.0 25.9 %copy-start = (f32[2,256,256]{2,1,0:T(8,128)S(1)}, f32[2,256,256]{2,1,0:T(8,128)}, u32[]{:S(2)}) copy-start(f32[2,256,256]{2,1,0:T(8,128)} %refs_9_.1) | copy-start | bytes 1572868
  43.0 4.7 %collective-permute-start.6 = (f32[96,256]{1,0:T(8,128)S(1)}, f32[96,256]{1,0:T(8,128)S(1)}, u32[]{:S(2)}, u32[]{:S(2)}) collective-permute-start(f32[96,256]{1,0:T(8,128)S(1)} %get-tuple-element.57), channel_id=1, source_target_pairs={{0,4},{1,3},{2,6},{3,1},{4,0},{5,7},{6,2},{7,5},{8,12},{9,11},{10,... | collective-permute-start | bytes 294920 | tf_op jit(solution)/shard_map/ppermute | solution.py:640
  47.8 5.7 %collective-permute-start.9 = (f32[96,256]{1,0:T(8,128)S(1)}, f32[96,256]{1,0:T(8,128)S(1)}, u32[]{:S(2)}, u32[]{:S(2)}) collective-permute-start(f32[96,256]{1,0:T(8,128)S(1)} %fusion), channel_id=1, source_target_pairs={{0,8},{1,17},{2,10},{3,19},{4,12},{5,21},{6,14},{7,23},{8,0},{9,25... | collective-permute-start | bytes 294920 | tf_op jit(solution)/shard_map/ppermute | solution.py:640
  53.5 15.4 %copy-start.5 = (f32[283,128]{1,0:T(8,128)S(1)}, f32[283,128]{1,0:T(8,128)}, u32[]{:S(2)}) copy-start(f32[283,128]{1,0:T(8,128)} %refs_15_.1) | copy-start | bytes 434692
  53.5 15.4 %copy-start.6 = (f32[283,128]{1,0:T(8,128)S(1)}, f32[283,128]{1,0:T(8,128)}, u32[]{:S(2)}) copy-start(f32[283,128]{1,0:T(8,128)} %refs_20_.1) | copy-start | bytes 434692
  53.6 15.4 %copy-start.1 = (f32[283,128]{1,0:T(8,128)S(1)}, f32[283,128]{1,0:T(8,128)}, u32[]{:S(2)}) copy-start(f32[283,128]{1,0:T(8,128)} %refs_10_.1) | copy-start | bytes 434692
  53.6 15.4 %copy-start.4 = (f32[96,256]{1,0:T(8,128)S(1)}, f32[96,256]{1,0:T(8,128)}, u32[]{:S(2)}) copy-start(f32[96,256]{1,0:T(8,128)} %refs_8_.1) | copy-start | bytes 294916
  53.6 5.8 %collective-permute-start.10 = (f32[96,256]{1,0:T(8,128)S(1)}, f32[96,256]{1,0:T(8,128)S(1)}, u32[]{:S(2)}, u32[]{:S(2)}) collective-permute-start(f32[96,256]{1,0:T(8,128)S(1)} %add.24), channel_id=1, source_target_pairs={{0,16},{1,9},{2,18},{3,11},{4,20},{5,13},{6,22},{7,15},{8,24},{9,1... | collective-permute-start | bytes 294920 | tf_op jit(solution)/shard_map/ppermute | solution.py:640
  59.4 9.6 %copy-start.9 = (f32[1156]{0:T(1024)S(1)}, f32[1156]{0:T(1024)}, u32[]{:S(2)}) copy-start(f32[1156]{0:T(1024)} %refs_12_.1) | copy-start | bytes 13876
  59.4 9.6 %copy-start.10 = (f32[1156]{0:T(1024)S(1)}, f32[1156]{0:T(1024)}, u32[]{:S(2)}) copy-start(f32[1156]{0:T(1024)} %refs_17_.1) | copy-start | bytes 13876
  59.4 9.6 %copy-start.12 = (f32[128,3]{0,1:T(4,128)S(1)}, f32[128,3]{0,1:T(4,128)}, u32[]{:S(2)}) copy-start(f32[128,3]{0,1:T(4,128)} %param.32) | copy-start | bytes 4612
  59.4 5.6 %collective-permute-start.13 = (f32[96,256]{1,0:T(8,128)S(1)}, f32[96,256]{1,0:T(8,128)S(1)}, u32[]{:S(2)}, u32[]{:S(2)}) collective-permute-start(f32[96,256]{1,0:T(8,128)S(1)} %add.25.refs_0_), channel_id=1, source_target_pairs={{0,6},{1,7},{2,4},{3,5},{4,2},{5,3},{6,0},{7,1},{8,14},{9,15},{10,... | collective-permute-start | bytes 294920 | tf_op jit(solution)/shard_map/ppermute | solution.py:640
  62.1 4.6 %collective-permute-start.12 = (f32[96,256]{1,0:T(8,128)S(1)}, f32[96,256]{1,0:T(8,128)S(1)}, u32[]{:S(2)}, u32[]{:S(2)}) collective-permute-start(f32[96,256]{1,0:T(8,128)S(1)} %add.25.refs_0_), channel_id=1, source_target_pairs={{0,2},{1,5},{2,0},{3,7},{4,6},{5,1},{6,4},{7,3},{8,10},{9,13},{10,... | collective-permute-start | bytes 294920 | tf_op jit(solution)/shard_map/ppermute | solution.py:640
  62.9 4.6 %collective-permute-start.11 = (f32[96,256]{1,0:T(8,128)S(1)}, f32[96,256]{1,0:T(8,128)S(1)}, u32[]{:S(2)}, u32[]{:S(2)}) collective-permute-start(f32[96,256]{1,0:T(8,128)S(1)} %add.25.refs_0_), channel_id=1, source_target_pairs={{0,4},{1,3},{2,6},{3,1},{4,0},{5,7},{6,2},{7,5},{8,12},{9,11},{10,... | collective-permute-start | bytes 294920 | tf_op jit(solution)/shard_map/ppermute | solution.py:640
  63.0 4.6 %collective-permute-start.14 = (f32[96,256]{1,0:T(8,128)S(1)}, f32[96,256]{1,0:T(8,128)S(1)}, u32[]{:S(2)}, u32[]{:S(2)}) collective-permute-start(f32[96,256]{1,0:T(8,128)S(1)} %add.25.refs_0_), channel_id=1, source_target_pairs={{0,1},{1,0},{2,3},{3,2},{4,5},{5,4},{6,7},{7,6},{8,9},{9,8},{10,11... | collective-permute-start | bytes 294920 | tf_op jit(solution)/shard_map/ppermute | solution.py:640
  65.0 2.6 %collective-permute-start.17 = (f32[96,256]{1,0:T(8,128)S(1)}, f32[96,256]{1,0:T(8,128)S(1)}, u32[]{:S(2)}, u32[]{:S(2)}) collective-permute-start(f32[96,256]{1,0:T(8,128)S(1)} %collective-permute-done.13.refs_3_), channel_id=1, source_target_pairs={{0,1},{1,0},{2,3},{3,2},{4,5},{5,4},{6,7},{7,6},{8,9},{9,8},{10,11... | collective-permute-start | bytes 294920 | tf_op jit(solution)/shard_map/ppermute | solution.py:640
  66.7 1.3 %collective-permute-start.16 = (f32[96,256]{1,0:T(8,128)S(1)}, f32[96,256]{1,0:T(8,128)S(1)}, u32[]{:S(2)}, u32[]{:S(2)}) collective-permute-start(f32[96,256]{1,0:T(8,128)S(1)} %collective-permute-done.12.refs_2_), channel_id=1, source_target_pairs={{0,1},{1,0},{2,3},{3,2},{4,5},{5,4},{6,7},{7,6},{8,9},{9,8},{10,11... | collective-permute-start | bytes 294920 | tf_op jit(solution)/shard_map/ppermute | solution.py:640
  67.5 1.3 %collective-permute-start.15 = (f32[96,256]{1,0:T(8,128)S(1)}, f32[96,256]{1,0:T(8,128)S(1)}, u32[]{:S(2)}, u32[]{:S(2)}) collective-permute-start(f32[96,256]{1,0:T(8,128)S(1)} %collective-permute-done.11.refs_1_), channel_id=1, source_target_pairs={{0,1},{1,0},{2,3},{3,2},{4,5},{5,4},{6,7},{7,6},{8,9},{9,8},{10,11... | collective-permute-start | bytes 294920 | tf_op jit(solution)/shard_map/ppermute | solution.py:640
